TPU v7x, 128 devices: a whole 4x4x4 slice. The times are simulated.
128 devices in a mesh: ctx: 8 (over x_lo, z), head: 16 (over x_hi, y, core).
Axes of the slice: x: 4 (x_hi: 2, x_lo: 2; x = x_hi * 2 + x_lo), y: 4, z: 4, core: 2. Of those that a mesh axis runs over, the one named last changes fastest.
Arguments:
- q_nope: bfloat16 [2048, 16384], P('ctx', 'head'), may hold values from -6 to 6
- q_rope: bfloat16 [2048, 8192], P('ctx', 'head'), may hold values from -8 to 8
- latent: bfloat16 [2048, 512], P('ctx'), may hold values from -6 to 6
- latent_gain: bfloat16 [512], replicated, may hold values from 0.25 to 1.75
- k_rope_t: bfloat16 [64, 2048], P(None, 'ctx'), may hold values from -8 to 8
- w_uk: bfloat16 [16384, 512], P('head'), may hold values from -0.25 to 0.25
- w_uv: bfloat16 [16384, 512], P('head'), may hold values from -0.25 to 0.25
- d_out: bfloat16 [2048, 16384], P('ctx', 'head'), may hold values from -6 to 6
- group_ids: int32 [2048], P('ctx'), may hold values from 0 to 1, as said below
- comp_ids: int32 [2048], P('ctx'), may hold values from 0 to 8, as said below
- comp_lengths: int32 [2, 8], replicated, may hold values from 64 to 112, as said below
Outputs:
- attn_out: bfloat16 [2048, 16384], P('ctx', 'head')
- d_q_nope: bfloat16 [2048, 16384], P('ctx', 'head')
- d_q_rope: bfloat16 [2048, 8192], P('ctx', 'head')
- d_latent: bfloat16 [2048, 512], P('ctx')
- d_k_rope_t: bfloat16 [64, 2048], P(None, 'ctx')
- d_w_uk: bfloat16 [16384, 512], P('head')
- d_w_uv: bfloat16 [16384, 512], P('head')
Inputs may be any that keep to these rules, and one draw needn't show every extreme that they name: `group_ids`: non-decreasing; every one of the 2 groups holds tokens. `comp_ids`: each group opens with a prompt of 2 or more tokens (id 0), then completions 1 to 8 follow in order, each of 64 to 112 tokens. comp_lengths[g, k] is the number of tokens with group g and completion k + 1.
All inputs are finite; a program needn't handle non-finite values.
Results may differ from a plain program's by a relative error of at most 0.025.
Values may be sent and summed in bfloat16 or wider, within the bound.
No kernel may reach another device: no remote copies, remote signals or barrier semaphores. Data moves between devices by JAX's collectives and lax.ppermute only.
A program may use at most 128 MiB of HBM per device.

v0:
```python
import math

import jax
import jax.numpy as jnp
from jax import lax
from jax.sharding import PartitionSpec as P

D_ROPE = 64
D_NOPE = 128
D_V = 128
GROUPS = 2
COMP = 8


def token_weights(group_ids, comp_ids, comp_lengths):
    slot_index = group_ids * COMP + comp_ids - 1
    table = jnp.arange(GROUPS * COMP, dtype=jnp.int32)
    onehot = (slot_index[:, None] == table[None, :]) & (comp_ids[:, None] > 0)
    flat_len = comp_lengths.reshape(-1).astype(jnp.float32)
    length = jnp.sum(jnp.where(onehot, flat_len[None, :], 0.0), axis=1) + (comp_ids == 0).astype(
        jnp.float32
    )
    return jnp.where(comp_ids > 0, 64.0 / length, 0.0)


def norm_backward(grad_rows, latent_rows, inverse_rows, gain_f):
    lifted = grad_rows * gain_f
    centred = jnp.mean(lifted * latent_rows, axis=1, keepdims=True)
    return (inverse_rows * lifted - latent_rows * inverse_rows**3 * centred).astype(jnp.bfloat16)


def on_device(
    q_nope,
    q_rope,
    latent,
    latent_gain,
    k_rope_t,
    w_uk,
    w_uv,
    d_out,
    group_ids,
    comp_ids,
    comp_lengths,
):
    scaling = 1.0 / math.sqrt(D_NOPE + D_ROPE)
    query_rows = q_nope.shape[0]
    pair_count = w_uk.shape[0] // (2 * D_NOPE)
    ctx_index = lax.axis_index("ctx")
    latent_f = latent.astype(jnp.float32)
    gain_f = latent_gain.astype(jnp.float32)
    inverse = lax.rsqrt(jnp.mean(latent_f * latent_f, axis=1, keepdims=True) + 1e-06)
    normed = (latent_f * inverse * gain_f).astype(jnp.bfloat16)
    own_codes = (group_ids * (COMP + 1) + comp_ids).astype(jnp.bfloat16)
    keys_lat, keys_rope, key_codes = (
        lax.all_gather(normed, "ctx", axis=0, tiled=True),
        lax.all_gather(k_rope_t, "ctx", axis=1, tiled=True),
        lax.all_gather(own_codes, "ctx", axis=0, tiled=True),
    )
    key_code = key_codes.astype(jnp.int32)
    key_group = key_code // (COMP + 1)
    key_comp = key_code - key_group * (COMP + 1)
    key_count = keys_lat.shape[0]
    key_pos = jnp.arange(key_count, dtype=jnp.int32)
    query_pos = ctx_index * query_rows + jnp.arange(query_rows, dtype=jnp.int32)
    visible = (
        (group_ids[:, None] == key_group[None, :])
        & ((key_comp[None, :] == 0) | (key_comp[None, :] == comp_ids[:, None]))
        & (key_pos[None, :] <= query_pos[:, None])
    )
    weight = token_weights(group_ids, comp_ids, comp_lengths)

    def one_pair(running, pair_index):
        d_normed, d_rope = running
        query_n = lax.dynamic_slice_in_dim(q_nope, pair_index * 2 * D_NOPE, 2 * D_NOPE, 1).reshape(
            query_rows, 2, D_NOPE
        )
        query_r = lax.dynamic_slice_in_dim(q_rope, pair_index * 2 * D_ROPE, 2 * D_ROPE, 1).reshape(
            query_rows, 2, D_ROPE
        )
        key_up = lax.dynamic_slice_in_dim(w_uk, pair_index * 2 * D_NOPE, 2 * D_NOPE, 0).reshape(
            2, D_NOPE, -1
        )
        value_up = lax.dynamic_slice_in_dim(w_uv, pair_index * 2 * D_V, 2 * D_V, 0).reshape(
            2, D_V, -1
        )
        grad_out = lax.dynamic_slice_in_dim(d_out, pair_index * 2 * D_V, 2 * D_V, 1).reshape(
            query_rows, 2, D_V
        )
        q_lat = jnp.einsum(
            "qhd,hdl->hql", query_n, key_up, preferred_element_type=jnp.float32
        ).astype(jnp.bfloat16)
        scores = (
            jnp.einsum("hql,kl->hqk", q_lat, keys_lat, preferred_element_type=jnp.float32)
            + jnp.einsum("qhr,rk->hqk", query_r, keys_rope, preferred_element_type=jnp.float32)
        ) * scaling
        maxima = jnp.max(jnp.where(visible[None], scores, -jnp.inf), axis=2, keepdims=True)
        expos = jnp.where(visible[None], jnp.exp(scores - maxima), 0.0)
        attention = (expos / jnp.sum(expos, axis=2, keepdims=True)).astype(jnp.bfloat16)
        o_lat = jnp.einsum(
            "hqk,kl->hql", attention, keys_lat, preferred_element_type=jnp.float32
        ).astype(jnp.bfloat16)
        head_out = jnp.einsum(
            "hql,hdl->qhd", o_lat, value_up, preferred_element_type=jnp.float32
        ).astype(jnp.bfloat16)
        weighted = (grad_out.astype(jnp.float32) * weight[:, None, None]).astype(jnp.bfloat16)
        do_lat = jnp.einsum(
            "qhd,hdl->hql", weighted, value_up, preferred_element_type=jnp.float32
        ).astype(jnp.bfloat16)
        grad_wv = jnp.einsum("qhd,hql->hdl", weighted, o_lat, preferred_element_type=jnp.float32)
        dprobs = jnp.einsum("hql,kl->hqk", do_lat, keys_lat, preferred_element_type=jnp.float32)
        att_f = attention.astype(jnp.float32)
        row_dot = jnp.sum(att_f * dprobs, axis=2, keepdims=True)
        dscores = (att_f * (dprobs - row_dot) * scaling).astype(jnp.bfloat16)
        dq_lat = jnp.einsum(
            "hqk,kl->hql", dscores, keys_lat, preferred_element_type=jnp.float32
        ).astype(jnp.bfloat16)
        grad_qn = jnp.einsum(
            "hql,hdl->qhd", dq_lat, key_up, preferred_element_type=jnp.float32
        ).astype(jnp.bfloat16)
        grad_wk = jnp.einsum("qhd,hql->hdl", query_n, dq_lat, preferred_element_type=jnp.float32)
        grad_qr = jnp.einsum(
            "hqk,rk->qhr", dscores, keys_rope, preferred_element_type=jnp.float32
        ).astype(jnp.bfloat16)
        d_normed = (
            d_normed
            + jnp.einsum("hqk,hql->kl", dscores, q_lat, preferred_element_type=jnp.float32)
            + jnp.einsum("hqk,hql->kl", attention, do_lat, preferred_element_type=jnp.float32)
        )
        d_rope = d_rope + jnp.einsum(
            "qhr,hqk->rk", query_r, dscores, preferred_element_type=jnp.float32
        )
        outputs = (
            head_out.reshape(query_rows, 2 * D_V),
            grad_qn.reshape(query_rows, 2 * D_NOPE),
            grad_qr.reshape(query_rows, 2 * D_ROPE),
            grad_wk,
            grad_wv,
        )
        return ((d_normed, d_rope), outputs)

    start_state = (
        jnp.zeros((key_count, keys_lat.shape[1]), jnp.float32),
        jnp.zeros((keys_rope.shape[0], key_count), jnp.float32),
    )
    (d_normed, d_rope), stacked = lax.scan(
        one_pair, start_state, jnp.arange(pair_count, dtype=jnp.int32)
    )
    head_out, grad_qn, grad_qr, grad_wk, grad_wv = stacked
    attn_out = jnp.transpose(head_out, (1, 0, 2)).reshape(query_rows, -1)
    d_q_nope = jnp.transpose(grad_qn, (1, 0, 2)).reshape(query_rows, -1)
    d_q_rope = jnp.transpose(grad_qr, (1, 0, 2)).reshape(query_rows, -1)
    local_wk = grad_wk.reshape(-1, grad_wk.shape[-1])
    local_wv = grad_wv.reshape(-1, grad_wv.shape[-1])
    summed_wk, summed_wv = (
        lax.psum(local_wk.astype(jnp.bfloat16), "ctx").astype(jnp.float32),
        lax.psum(local_wv.astype(jnp.bfloat16), "ctx").astype(jnp.float32),
    )
    headed_lat, headed_rope = (
        lax.psum(d_normed.astype(jnp.bfloat16), "head").astype(jnp.float32),
        lax.psum(d_rope.astype(jnp.bfloat16), "head").astype(jnp.float32),
    )
    owned_lat, owned_rope = (
        lax.psum_scatter(
            headed_lat.astype(jnp.bfloat16), "ctx", scatter_dimension=0, tiled=True
        ).astype(jnp.float32),
        lax.psum_scatter(
            headed_rope.astype(jnp.bfloat16), "ctx", scatter_dimension=1, tiled=True
        ).astype(jnp.float32),
    )
    d_latent = norm_backward(owned_lat, latent_f, inverse, gain_f)
    d_k_rope_t = owned_rope.astype(jnp.bfloat16)
    return (
        attn_out,
        d_q_nope,
        d_q_rope,
        d_latent,
        d_k_rope_t,
        summed_wk.astype(jnp.bfloat16),
        summed_wv.astype(jnp.bfloat16),
    )


def solution(mesh):
    return jax.shard_map(
        on_device,
        mesh=mesh,
        in_specs=(
            P("ctx", "head"),
            P("ctx", "head"),
            P("ctx", None),
            P(),
            P(None, "ctx"),
            P("head", None),
            P("head", None),
            P("ctx", "head"),
            P("ctx"),
            P("ctx"),
            P(),
        ),
        out_specs=(
            P("ctx", "head"),
            P("ctx", "head"),
            P("ctx", "head"),
            P("ctx", None),
            P(None, "ctx"),
            P("head", None),
            P("head", None),
        ),
        check_vma=False,
    )
```

profile of v0, /device:TPU:1, one launch (start us, length us, event | category | flops | bytes accessed | tf_op | source)
XLA Modules:
  0.0 632.6 jit_solution(18203079412922272326)
XLA Ops:
  13.6 17.9 %all-gather = bf16[8,1,256]{2,1,0:T(2,128)(2,1)S(1)} all-gather(bf16[1,1,256]{2,1,0:T(2,128)(2,1)S(1)} %reshape.115), channel_id=1, replica_groups=mesh['ctx'=8,'head'=16] {'ctx'}, dimensions={0}, use_global_device_ids=true | all-gather | bytes 4608 | tf_op jit(solution)/shard_map/all_gather | solution.py:57
  32.8 26.1 %all_gather.11 = bf16[64,2048]{1,0:T(8,128)(2,1)} all-gather(bf16[64,256]{1,0:T(8,128)(2,1)} %param.17), channel_id=1, replica_groups=mesh['ctx'=8,'head'=16] {'ctx'}, dimensions={1}, use_global_device_ids=true | all-gather | bytes 294912 | tf_op jit(solution)/shard_map/all_gather | solution.py:56
  61.4 247.1 %while.25 = (s32[]{:T(128)}, f32[2048,512]{1,0:T(8,128)}, f32[64,2048]{1,0:T(8,128)}, bf16[4,256,256]{1,2,0:T(8,128)(2,1)}, bf16[4,256,256]{1,2,0:T(8,128)(2,1)}...) while((s32[]{:T(128)}, f32[2048,512]{1,0:T(8,128)}, ...), condition=%wide.region_6.7_spmd.clone, body=%wide.region_2.6_spmd.clone.sunk | while | flops 7293677568 | bytes 130121360 | solution.py:145
  72.8 3.3 fusion.145
  81.8 6.0 fusion.150
  88.4 6.7 %fusion.147 = f32[64,2048]{1,0:T(8,128)} fusion(bf16[256,2,64]{0,2,1:T(8,128)(2,1)S(1)} %bitcast.180, bf16[2,256,2048]{2,1,0:T(8,128)(2,1)} %divide_convert_fusion.2, f32[2,256,2048]{2,1,0:T(8,128)} %fusion.145, f32[64,2048]{1,0:T(8,128)} %get-tuple-element.650, pred[]{:T(512)S(6)} %compare.3), kind=kOutput, calls=%fused_computation.17.clone.1 | convolution fusion | flops 141822464 | bytes 7405569 | tf_op jit(solution)/shard_map/while/body/eval_jaxpr/qhr,hqk->rk/dot_general | solution.py:129
  99.9 6.3 fusion.148
  106.1 8.7 %fusion.146 = f32[2048,512,1]{1,0,2:T(8,128)} fusion(bf16[2,256,512]{2,1,0:T(8,128)(2,1)} %copy-done.2, bf16[2,256,2048]{2,1,0:T(8,128)(2,1)} %divide_convert_fusion.2, f32[2,256,2048]{2,1,0:T(8,128)} %fusion.145), kind=kOutput, calls=%fused_computation.29.clone.1 | convolution fusion | flops 1081084416 | bytes 11010048 | tf_op jit(solution)/shard_map/while/body/eval_jaxpr/hqk,hql->kl/dot_general | solution.py:126
  114.8 5.6 bitcast_add_fusion.4
  142.5 6.0 fusion.150
  149.1 6.9 %fusion.147 = f32[64,2048]{1,0:T(8,128)} fusion(bf16[256,2,64]{0,2,1:T(8,128)(2,1)S(1)} %bitcast.180, bf16[2,256,2048]{2,1,0:T(8,128)(2,1)} %divide_convert_fusion.2, f32[2,256,2048]{2,1,0:T(8,128)} %fusion.145, f32[64,2048]{1,0:T(8,128)} %get-tuple-element.650, pred[]{:T(512)S(6)} %compare.3), kind=kOutput, calls=%fused_computation.17.clone.1 | convolution fusion | flops 141822464 | bytes 7405569 | tf_op jit(solution)/shard_map/while/body/eval_jaxpr/qhr,hqk->rk/dot_general | solution.py:129
  160.8 6.3 fusion.148
  167.0 8.7 %fusion.146 = f32[2048,512,1]{1,0,2:T(8,128)} fusion(bf16[2,256,512]{2,1,0:T(8,128)(2,1)} %copy-done.2, bf16[2,256,2048]{2,1,0:T(8,128)(2,1)} %divide_convert_fusion.2, f32[2,256,2048]{2,1,0:T(8,128)} %fusion.145), kind=kOutput, calls=%fused_computation.29.clone.1 | convolution fusion | flops 1081084416 | bytes 11010048 | tf_op jit(solution)/shard_map/while/body/eval_jaxpr/hqk,hql->kl/dot_general | solution.py:126
  175.7 6.9 %bitcast_add_fusion.4 = f32[2048,512]{1,0:T(8,128)} fusion(f32[2048,512,1]{1,0,2:T(8,128)} %fusion.146, f32[2048,512]{1,0:T(8,128)} %get-tuple-element.649, bf16[2,256,2048]{2,1,0:T(8,128)(2,1)S(1)} %copy-done.1, bf16[2,256,512]{2,1,0:T(8,128)(2,1)S(1)} %convolution_convert_fusion.9, pred[]{:T(512)S(6)} %compare.3), kind=kOutput, calls=%fused_computation.7.clone.1 | convolution fusion | flops 1076887552 | bytes 15204353 | tf_op jit(solution)/shard_map/while/body/eval_jaxpr/hqk,hql->kl/dot_general | solution.py:127
  195.6 3.3 fusion.145
  204.6 6.0 fusion.150
  211.2 6.9 %fusion.147 = f32[64,2048]{1,0:T(8,128)} fusion(bf16[256,2,64]{0,2,1:T(8,128)(2,1)S(1)} %bitcast.180, bf16[2,256,2048]{2,1,0:T(8,128)(2,1)} %divide_convert_fusion.2, f32[2,256,2048]{2,1,0:T(8,128)} %fusion.145, f32[64,2048]{1,0:T(8,128)} %get-tuple-element.650, pred[]{:T(512)S(6)} %compare.3), kind=kOutput, calls=%fused_computation.17.clone.1 | convolution fusion | flops 141822464 | bytes 7405569 | tf_op jit(solution)/shard_map/while/body/eval_jaxpr/qhr,hqk->rk/dot_general | solution.py:129
  222.9 6.2 fusion.148
  229.2 8.7 %fusion.146 = f32[2048,512,1]{1,0,2:T(8,128)} fusion(bf16[2,256,512]{2,1,0:T(8,128)(2,1)} %copy-done.2, bf16[2,256,2048]{2,1,0:T(8,128)(2,1)} %divide_convert_fusion.2, f32[2,256,2048]{2,1,0:T(8,128)} %fusion.145), kind=kOutput, calls=%fused_computation.29.clone.1 | convolution fusion | flops 1081084416 | bytes 11010048 | tf_op jit(solution)/shard_map/while/body/eval_jaxpr/hqk,hql->kl/dot_general | solution.py:126
  237.8 6.9 %bitcast_add_fusion.4 = f32[2048,512]{1,0:T(8,128)} fusion(f32[2048,512,1]{1,0,2:T(8,128)} %fusion.146, f32[2048,512]{1,0:T(8,128)} %get-tuple-element.649, bf16[2,256,2048]{2,1,0:T(8,128)(2,1)S(1)} %copy-done.1, bf16[2,256,512]{2,1,0:T(8,128)(2,1)S(1)} %convolution_convert_fusion.9, pred[]{:T(512)S(6)} %compare.3), kind=kOutput, calls=%fused_computation.7.clone.1 | convolution fusion | flops 1076887552 | bytes 15204353 | tf_op jit(solution)/shard_map/while/body/eval_jaxpr/hqk,hql->kl/dot_general | solution.py:127
  257.8 3.3 fusion.145
  266.8 6.0 fusion.150
  273.4 6.9 %fusion.147 = f32[64,2048]{1,0:T(8,128)} fusion(bf16[256,2,64]{0,2,1:T(8,128)(2,1)S(1)} %bitcast.180, bf16[2,256,2048]{2,1,0:T(8,128)(2,1)} %divide_convert_fusion.2, f32[2,256,2048]{2,1,0:T(8,128)} %fusion.145, f32[64,2048]{1,0:T(8,128)} %get-tuple-element.650, pred[]{:T(512)S(6)} %compare.3), kind=kOutput, calls=%fused_computation.17.clone.1 | convolution fusion | flops 141822464 | bytes 7405569 | tf_op jit(solution)/shard_map/while/body/eval_jaxpr/qhr,hqk->rk/dot_general | solution.py:129
  285.0 6.2 fusion.148
  291.3 8.7 %fusion.146 = f32[2048,512,1]{1,0,2:T(8,128)} fusion(bf16[2,256,512]{2,1,0:T(8,128)(2,1)} %copy-done.2, bf16[2,256,2048]{2,1,0:T(8,128)(2,1)} %divide_convert_fusion.2, f32[2,256,2048]{2,1,0:T(8,128)} %fusion.145), kind=kOutput, calls=%fused_computation.29.clone.1 | convolution fusion | flops 1081084416 | bytes 11010048 | tf_op jit(solution)/shard_map/while/body/eval_jaxpr/hqk,hql->kl/dot_general | solution.py:126
  300.0 6.9 %bitcast_add_fusion.4 = f32[2048,512]{1,0:T(8,128)} fusion(f32[2048,512,1]{1,0,2:T(8,128)} %fusion.146, f32[2048,512]{1,0:T(8,128)} %get-tuple-element.649, bf16[2,256,2048]{2,1,0:T(8,128)(2,1)S(1)} %copy-done.1, bf16[2,256,512]{2,1,0:T(8,128)(2,1)S(1)} %convolution_convert_fusion.9, pred[]{:T(512)S(6)} %compare.3), kind=kOutput, calls=%fused_computation.7.clone.1 | convolution fusion | flops 1076887552 | bytes 15204353 | tf_op jit(solution)/shard_map/while/body/eval_jaxpr/hqk,hql->kl/dot_general | solution.py:127
  308.5 3.8 convert_element_type.154
  313.2 43.3 %reduce-scatter.3.cloned.1.call-done = bf16[256,512]{1,0:T(8,128)(2,1)} async-done(((bf16[2048,512]{1,0:T(8,128)(2,1)}), bf16[256,512]{1,0:T(8,128)(2,1)}) %reduce-scatter.3.cloned.1.call-update) | async-done | bytes 262160 | tf_op jit(solution)/shard_map/reduce_scatter | solution.py:163
  360.0 35.1 %reduce-scatter.5.cloned.1.call-done = bf16[64,256]{1,0:T(8,128)(2,1)} async-done(((bf16[64,2048]{1,0:T(8,128)(2,1)}), bf16[64,256]{1,0:T(8,128)(2,1)}) %reduce-scatter.5.cloned.1.call-update) | async-done | bytes 32784 | tf_op jit(solution)/shard_map/reduce_scatter | solution.py:166
  395.2 65.4 %psum.33 = bf16[64,256]{1,0:T(8,128)(2,1)} all-reduce(bf16[64,256]{1,0:T(8,128)(2,1)} %reduce-scatter.5.cloned.1.call-done), channel_id=1, replica_groups=mesh['ctx'=8,'head'=16] {'head'}, use_global_device_ids=true, to_apply=%region_10.11 | all-reduce | flops 16384 | bytes 65536 | tf_op jit(solution)/shard_map/psum | solution.py:160
  460.5 78.3 %all-reduce.4.cloned.1.call-done = bf16[256,512]{1,0:T(8,128)(2,1)} async-done(((bf16[256,512]{1,0:T(8,128)(2,1)}), bf16[256,512]{1,0:T(8,128)(2,1)}) %all-reduce.4.cloned.1.call-update) | async-done | bytes 262160 | tf_op jit(solution)/shard_map/psum | solution.py:159
  541.9 79.7 %all-reduce.6.cloned.1.call-done = (bf16[1024,512]{1,0:T(8,128)(2,1)}, bf16[1024,512]{1,0:T(8,128)(2,1)}) async-done(((bf16[1024,512]{1,0:T(8,128)(2,1)}, bf16[1024,512]{1,0:T(8,128)(2,1)}), (bf16[1024,512]{1,0:T(8,128)(2,1)}, bf16[1024,512]{1,0:T(8,128)(2,1)})) %all-reduce.6.cloned.1.call-update) | async-done | bytes 2097168 | tf_op jit(solution)/shard_map/psum | solution.py:155
  (228 shorter events, 116.2 us)
Async XLA Ops:
  7.2 53.6 %all-gather.3.cloned.1.call-start = ((), (), s32[]{:S(2)}) async-start(), calls=%async_computation.2 | async-start | bytes 2359296 | tf_op jit(solution)/shard_map/all_gather | solution.py:55
  12.0 344.6 %reduce-scatter.3.cloned.1.call-start = ((), (), s32[]{:S(2)}) async-start(), calls=%async_computation.3 | async-start | bytes 2359296 | tf_op jit(solution)/shard_map/reduce_scatter | solution.py:163
  61.4 11.4 %copy-start = (bf16[2048,512]{1,0:T(8,128)(2,1)S(1)}, bf16[2048,512]{1,0:T(8,128)(2,1)}, u32[]{:S(2)}) copy-start(bf16[2048,512]{1,0:T(8,128)(2,1)} %get-tuple-element.688) | copy-start | bytes 6291460 | tf_op jit(solution)/shard_map/while
  70.0 7.3 %copy-start.2 = (bf16[2,256,512]{2,1,0:T(8,128)(2,1)}, bf16[2,256,512]{2,1,0:T(8,128)(2,1)S(1)}, u32[]{:S(2)}) copy-start(bf16[2,256,512]{2,1,0:T(8,128)(2,1)S(1)} %convolution_convert_fusion.8) | copy-start | bytes 1572868 | tf_op jit(solution)/shard_map/while
  106.1 8.7 %copy-start.1 = (bf16[2,256,2048]{2,1,0:T(8,128)(2,1)S(1)}, bf16[2,256,2048]{2,1,0:T(8,128)(2,1)}, u32[]{:S(2)}) copy-start(bf16[2,256,2048]{2,1,0:T(8,128)(2,1)} %divide_convert_fusion.2) | copy-start | bytes 6291460 | tf_op jit(solution)/shard_map/while
  114.8 5.9 copy-start.7
  114.8 6.2 copy-start.3
  122.1 11.4 %copy-start = (bf16[2048,512]{1,0:T(8,128)(2,1)S(1)}, bf16[2048,512]{1,0:T(8,128)(2,1)}, u32[]{:S(2)}) copy-start(bf16[2048,512]{1,0:T(8,128)(2,1)} %get-tuple-element.688) | copy-start | bytes 6291460 | tf_op jit(solution)/shard_map/while
  130.7 7.3 %copy-start.2 = (bf16[2,256,512]{2,1,0:T(8,128)(2,1)}, bf16[2,256,512]{2,1,0:T(8,128)(2,1)S(1)}, u32[]{:S(2)}) copy-start(bf16[2,256,512]{2,1,0:T(8,128)(2,1)S(1)} %convolution_convert_fusion.8) | copy-start | bytes 1572868 | tf_op jit(solution)/shard_map/while
  167.0 8.7 %copy-start.1 = (bf16[2,256,2048]{2,1,0:T(8,128)(2,1)S(1)}, bf16[2,256,2048]{2,1,0:T(8,128)(2,1)}, u32[]{:S(2)}) copy-start(bf16[2,256,2048]{2,1,0:T(8,128)(2,1)} %divide_convert_fusion.2) | copy-start | bytes 6291460 | tf_op jit(solution)/shard_map/while
  175.7 7.2 %copy-start.7 = (bf16[4,2,128,512]{3,2,1,0:T(8,128)(2,1)S(1)}, bf16[4,2,128,512]{3,2,1,0:T(8,128)(2,1)}, u32[]{:S(2)}) copy-start(bf16[4,2,128,512]{3,2,1,0:T(8,128)(2,1)} %get-tuple-element.654) | copy-start | bytes 3145732 | tf_op jit(solution)/shard_map/while
  175.7 7.4 %copy-start.3 = (bf16[2,128,256]{2,1,0:T(8,128)(2,1)S(1)}, bf16[2,128,256]{2,1,0:T(8,128)(2,1)}, u32[]{:S(2)}) copy-start(bf16[2,128,256]{2,1,0:T(8,128)(2,1)} %convolution_convert_fusion.11) | copy-start | bytes 393220 | tf_op jit(solution)/shard_map/while
  184.2 11.4 %copy-start = (bf16[2048,512]{1,0:T(8,128)(2,1)S(1)}, bf16[2048,512]{1,0:T(8,128)(2,1)}, u32[]{:S(2)}) copy-start(bf16[2048,512]{1,0:T(8,128)(2,1)} %get-tuple-element.688) | copy-start | bytes 6291460 | tf_op jit(solution)/shard_map/while
  192.9 7.3 %copy-start.2 = (bf16[2,256,512]{2,1,0:T(8,128)(2,1)}, bf16[2,256,512]{2,1,0:T(8,128)(2,1)S(1)}, u32[]{:S(2)}) copy-start(bf16[2,256,512]{2,1,0:T(8,128)(2,1)S(1)} %convolution_convert_fusion.8) | copy-start | bytes 1572868 | tf_op jit(solution)/shard_map/while
  229.1 8.7 %copy-start.1 = (bf16[2,256,2048]{2,1,0:T(8,128)(2,1)S(1)}, bf16[2,256,2048]{2,1,0:T(8,128)(2,1)}, u32[]{:S(2)}) copy-start(bf16[2,256,2048]{2,1,0:T(8,128)(2,1)} %divide_convert_fusion.2) | copy-start | bytes 6291460 | tf_op jit(solution)/shard_map/while
  237.8 7.2 %copy-start.7 = (bf16[4,2,128,512]{3,2,1,0:T(8,128)(2,1)S(1)}, bf16[4,2,128,512]{3,2,1,0:T(8,128)(2,1)}, u32[]{:S(2)}) copy-start(bf16[4,2,128,512]{3,2,1,0:T(8,128)(2,1)} %get-tuple-element.654) | copy-start | bytes 3145732 | tf_op jit(solution)/shard_map/while
  237.8 7.4 %copy-start.3 = (bf16[2,128,256]{2,1,0:T(8,128)(2,1)S(1)}, bf16[2,128,256]{2,1,0:T(8,128)(2,1)}, u32[]{:S(2)}) copy-start(bf16[2,128,256]{2,1,0:T(8,128)(2,1)} %convolution_convert_fusion.11) | copy-start | bytes 393220 | tf_op jit(solution)/shard_map/while
  246.3 11.4 %copy-start = (bf16[2048,512]{1,0:T(8,128)(2,1)S(1)}, bf16[2048,512]{1,0:T(8,128)(2,1)}, u32[]{:S(2)}) copy-start(bf16[2048,512]{1,0:T(8,128)(2,1)} %get-tuple-element.688) | copy-start | bytes 6291460 | tf_op jit(solution)/shard_map/while
  255.0 7.3 %copy-start.2 = (bf16[2,256,512]{2,1,0:T(8,128)(2,1)}, bf16[2,256,512]{2,1,0:T(8,128)(2,1)S(1)}, u32[]{:S(2)}) copy-start(bf16[2,256,512]{2,1,0:T(8,128)(2,1)S(1)} %convolution_convert_fusion.8) | copy-start | bytes 1572868 | tf_op jit(solution)/shard_map/while
  291.3 8.7 %copy-start.1 = (bf16[2,256,2048]{2,1,0:T(8,128)(2,1)S(1)}, bf16[2,256,2048]{2,1,0:T(8,128)(2,1)}, u32[]{:S(2)}) copy-start(bf16[2,256,2048]{2,1,0:T(8,128)(2,1)} %divide_convert_fusion.2) | copy-start | bytes 6291460 | tf_op jit(solution)/shard_map/while
  300.0 7.2 %copy-start.7 = (bf16[4,2,128,512]{3,2,1,0:T(8,128)(2,1)S(1)}, bf16[4,2,128,512]{3,2,1,0:T(8,128)(2,1)}, u32[]{:S(2)}) copy-start(bf16[4,2,128,512]{3,2,1,0:T(8,128)(2,1)} %get-tuple-element.654) | copy-start | bytes 3145732 | tf_op jit(solution)/shard_map/while
  300.0 7.4 %copy-start.3 = (bf16[2,128,256]{2,1,0:T(8,128)(2,1)S(1)}, bf16[2,128,256]{2,1,0:T(8,128)(2,1)}, u32[]{:S(2)}) copy-start(bf16[2,128,256]{2,1,0:T(8,128)(2,1)} %convolution_convert_fusion.11) | copy-start | bytes 393220 | tf_op jit(solution)/shard_map/while
  312.3 44.9 %copy-start.12 = (bf16[4,256,128]{1,2,0:T(8,128)(2,1)S(1)}, bf16[4,256,128]{1,2,0:T(8,128)(2,1)}, u32[]{:S(2)}) copy-start(bf16[4,256,128]{1,2,0:T(8,128)(2,1)} %get-tuple-element.237) | copy-start | bytes 786436
  312.3 45.7 %copy-start.11 = (bf16[4,256,256]{1,2,0:T(8,128)(2,1)S(1)}, bf16[4,256,256]{1,2,0:T(8,128)(2,1)}, u32[]{:S(2)}) copy-start(bf16[4,256,256]{1,2,0:T(8,128)(2,1)} %get-tuple-element.235) | copy-start | bytes 1572868
  312.3 46.7 %copy-start.10 = (bf16[4,256,256]{1,2,0:T(8,128)(2,1)S(1)}, bf16[4,256,256]{1,2,0:T(8,128)(2,1)}, u32[]{:S(2)}) copy-start(bf16[4,256,256]{1,2,0:T(8,128)(2,1)} %get-tuple-element.236) | copy-start | bytes 1572868
  312.3 226.6 %copy-start.6 = (bf16[256,512]{1,0:T(8,128)(2,1)S(1)}, bf16[256,512]{1,0:T(8,128)(2,1)}, u32[]{:S(2)}) copy-start(bf16[256,512]{1,0:T(8,128)(2,1)} %param.15) | copy-start | bytes 786436
  312.3 226.5 %copy-start.15 = (f32[512]{0:T(512)S(1)}, f32[512]{0:T(512)}, u32[]{:S(2)}) copy-start(f32[512]{0:T(512)} %copy-done.14) | copy-start | bytes 6148
  312.3 227.7 %copy-start.17 = (f32[256]{0:T(256)S(1)}, f32[256]{0:T(256)}, u32[]{:S(2)}) copy-start(f32[256]{0:T(256)} %copy-done.16) | copy-start | bytes 3076
  312.3 227.7 %copy-start.18 = (f32[256]{0:T(256)S(1)}, f32[256]{0:T(256)}, u32[]{:S(2)}) copy-start(f32[256]{0:T(256)} %get-tuple-element.470) | copy-start | bytes 3076
  312.4 82.8 %reduce-scatter.5.cloned.1.call-start = ((), (), s32[]{:S(2)}) async-start(), calls=%async_computation.5 | async-start | bytes 294912 | tf_op jit(solution)/shard_map/reduce_scatter | solution.py:166
  313.2 225.7 %all-reduce.4.cloned.1.call-start = ((), (), s32[]{:S(2)}) async-start(), calls=%async_computation.4 | async-start | bytes 524288 | tf_op jit(solution)/shard_map/psum | solution.py:159
  356.6 265.0 %all-reduce.6.cloned.1.call-start = ((), (), s32[]{:S(2)}) async-start(), calls=%async_computation.6 | async-start | bytes 4194304 | tf_op jit(solution)/shard_map/psum | solution.py:155
  (19 other events, 35.2 us)
Sparse Core Ops, SparseCore 0:
  12.1 40.3 all-gather.2
  312.5 44.0 reduce-scatter.2
  358.9 36.2 reduce-scatter.4
  397.6 141.1 all-reduce.3
  541.8 79.6 all-reduce.5
where the time goes:
time: 638 us; the launch traced here: 633 us
  waiting for transfers between devices  237 us (37%)
  matrix products  185 us (29%)
  blocking collectives  109 us (17%)
  local copies, waits for them, and re-layouts  43.4 us (7%)
  other arithmetic  38 us (6%)
  between operations  13.9 us (2%)
    psum x1, waiting for transfers between devices, on_device(): lax.psum(local_wk.astype(jnp.bfloat16), 'ctx').astype(jnp.float32)  79.7 us
    psum x1, waiting for transfers between devices, on_device(): lax.psum(d_normed.astype(jnp.bfloat16), 'head').astype(jnp.float32)  78.3 us
    psum x1, blocking collectives, on_device(): lax.psum(d_rope.astype(jnp.bfloat16), 'head').astype(jnp.float32)  65.4 us
    reduce_scatter x1, waiting for transfers between devices, on_device(): lax.psum_scatter(headed_lat.astype(jnp.bfloat16), 'ctx', scatter_dimensio...  43.3 us
    reduce_scatter x1, waiting for transfers between devices, on_device(): lax.psum_scatter(headed_rope.astype(jnp.bfloat16), 'ctx', scatter_dimensi...  35.1 us
    dot_general x4, matrix products, one_pair(): jnp.einsum('hqk,hql->kl', dscores, q_lat, preferred_element_type=jnp.floa...  34.7 us
    dot_general x4, matrix products, one_pair(): jnp.einsum('qhr,hqk->rk', query_r, dscores, preferred_element_type=jnp.fl...  27.4 us
    dot_general x4, matrix products, one_pair(): jnp.einsum('hqk,hql->kl', attention, do_lat, preferred_element_type=jnp.f...  26.2 us
  transfers between devices with their start and end apart: 5, of which 4 were waited for; matrix products, arithmetic and copies ran while one was open for 2% of the time, Pallas kernels for 0%

commit v1 on v0

v1 whole, which is shorter than its diff:
```python
import functools
import math

import jax
import jax.numpy as jnp
from jax import lax
from jax.experimental import pallas as pl
from jax.experimental.pallas import tpu as pltpu
from jax.sharding import Mesh
from jax.sharding import PartitionSpec as P

D_LAT = 512
D_ROPE = 64
D_NOPE = 128
D_V = 128
GROUPS = 2
COMP = 8
CODES = GROUPS * (COMP + 1)
TOKENS = 2048
CTX = 8
ROWS = TOKENS // CTX
BLOCK = 16
TILE = 256
MAX_TILES = 6
WIDE = (3,)
PACK = 640
EXTRA = PACK - D_LAT
PAD_COL = PACK - 1
HIDE = -1e30
SCALING = 1.0 / math.sqrt(D_NOPE + D_ROPE)
BF = jnp.bfloat16
F32 = jnp.float32
CTX_AXES = ("xl", "z")
HEAD_AXES = ("xh", "y", "core")
LOCAL = pltpu.VMEM


def dot(a, b):
    return lax.dot_general(a, b, (((1,), (0,)), ((), ())), preferred_element_type=F32)


def dot_nt(a, b):
    return lax.dot_general(a, b, (((1,), (1,)), ((), ())), preferred_element_type=F32)


def attention_kernel(*refs):
    info, own, mine, other, bias, weight, qn, qr, do, wk, wv = refs[:11]
    out, dqn, dqr, dw, kept, sent = refs[11:17]
    keys, acc, kf, vv, s, dp, e, qf, qt, gb, git, wb, wt, wgrad, meta = refs[17:]
    step = pl.program_id(0)

    def key_rows(t):
        return pl.ds(pl.multiple_of(t * TILE, TILE), TILE)

    @pl.when(step == 0)
    def _():
        chunk, core, group, comp = info[0], info[1], info[2], info[3]
        inside, length, len0, len1 = info[4], info[5], info[6], info[7]
        tags = jnp.sum(
            mine[:, D_LAT:].astype(F32) + other[:, D_LAT:].astype(F32), axis=0, keepdims=True
        )
        lane = lax.broadcasted_iota(jnp.int32, tags.shape, 1) - D_ROPE
        start1 = jnp.sum(jnp.where((lane >= 0) & (lane < COMP + 1), tags, 0.0)).astype(jnp.int32)
        begin = chunk * ROWS
        low1 = jnp.where(group == 0, 0, start1)
        high1 = jnp.minimum(jnp.where(group == 0, start1 - len0, TOKENS - len1), begin)
        block1 = low1 // BLOCK
        n1 = jnp.where(high1 > low1, (high1 + BLOCK - 1) // BLOCK - block1, 0)
        prior = jnp.where(comp > 0, length - inside, 0)
        block2 = jnp.maximum((begin - prior) // BLOCK, jnp.where(n1 > 0, block1 + n1, 0))
        count = n1 + jnp.maximum(begin // BLOCK - block2, 0)
        count = jnp.minimum(count, (MAX_TILES - 1) * (TILE // BLOCK))
        tiles = 1 + (count + TILE // BLOCK - 1) // (TILE // BLOCK)
        meta[0], meta[1], meta[2], meta[3], meta[4] = tiles, n1, block1, block2, count
        keys[0:ROWS, :] = own[...]

        def copy_block(index, carry):
            block = jnp.where(index < n1, block1 + index, block2 + index - n1)
            place = (block // 16) * 8 + block % 8
            rows = pl.ds(pl.multiple_of(place * BLOCK, BLOCK), BLOCK)
            from_mine = ((block % 16) // 8 == core).astype(jnp.int32)
            keys[pl.ds(pl.multiple_of(ROWS + index * BLOCK, BLOCK), BLOCK), :] = jnp.where(
                from_mine == 1, mine[rows, :], other[rows, :]
            )
            return carry

        lax.fori_loop(0, count, copy_block, 0)
        filler = (lax.broadcasted_iota(jnp.int32, (BLOCK, PACK), 1) == PAD_COL).astype(F32).astype(BF)

        def pad_block(index, carry):
            keys[pl.ds(pl.multiple_of(ROWS + index * BLOCK, BLOCK), BLOCK), :] = filler
            return carry

        lax.fori_loop(count, (tiles - 1) * (TILE // BLOCK), pad_block, 0)

        def start_acc(t, carry):
            acc[:, key_rows(t)] = jnp.zeros((acc.shape[0], TILE), F32)
            return carry

        lax.fori_loop(0, tiles, start_acc, 0)

    tiles = meta[0]

    def each_tile(body, carry):
        return lax.fori_loop(0, tiles, body, carry)

    row_weight = weight[...]
    for h in range(2):
        nope = qn[:, h * D_NOPE : (h + 1) * D_NOPE]
        rope = qr[:, h * D_ROPE : (h + 1) * D_ROPE]
        qf[h] = jnp.concatenate([nope, rope, bias[...]], axis=1)
        qt[h] = jnp.concatenate([nope.T, rope.T], axis=0)
        gb[h] = (do[:, h * D_V : (h + 1) * D_V].astype(F32) * row_weight).astype(BF)
        w_head = jnp.concatenate(
            [wk[h * D_NOPE : (h + 1) * D_NOPE, :], wv[h * D_V : (h + 1) * D_V, :]], axis=0
        )
        wb[h * 256 : (h + 1) * 256, :] = w_head
        wt[:, h * 256 : (h + 1) * 256] = w_head.T

    base2 = SCALING * math.log2(math.e)

    def finish_heads(dq, grad):
        for h in range(2):
            dqn[:, h * D_NOPE : (h + 1) * D_NOPE] = dq[h][:, :D_NOPE].astype(BF)
            dw[0, h * D_NOPE : (h + 1) * D_NOPE] = grad[h * 256 : h * 256 + 128].astype(BF)
            dw[1, h * D_V : (h + 1) * D_V] = grad[h * 256 + 128 : (h + 1) * 256].astype(BF)
        dqr[...] = jnp.concatenate(
            [dq[h][:, D_NOPE : D_NOPE + D_ROPE] for h in range(2)], axis=1
        ).astype(BF)

    def wide_step(count):
        width = count * TILE
        all_keys = keys[:width, :]
        both = dot_nt(all_keys[:, :D_LAT], wb[...]).astype(BF)
        shown = lax.broadcasted_iota(jnp.int32, (ROWS, TILE), 1) <= lax.broadcasted_iota(
            jnp.int32, (ROWS, TILE), 0
        )
        parts, rope_sum, dq = [], None, []
        for h in range(2):
            k_full = jnp.concatenate(
                [both[:, h * 256 : h * 256 + 128], all_keys[:, D_LAT:]], axis=1
            )
            value = both[:, h * 256 + 128 : (h + 1) * 256]
            score = dot_nt(qf[h], k_full)
            score = jnp.concatenate(
                [jnp.where(shown, score[:, :TILE], HIDE), score[:, TILE:]], axis=1
            )
            shift = jnp.max(score, axis=1, keepdims=True) * base2
            expo = jnp.exp2(score * base2 - shift)
            inv = 1.0 / jnp.sum(expo, axis=1, keepdims=True)
            expo = expo.astype(BF)
            mixed = dot(expo, value) * inv
            out[:, h * D_V : (h + 1) * D_V] = mixed.astype(BF)
            g = gb[h].astype(F32)
            row_dot = jnp.sum(mixed * g, axis=1, keepdims=True)
            slope = inv * SCALING
            offset = row_dot * slope
            dprobs = dot_nt(gb[h], value)
            ds = (expo.astype(F32) * (dprobs * slope - offset)).astype(BF)
            dq.append(dot(ds, k_full))
            dk = dot(qt[h], ds)
            dv = dot((g * inv).astype(BF).T, expo)
            parts += [dk[:D_NOPE].astype(BF), dv.astype(BF)]
            rope_sum = dk[D_NOPE:] if h == 0 else rope_sum + dk[D_NOPE:]
        dkv = jnp.concatenate(parts, axis=0)
        acc[:D_LAT, :width] += dot(wt[...], dkv)
        acc[D_LAT:, :width] += rope_sum
        finish_heads(dq, dot(dkv, all_keys[:, :D_LAT]))

    def loop_step():
        row = lax.broadcasted_iota(jnp.int32, (ROWS, TILE), 0)
        col = lax.broadcasted_iota(jnp.int32, (ROWS, TILE), 1)

        def score_tile(t, maxima):
            tile_keys = keys[key_rows(t), :]
            both = dot_nt(tile_keys[:, :D_LAT], wb[...]).astype(BF)
            shown = col <= row + t * (MAX_TILES * TILE)
            new = []
            for h in range(2):
                k_nope = both[:, h * 256 : h * 256 + 128]
                value = both[:, h * 256 + 128 : (h + 1) * 256]
                k_full = jnp.concatenate([k_nope, tile_keys[:, D_LAT:]], axis=1)
                kf[h, t] = k_full
                vv[h, t] = value
                score = jnp.where(shown, dot_nt(qf[h], k_full), HIDE)
                s[h, t] = score
                dp[h, t] = dot_nt(gb[h], value)
                new.append(jnp.maximum(maxima[h], jnp.maximum(score[:, :128], score[:, 128:])))
            return tuple(new)

        low = jnp.full((ROWS, 128), HIDE, F32)
        maxima = each_tile(score_tile, (low, low))
        shifts = [jnp.max(m, axis=1, keepdims=True) * base2 for m in maxima]

        def prob_tile(t, carry):
            new = []
            for h in range(2):
                total, mixed = carry[h]
                expo = jnp.exp2(s[h, t] * base2 - shifts[h])
                total = total + (expo[:, :128] + expo[:, 128:])
                expo = expo.astype(BF)
                e[h, t] = expo
                new.append((total, mixed + dot(expo, vv[h, t])))
            return tuple(new)

        nothing = jnp.zeros((ROWS, 128), F32)
        mixes = each_tile(prob_tile, ((nothing, nothing), (nothing, nothing)))
        slopes, offsets = [], []
        for h in range(2):
            total, mixed = mixes[h]
            inv = 1.0 / jnp.sum(total, axis=1, keepdims=True)
            mixed = mixed * inv
            out[:, h * D_V : (h + 1) * D_V] = mixed.astype(BF)
            g = gb[h].astype(F32)
            row_dot = jnp.sum(mixed * g, axis=1, keepdims=True)
            slopes.append(inv * SCALING)
            offsets.append(row_dot * (inv * SCALING))
            git[h] = (g * inv).astype(BF).T

        wgrad[...] = jnp.zeros(wgrad.shape, F32)

        def back_tile(t, carry):
            tile_keys = keys[key_rows(t), :D_LAT]
            parts, rope_sum, new = [], None, []
            for h in range(2):
                expo = e[h, t]
                ds = (expo.astype(F32) * (dp[h, t] * slopes[h] - offsets[h])).astype(BF)
                new.append(carry[h] + dot(ds, kf[h, t]))
                dk = dot(qt[h], ds)
                dv = dot(git[h], expo)
                parts += [dk[:D_NOPE].astype(BF), dv.astype(BF)]
                rope_sum = dk[D_NOPE:] if h == 0 else rope_sum + dk[D_NOPE:]
            dkv = jnp.concatenate(parts, axis=0)
            acc[:D_LAT, key_rows(t)] += dot(wt[...], dkv)
            acc[D_LAT:, key_rows(t)] += rope_sum
            wgrad[...] += dot(dkv, tile_keys)
            return tuple(new)

        empty = jnp.zeros((ROWS, 256), F32)
        dq = each_tile(back_tile, (empty, empty))
        finish_heads(dq, wgrad[...])

    for count in WIDE:

        @pl.when(tiles == count)
        def _(count=count):
            wide_step(count)

    @pl.when(functools.reduce(lambda x, y: x & y, [tiles != count for count in WIDE]))
    def _():
        loop_step()

    @pl.when(step == pl.num_programs(0) - 1)
    def _():
        chunk, core = info[0], info[1]
        n1, block1, block2, count = meta[1], meta[2], meta[3], meta[4]
        kept[...] = jnp.zeros(kept.shape, BF)
        sent[...] = jnp.zeros(sent.shape, BF)

        def turn(t, carry):
            keys[key_rows(t), :D_LAT] = acc[:D_LAT, key_rows(t)].astype(BF).T
            keys[key_rows(t), D_LAT:] = jnp.concatenate(
                [acc[D_LAT:, key_rows(t)].astype(BF), jnp.zeros((EXTRA - D_ROPE, TILE), BF)], axis=0
            ).T
            return carry

        lax.fori_loop(0, tiles, turn, 0)

        def place(index, carry):
            past = index - ROWS // BLOCK
            block = jnp.where(past < n1, block1 + past, block2 + past - n1)
            block = jnp.where(past < 0, chunk * (ROWS // BLOCK) + index, block)
            pair = block // 2
            where = (pair % 4) * 16 + ((pair // 8) % 4) * 4 + (pair // 32) * 2 + (pair // 4) % 2
            rows = pl.ds(pl.multiple_of(where * BLOCK, BLOCK), BLOCK)
            values = keys[pl.ds(pl.multiple_of(index * BLOCK, BLOCK), BLOCK), :]

            @pl.when((block + core) % 2 == 0)
            def _():
                kept[rows, :] = values

            @pl.when((block + core) % 2 == 1)
            def _():
                sent[rows, :] = values

            return carry

        lax.fori_loop(0, ROWS // BLOCK + count, place, 0)


def attention(shared, q_nope, q_rope, d_out, w_uk, w_uv):
    rows = q_nope.shape[0]
    pairs = w_uk.shape[0] // (2 * D_NOPE)

    def columns(size):
        return pl.BlockSpec((rows, size), lambda i: (0, i))

    def heads(size):
        return pl.BlockSpec((size, D_LAT), lambda i: (i, 0))

    whole = pl.BlockSpec(memory_space=pltpu.VMEM)
    in_specs = [pl.BlockSpec(memory_space=pltpu.SMEM)] + [whole] * 5
    in_specs += [columns(256), columns(128), columns(256), heads(256), heads(256)]
    half = jax.ShapeDtypeStruct((TOKENS // 2, PACK), BF)
    return pl.pallas_call(
        attention_kernel,
        grid=(pairs,),
        in_specs=in_specs,
        out_specs=[
            columns(256),
            columns(256),
            columns(128),
            pl.BlockSpec((2, 256, D_LAT), lambda i: (0, i, 0)),
            whole,
            whole,
        ],
        out_shape=[
            jax.ShapeDtypeStruct(q_nope.shape, BF),
            jax.ShapeDtypeStruct(q_nope.shape, BF),
            jax.ShapeDtypeStruct(q_rope.shape, BF),
            jax.ShapeDtypeStruct((2, pairs * 256, D_LAT), BF),
            half,
            half,
        ],
        scratch_shapes=[
            pltpu.VMEM((MAX_TILES * TILE, PACK), BF),
            pltpu.VMEM((D_LAT + D_ROPE, MAX_TILES * TILE), F32),
            pltpu.VMEM((2, MAX_TILES, TILE, 256), BF),
            pltpu.VMEM((2, MAX_TILES, TILE, D_V), BF),
            pltpu.VMEM((2, MAX_TILES, ROWS, TILE), F32),
            pltpu.VMEM((2, MAX_TILES, ROWS, TILE), F32),
            pltpu.VMEM((2, MAX_TILES, ROWS, TILE), BF),
            pltpu.VMEM((2, ROWS, 256), BF),
            pltpu.VMEM((2, D_NOPE + D_ROPE, ROWS), BF),
            pltpu.VMEM((2, ROWS, D_V), BF),
            pltpu.VMEM((2, D_V, ROWS), BF),
            pltpu.VMEM((512, D_LAT), BF),
            pltpu.VMEM((D_LAT, 512), BF),
            pltpu.VMEM((512, D_LAT), F32),
            pltpu.SMEM((8,), jnp.int32),
        ],
        compiler_params=pltpu.CompilerParams(vmem_limit_bytes=56 << 20),
        cost_estimate=pl.CostEstimate(
            flops=pairs * 2600000000, bytes_accessed=16 << 20, transcendentals=pairs * 400000
        ),
        name="attention",
    )(*shared, q_nope, q_rope, d_out, w_uk, w_uv)


def prepare_kernel(latent, gain, rope_t, gid, cid, gid_s, cid_s, lengths, own, send, bias, weight, inverse, info):
    chunk = lax.axis_index("xl") * 4 + lax.axis_index("z")
    core = lax.axis_index("core")
    latent_f = latent[...].astype(F32)
    inv = lax.rsqrt(jnp.mean(latent_f * latent_f, axis=1, keepdims=True) + 1e-06)
    inverse[...] = inv
    normed = (latent_f * inv * gain[...].astype(F32)).astype(BF)
    group = jnp.broadcast_to(gid[...].astype(F32), (8, ROWS)).T[:, :1].astype(jnp.int32)
    comp = jnp.broadcast_to(cid[...].astype(F32), (8, ROWS)).T[:, :1].astype(jnp.int32)
    code = group * (COMP + 1) + comp
    column = lax.broadcasted_iota(jnp.int32, (ROWS, EXTRA - D_ROPE), 1)
    tags = jnp.where(column == code, 1.0, 0.0).astype(BF)
    seen = (column == code) | (column == group * (COMP + 1))
    bias[...] = jnp.where(seen, 0.0, HIDE).astype(BF)
    own[...] = jnp.concatenate([normed, rope_t[...].T, tags], axis=1)
    half = own[pl.ds(pl.multiple_of(core * (ROWS // 2), ROWS // 2), ROWS // 2), :]
    for i in range(CTX):
        send[i] = half
    length = jnp.ones((ROWS, 1), F32)
    for g in range(GROUPS):
        for k in range(COMP):
            length = jnp.where(code == g * (COMP + 1) + k + 1, lengths[g, k].astype(F32), length)
    weight[...] = jnp.where(comp > 0, 64.0 / length, 0.0)
    group0, comp0 = gid_s[0], cid_s[0]
    info[0], info[1], info[2], info[3] = chunk, core, group0, comp0
    info[4] = jnp.sum(
        jnp.where(gid[...] * (COMP + 1) + cid[...] == group0 * (COMP + 1) + comp0, 1.0, 0.0)
    ).astype(jnp.int32)
    info[5] = lengths[group0, jnp.maximum(comp0 - 1, 0)]
    for g in range(GROUPS):
        info[6 + g] = sum([lengths[g, k] for k in range(1, COMP)], lengths[g, 0])


def prepare(latent, latent_gain, k_rope_t, group_ids, comp_ids, comp_lengths):
    vector = pl.BlockSpec(memory_space=LOCAL)
    scalar = pl.BlockSpec(memory_space=pltpu.SMEM)
    return pl.pallas_call(
        prepare_kernel,
        in_specs=[vector] * 5 + [scalar] * 3,
        out_specs=[vector] * 5 + [scalar],
        out_shape=[
            jax.ShapeDtypeStruct((ROWS, PACK), BF),
            jax.ShapeDtypeStruct((CTX, ROWS // 2, PACK), BF),
            jax.ShapeDtypeStruct((ROWS, EXTRA - D_ROPE), BF),
            jax.ShapeDtypeStruct((ROWS, 1), F32),
            jax.ShapeDtypeStruct((ROWS, 1), F32),
            jax.ShapeDtypeStruct((8,), jnp.int32),
        ],
        name="prepare",
    )(
        latent,
        latent_gain[None, :],
        k_rope_t,
        group_ids[None, :],
        comp_ids[None, :],
        group_ids,
        comp_ids,
        comp_lengths,
    )


def relative(axis, distance):
    if axis == "x":
        return (lax.axis_index("xl") * 2 + lax.axis_index("xh")) ^ distance
    return (lax.axis_index(axis) + distance) & 3


def move(x, axis, distance):
    if axis == "x":
        names = ("xl", "xh")
        return lax.ppermute(x, names, [(i, i ^ distance) for i in range(4)])
    return lax.ppermute(x, axis, [(i, (i + distance) % 4) for i in range(4)])


def fold_kernel(axis, count, *refs):
    parts, outs = refs[:count], refs[count:]
    size = outs[0].shape[0]
    for distance in range(4):
        start = pl.multiple_of(relative(axis, distance) * size, BLOCK)
        total = parts[0][pl.ds(start, size), :].astype(F32)
        for part in parts[1:]:
            total = total + part[pl.ds(start, size), :].astype(F32)
        outs[distance][...] = total.astype(BF)


def fold(axis, parts):
    vector = pl.BlockSpec(memory_space=LOCAL)
    shape = jax.ShapeDtypeStruct((parts[0].shape[0] // 4, PACK), BF)
    return pl.pallas_call(
        functools.partial(fold_kernel, axis, len(parts)),
        in_specs=[vector] * len(parts),
        out_specs=[vector] * 4,
        out_shape=[shape] * 4,
        name="fold_" + axis,
    )(*parts)


def scatter(axis, parts):
    cut = fold(axis, parts)
    return [cut[0]] + [move(cut[d], axis, d) for d in (2, 1, 3)]


def finish_kernel(a, b, c, d, latent, inverse, gain, out):
    head = lax.axis_index("xh") * 8 + lax.axis_index("y") * 2 + lax.axis_index("core")
    rows = pl.ds(pl.multiple_of(head * BLOCK, BLOCK), BLOCK)
    total = a[...].astype(F32) + b[...].astype(F32) + c[...].astype(F32) + d[...].astype(F32)
    lifted = total[:, :D_LAT] * gain[...].astype(F32)
    own, inv = latent[rows, :].astype(F32), inverse[rows, :]
    centred = jnp.mean(lifted * own, axis=1, keepdims=True)
    out[:, :D_LAT] = (inv * lifted - own * inv**3 * centred).astype(BF)
    out[:, D_LAT:] = total[:, D_LAT:].astype(BF)


def finish(parts, latent, inverse, latent_gain):
    vector = pl.BlockSpec(memory_space=LOCAL)
    return pl.pallas_call(
        finish_kernel,
        in_specs=[vector] * 7,
        out_specs=vector,
        out_shape=jax.ShapeDtypeStruct((BLOCK, PACK), BF),
        name="finish",
    )(*parts, latent, inverse, latent_gain[None, :])


def assemble_kernel(*refs):
    pieces, out, rope = refs[:16], refs[16], refs[17]
    xh, y, core = lax.axis_index("xh"), lax.axis_index("y"), lax.axis_index("core")
    everything = []
    for index, piece in enumerate(pieces):
        other, place = index // 8, index % 8
        head = (xh ^ (place // 4)) * 8 + ((y - place % 4) & 3) * 2 + (core ^ other)
        rows = pl.ds(pl.multiple_of(head * BLOCK, BLOCK), BLOCK)
        out[rows, :] = piece[:, :D_LAT]
        refs[18][rows, :] = piece[:, D_LAT:].astype(F32)
    rope[...] = refs[18][...].T[:D_ROPE].astype(BF)


def assemble(pieces):
    vector = pl.BlockSpec(memory_space=LOCAL)
    return pl.pallas_call(
        assemble_kernel,
        in_specs=[vector] * 16,
        out_specs=[vector] * 2,
        out_shape=[
            jax.ShapeDtypeStruct((ROWS, D_LAT), BF),
            jax.ShapeDtypeStruct((D_ROPE, ROWS), BF),
        ],
        scratch_shapes=[pltpu.VMEM((ROWS, EXTRA), F32)],
        name="assemble",
    )(*pieces)


def total_kernel(pieces, out):
    total = pieces[0].astype(F32)
    for i in range(1, CTX):
        total = total + pieces[i].astype(F32)
    total = total.astype(BF)
    for i in range(CTX):
        out[i] = total


def total_and_copy(pieces):
    count, rows, width = pieces.shape
    spec = pl.BlockSpec((count, rows // 4, width), lambda i: (0, i, 0))
    return pl.pallas_call(
        total_kernel,
        grid=(4,),
        in_specs=[spec],
        out_specs=spec,
        out_shape=jax.ShapeDtypeStruct(pieces.shape, BF),
        name="total",
    )(pieces)


def swap_core(x):
    return lax.ppermute(x, "core", [(0, 1), (1, 0)])


def exchange(x, axes):
    return lax.all_to_all(x, axes, 0, 0, tiled=True)


def on_device(
    q_nope,
    q_rope,
    latent,
    latent_gain,
    k_rope_t,
    w_uk,
    w_uv,
    d_out,
    group_ids,
    comp_ids,
    comp_lengths,
):
    own, send, bias, weight, inverse, info = prepare(
        latent, latent_gain, k_rope_t, group_ids, comp_ids, comp_lengths
    )
    mine = exchange(send, CTX_AXES).reshape(-1, PACK)
    other = swap_core(mine)
    shared = (info, own, mine, other, bias, weight)
    out, dqn, dqr, dw, kept, sent = attention(shared, q_nope, q_rope, d_out, w_uk, w_uv)
    pieces = exchange(dw.reshape(CTX, -1, D_LAT), CTX_AXES)
    total = total_and_copy(pieces)
    parts = scatter("y", [kept, swap_core(sent)])
    parts, total = lax.optimization_barrier((parts, total))
    weights = exchange(total, CTX_AXES).reshape(2, -1, D_LAT)
    parts = scatter("x", scatter("z", parts))
    final = finish(parts, latent, inverse, latent_gain)
    pieces = [final] + [
        lax.ppermute(
            final,
            ("xh", "y"),
            [(i, ((i // 4) ^ (d // 4)) * 4 + (i + d) % 4) for i in range(8)],
        )
        for d in range(1, 8)
    ]
    swapped = swap_core(jnp.stack(pieces))
    d_latent, d_k_rope_t = assemble(pieces + [swapped[i] for i in range(8)])
    return out, dqn, dqr, d_latent, d_k_rope_t, weights[0], weights[1]


def solution(mesh):
    fine = Mesh(mesh.devices.reshape(2, 4, 2, 4, 2), CTX_AXES + HEAD_AXES)
    return jax.shard_map(
        on_device,
        mesh=fine,
        in_specs=(
            P(CTX_AXES, HEAD_AXES),
            P(CTX_AXES, HEAD_AXES),
            P(CTX_AXES, None),
            P(),
            P(None, CTX_AXES),
            P(HEAD_AXES, None),
            P(HEAD_AXES, None),
            P(CTX_AXES, HEAD_AXES),
            P(CTX_AXES),
            P(CTX_AXES),
            P(),
        ),
        out_specs=(
            P(CTX_AXES, HEAD_AXES),
            P(CTX_AXES, HEAD_AXES),
            P(CTX_AXES, HEAD_AXES),
            P(CTX_AXES, None),
            P(None, CTX_AXES),
            P(HEAD_AXES, None),
            P(HEAD_AXES, None),
        ),
        check_vma=False,
    )
```

time: 638 us -> 149 us (0.23)
  waiting for transfers between devices: 237 us -> 34.3 us
  matrix products: 185 us -> 0 us
  blocking collectives: 109 us -> 23.9 us
  starting transfers between devices: 0.2 us -> 46.4 us
  other arithmetic: 38 us -> 0 us
  Pallas kernels: 0 us -> 33.6 us
  local copies, waits for them, and re-layouts: 43.4 us -> 9.97 us
  between operations: 13.9 us -> 0.83 us
    dot_general x60 -> x0, matrix products: 185 us -> none  [the longest x4 34.7 us: one_pair(): jnp.einsum('hqk,hql->kl', dscores, q_lat, preferred_element_type=jnp.floa...]
    psum x2 -> x0, waiting for transfers between devices: 158 us -> none  [the longest x1 79.7 us: on_device(): lax.psum(local_wk.astype(jnp.bfloat16), 'ctx').astype(jnp.float32)]
    reduce_scatter x2 -> x0, waiting for transfers between devices: 78.5 us -> none  [the longest x1 43.3 us: on_device(): lax.psum_scatter(headed_lat.astype(jnp.bfloat16), 'ctx', scatter_dimensio...]
    psum x1 -> x0, blocking collectives: 65.4 us -> none  [on_device(): lax.psum(d_rope.astype(jnp.bfloat16), 'head').astype(jnp.float32)]
    all_gather x2 -> x0, blocking collectives: 44 us -> none  [the longest x1 26.1 us: on_device(): lax.all_gather(k_rope_t, 'ctx', axis=1, tiled=True)]
    pallas_call x0 -> x8, Pallas kernels: none -> 33.6 us  [the longest x1 16.8 us: attention(): pl.pallas_call(attention_kernel, grid=(pairs,), in_specs=in_specs, out_sp...]
    ppermute x0 -> x19, starting transfers between devices: none -> 33 us  [the longest x7 12 us: on_device(): lax.ppermute(final, ('xh', 'y'), [(i, (i // 4 ^ d // 4) * 4 + (i + d) % 4...]
    dynamic_slice x36 -> x0, local copies, waits for them, and re-layouts: 27.9 us -> none  [the longest x8 6.37 us: one_pair(): lax.dynamic_slice_in_dim(q_rope, pair_index * 2 * D_ROPE, 2 * D_ROPE, 1)]
  transfers between devices with their start and end apart: 5 -> 21, of which waited for: 4 -> 12; matrix products, arithmetic and copies ran while one was open for 2% -> 1% of each run, Pallas kernels for 0% -> 7%
where the time goes in v1:
time: 149 us
  starting transfers between devices  46.4 us (31%)
  waiting for transfers between devices  34.3 us (23%)
  Pallas kernels  33.6 us (23%)
  blocking collectives  23.9 us (16%)
  local copies, waits for them, and re-layouts  9.97 us (7%)
    all_to_all x1, blocking collectives, exchange(): return lax.all_to_all(x, axes, 0, 0, tiled=True)  23.9 us
    pallas_call x1, Pallas kernels, attention(): pl.pallas_call(attention_kernel, grid=(pairs,), in_specs=in_specs, out_sp...  16.8 us
    all_to_all x2, starting transfers between devices, exchange(): return lax.all_to_all(x, axes, 0, 0, tiled=True)  13.4 us
    all_to_all x2, waiting for transfers between devices, exchange(): return lax.all_to_all(x, axes, 0, 0, tiled=True)  13.1 us
    ppermute x7, starting transfers between devices, on_device(): lax.ppermute(final, ('xh', 'y'), [(i, (i // 4 ^ d // 4) * 4 + (i + d) % 4...  12 us
    ppermute x7, waiting for transfers between devices, on_device(): lax.ppermute(final, ('xh', 'y'), [(i, (i // 4 ^ d // 4) * 4 + (i + d) % 4...  11.1 us
    ppermute x6, starting transfers between devices, move(): return lax.ppermute(x, axis, [(i, (i + distance) % 4) for i in range(4)])  9.15 us
    ppermute x3, starting transfers between devices, swap_core(): return lax.ppermute(x, 'core', [(0, 1), (1, 0)])  7.55 us
  transfers between devices with their start and end apart: 21, of which 12 were waited for; matrix products, arithmetic and copies ran while one was open for 1% of the time, Pallas kernels for 7%

profile of v1, /device:TPU:1, one launch (start us, length us, event | category | flops | bytes accessed | tf_op | source)
XLA Modules:
  0.0 149.0 jit_solution(10462744361760692055)
XLA Ops:
  1.9 2.8 %prepare.1 = (bf16[256,640]{1,0:T(8,128)(2,1)}, bf16[8,128,640]{2,1,0:T(8,128)(2,1)}, bf16[256,64]{1,0:T(8,128)(2,1)}, f32[256,1]{1,0:T(8,128)}, f32[256,1]{1,0:T(8,128)}, /*index=5*/s32[8]{0:T(128)}) custom-call(bf16[256,512]{1,0:T(8,128)(2,1)} %latent.3, bf16[1,512]{1,0:T(2,128)(2,1)} %broadcast_in_dim.10.gain, bf16[64,256]{1,0:T(8,128)(2,1)} %rope_t.1, ...), custom_call_target="tpu_custom_call" | custom-call | tf_op jit(solution)/shard_map/prepare/pallas_call | solution.py:386
  4.7 23.9 %all_to_all.15 = bf16[8,128,640]{2,1,0:T(8,128)(2,1)S(1)} all-to-all(bf16[8,128,640]{2,1,0:T(8,128)(2,1)} %get-tuple-element.40), channel_id=1, replica_groups=mesh['xl'=2,'z'=4,'xh'=2,'y'=4,'core'=2] {'xl','z'}, dimensions={0} | all-to-all | bytes 2621440 | tf_op jit(solution)/shard_map/all_to_all | solution.py:529
  28.6 2.4 %collective-permute-start = (bf16[1024,640]{1,0:T(8,128)(2,1)S(1)}, bf16[1024,640]{1,0:T(8,128)(2,1)S(1)}, u32[]{:S(2)}, u32[]{:S(2)}) collective-permute-start(bf16[1024,640]{1,0:T(8,128)(2,1)S(1)} %bitcast.39), channel_id=1, source_target_pairs={{0,1},{1,0},{2,3},{3,2},{4,5},{5,4},{6,7},{7,6},{8,9},{9,8},{10,11... | collective-permute-start | bytes 3932168 | tf_op jit(solution)/shard_map/ppermute | solution.py:525
  31.1 2.7 %collective-permute-done.refs_3_ = bf16[1024,640]{1,0:T(8,128)(2,1)S(1)} collective-permute-done((bf16[1024,640]{1,0:T(8,128)(2,1)S(1)}, bf16[1024,640]{1,0:T(8,128)(2,1)S(1)}, u32[]{:S(2)}, u32[]{:S(2)}) %collective-permute-start) | collective-permute-done | bytes 1310752 | tf_op jit(solution)/shard_map/ppermute | solution.py:525
  34.8 16.8 %attention.1 = (bf16[256,1024]{1,0:T(8,128)(2,1)}, bf16[256,1024]{1,0:T(8,128)(2,1)}, bf16[256,512]{1,0:T(8,128)(2,1)}, bf16[2,1024,512]{2,1,0:T(8,128)(2,1)}, b...) custom-call(s32[8]{0:T(128)} %get-tuple-element.38.refs_0_, bf16[256,640]{1,0:T(8,128)(2,1)} %get-tuple-element.39.refs_1_, ...), custom_call_target="tpu_custom_call" | custom-call | flops 10400000000 | bytes 16777216 | tf_op jit(solution)/shard_map/attention/pallas_call | solution.py:305
  51.6 9.8 %all-to-all-start.1 = ((bf16[8,256,512]{2,1,0:T(8,128)(2,1)}), bf16[8,256,512]{2,1,0:T(8,128)(2,1)S(1)}, u32[]{:S(2)}, u32[]{:S(2)}) async-start(bf16[8,256,512]{2,1,0:T(8,128)(2,1)} %bitcast.38), calls=%async_computation.1 | async-start | bytes 4194304 | tf_op jit(solution)/shard_map/all_to_all | solution.py:529
  62.1 2.9 %collective-permute-done.1.refs_1_ = bf16[1024,640]{1,0:T(8,128)(2,1)S(1)} collective-permute-done((bf16[1024,640]{1,0:T(8,128)(2,1)}, bf16[1024,640]{1,0:T(8,128)(2,1)S(1)}, u32[]{:S(2)}, u32[]{:S(2)}) %collective-permute-start.1) | collective-permute-done | bytes 1310752 | tf_op jit(solution)/shard_map/ppermute | solution.py:525
  66.0 2.9 %fold_y.1 = (bf16[256,640]{1,0:T(8,128)(2,1)}, bf16[256,640]{1,0:T(8,128)(2,1)}, bf16[256,640]{1,0:T(8,128)(2,1)}, bf16[256,640]{1,0:T(8,128)(2,1)}) custom-call(bf16[1024,640]{1,0:T(8,128)(2,1)} %get-tuple-element.46.refs_0_, bf16[1024,640]{1,0:T(8,128)(2,1)} %copy-done.2), custom_call_target="tpu_custom_call" | custom-call | tf_op jit(solution)/shard_map/fold_y/pallas_call | solution.py:438
  68.9 2.9 %collective-permute-start.2 = (bf16[256,640]{1,0:T(8,128)(2,1)}, bf16[256,640]{1,0:T(8,128)(2,1)S(1)}, u32[]{:S(2)}, u32[]{:S(2)}) collective-permute-start(bf16[256,640]{1,0:T(8,128)(2,1)} %get-tuple-element.49), channel_id=1, source_target_pairs={{0,4},{2,6},{4,0},{6,2},{1,5},{3,7},{5,1},{7,3},{8,12},{10,14},{12... | collective-permute-start | bytes 983048 | tf_op jit(solution)/shard_map/ppermute | solution.py:421
  72.2 2.3 %collective-permute-start.4 = (bf16[256,640]{1,0:T(8,128)(2,1)}, bf16[256,640]{1,0:T(8,128)(2,1)S(1)}, u32[]{:S(2)}, u32[]{:S(2)}) collective-permute-start(bf16[256,640]{1,0:T(8,128)(2,1)} %get-tuple-element.51), channel_id=1, source_target_pairs={{0,6},{2,0},{4,2},{6,4},{1,7},{3,1},{5,3},{7,5},{8,14},{10,8},{12,... | collective-permute-start | bytes 983048 | tf_op jit(solution)/shard_map/ppermute | solution.py:421
  74.5 13.1 %all-to-all-done.1.pieces = bf16[8,256,512]{2,1,0:T(8,128)(2,1)S(1)} async-done(((bf16[8,256,512]{2,1,0:T(8,128)(2,1)}), bf16[8,256,512]{2,1,0:T(8,128)(2,1)S(1)}, u32[]{:S(2)}, u32[]{:S(2)}) %all-to-all-start.1) | async-done | bytes 2097184 | tf_op jit(solution)/shard_map/all_to_all | solution.py:529
  87.6 1.3 copy-done
  89.0 3.9 %total.1 = bf16[8,256,512]{2,1,0:T(8,128)(2,1)} custom-call(bf16[8,256,512]{2,1,0:T(8,128)(2,1)} %copy-done), custom_call_target="tpu_custom_call" | custom-call | tf_op jit(solution)/shard_map/total/pallas_call | solution.py:514
  93.8 2.1 %fold_z.1 = (bf16[64,640]{1,0:T(8,128)(2,1)}, bf16[64,640]{1,0:T(8,128)(2,1)}, bf16[64,640]{1,0:T(8,128)(2,1)}, bf16[64,640]{1,0:T(8,128)(2,1)}) custom-call(bf16[256,640]{1,0:T(8,128)(2,1)} %get-tuple-element.53.refs_0_, bf16[256,640]{1,0:T(8,128)(2,1)} %copy-done.3, bf16[256,640]{1,0:T(8,128)(2,1)} %copy-done.4, bf16[256,640]{1,0:T(8,128)(2,1)} %copy-done.5), custom_call_target="tpu_custom_call" | custom-call | tf_op jit(solution)/shard_map/fold_z/pallas_call | solution.py:438
  97.4 2.0 %collective-permute-start.7 = (bf16[64,640]{1,0:T(8,128)(2,1)}, bf16[64,640]{1,0:T(8,128)(2,1)S(1)}, u32[]{:S(2)}, u32[]{:S(2)}) collective-permute-start(bf16[64,640]{1,0:T(8,128)(2,1)} %get-tuple-element.60), channel_id=1, source_target_pairs={{0,48},{16,0},{32,16},{48,32},{1,49},{17,1},{33,17},{49,33},{2,50}... | collective-permute-start | bytes 245768 | tf_op jit(solution)/shard_map/ppermute | solution.py:421
  99.4 1.5 collective-permute-done.5.refs_1_
  100.9 1.6 %collective-permute-done.6.refs_2_ = bf16[64,640]{1,0:T(8,128)(2,1)S(1)} collective-permute-done((bf16[64,640]{1,0:T(8,128)(2,1)}, bf16[64,640]{1,0:T(8,128)(2,1)S(1)}, u32[]{:S(2)}, u32[]{:S(2)}) %collective-permute-start.6) | collective-permute-done | bytes 81952 | tf_op jit(solution)/shard_map/ppermute | solution.py:421
  103.2 1.6 %fold_x.1 = (bf16[16,640]{1,0:T(8,128)(2,1)}, bf16[16,640]{1,0:T(8,128)(2,1)}, bf16[16,640]{1,0:T(8,128)(2,1)}, bf16[16,640]{1,0:T(8,128)(2,1)}) custom-call(bf16[64,640]{1,0:T(8,128)(2,1)} %get-tuple-element.57.refs_0_, bf16[64,640]{1,0:T(8,128)(2,1)} %copy-done.13, bf16[64,640]{1,0:T(8,128)(2,1)} %copy-done.14, bf16[64,640]{1,0:T(8,128)(2,1)} %copy-done.15), custom_call_target="tpu_custom_call" | custom-call | tf_op jit(solution)/shard_map/fold_x/pallas_call | solution.py:438
  104.8 1.8 %collective-permute-start.8 = (bf16[16,640]{1,0:T(8,128)(2,1)}, bf16[16,640]{1,0:T(8,128)(2,1)S(1)}, u32[]{:S(2)}, u32[]{:S(2)}) collective-permute-start(bf16[16,640]{1,0:T(8,128)(2,1)} %get-tuple-element.62), channel_id=1, source_target_pairs={{0,64},{8,72},{64,0},{72,8},{1,65},{9,73},{65,1},{73,9},{2,66},{10... | collective-permute-start | bytes 61448 | tf_op jit(solution)/shard_map/ppermute | solution.py:420
  106.7 2.5 %collective-permute-start.9 = (bf16[16,640]{1,0:T(8,128)(2,1)}, bf16[16,640]{1,0:T(8,128)(2,1)S(1)}, u32[]{:S(2)}, u32[]{:S(2)}) collective-permute-start(bf16[16,640]{1,0:T(8,128)(2,1)} %get-tuple-element.63), channel_id=1, source_target_pairs={{0,8},{8,0},{64,72},{72,64},{1,9},{9,1},{65,73},{73,65},{2,10},{10... | collective-permute-start | bytes 61448 | tf_op jit(solution)/shard_map/ppermute | solution.py:420
  109.1 3.6 %all-to-all-start.2 = ((bf16[8,256,512]{2,1,0:T(8,128)(2,1)}), bf16[8,256,512]{2,1,0:T(8,128)(2,1)S(1)}, u32[]{:S(2)}, u32[]{:S(2)}) async-start(bf16[8,256,512]{2,1,0:T(8,128)(2,1)} %total.1), calls=%async_computation.2 | async-start | bytes 4194304 | tf_op jit(solution)/shard_map/all_to_all | solution.py:529
  113.8 1.8 %finish.1.refs_0_ = bf16[16,640]{1,0:T(8,128)(2,1)} custom-call(bf16[16,640]{1,0:T(8,128)(2,1)} %get-tuple-element.61.a, bf16[16,640]{1,0:T(8,128)(2,1)} %copy-done.16, bf16[16,640]{1,0:T(8,128)(2,1)} %copy-done.17, bf16[16,640]{1,0:T(8,128)(2,1)} %copy-done.18, bf16[256,512]{1,0:T(8,128)(2,1)} %latent.3, f32[256,1]{1,0:T(8,128)} %get-tuple-element.65.inverse, ...), custom_call_target="tpu_custom_call" | custom-call | tf_op jit(solution)/shard_map/finish/pallas_call | solution.py:465
  115.6 4.6 %collective-permute-start.17 = (bf16[16,640]{1,0:T(8,128)(2,1)}, bf16[16,640]{1,0:T(8,128)(2,1)S(1)}, u32[]{:S(2)}, u32[]{:S(2)}) collective-permute-start(bf16[16,640]{1,0:T(8,128)(2,1)} %finish.1.refs_0_), channel_id=1, source_target_pairs={{0,14},{2,8},{4,10},{6,12},{8,6},{10,0},{12,2},{14,4},{1,15},{3,9}... | collective-permute-start | bytes 61448 | tf_op jit(solution)/shard_map/ppermute | solution.py:560
  121.0 2.6 %collective-permute-start.15 = (bf16[16,640]{1,0:T(8,128)(2,1)}, bf16[16,640]{1,0:T(8,128)(2,1)S(1)}, u32[]{:S(2)}, u32[]{:S(2)}) collective-permute-start(bf16[16,640]{1,0:T(8,128)(2,1)} %finish.1.refs_0_), channel_id=1, source_target_pairs={{0,10},{2,12},{4,14},{6,8},{8,2},{10,4},{12,6},{14,0},{1,11},{3,13... | collective-permute-start | bytes 61448 | tf_op jit(solution)/shard_map/ppermute | solution.py:560
  124.4 1.6 %collective-permute-start.11 = (bf16[16,640]{1,0:T(8,128)(2,1)}, bf16[16,640]{1,0:T(8,128)(2,1)S(1)}, u32[]{:S(2)}, u32[]{:S(2)}) collective-permute-start(bf16[16,640]{1,0:T(8,128)(2,1)} %finish.1.refs_0_), channel_id=1, source_target_pairs={{0,2},{2,4},{4,6},{6,0},{8,10},{10,12},{12,14},{14,8},{1,3},{3,5},... | collective-permute-start | bytes 61448 | tf_op jit(solution)/shard_map/ppermute | solution.py:560
  126.8 2.0 %collective-permute-done.11.refs_1_ = bf16[16,640]{1,0:T(8,128)(2,1)S(1)} collective-permute-done((bf16[16,640]{1,0:T(8,128)(2,1)}, bf16[16,640]{1,0:T(8,128)(2,1)S(1)}, u32[]{:S(2)}, u32[]{:S(2)}) %collective-permute-start.11) | collective-permute-done | bytes 20512 | tf_op jit(solution)/shard_map/ppermute | solution.py:560
  129.6 3.9 %collective-permute-done.12.refs_2_ = bf16[16,640]{1,0:T(8,128)(2,1)S(1)} collective-permute-done((bf16[16,640]{1,0:T(8,128)(2,1)}, bf16[16,640]{1,0:T(8,128)(2,1)S(1)}, u32[]{:S(2)}, u32[]{:S(2)}) %collective-permute-start.12) | collective-permute-done | bytes 20512 | tf_op jit(solution)/shard_map/ppermute | solution.py:560
  134.2 2.4 %collective-permute-done.13.refs_3_ = bf16[16,640]{1,0:T(8,128)(2,1)S(1)} collective-permute-done((bf16[16,640]{1,0:T(8,128)(2,1)}, bf16[16,640]{1,0:T(8,128)(2,1)S(1)}, u32[]{:S(2)}, u32[]{:S(2)}) %collective-permute-start.13) | collective-permute-done | bytes 20512 | tf_op jit(solution)/shard_map/ppermute | solution.py:560
  137.7 1.7 %collective-permute-done.15.refs_5_ = bf16[16,640]{1,0:T(8,128)(2,1)S(1)} collective-permute-done((bf16[16,640]{1,0:T(8,128)(2,1)}, bf16[16,640]{1,0:T(8,128)(2,1)S(1)}, u32[]{:S(2)}, u32[]{:S(2)}) %collective-permute-start.15) | collective-permute-done | bytes 20512 | tf_op jit(solution)/shard_map/ppermute | solution.py:560
  139.5 4.4 %collective-permute-start.18 = (bf16[8,16,640]{2,1,0:T(8,128)(2,1)S(1)}, bf16[8,16,640]{2,1,0:T(8,128)(2,1)S(1)}, u32[]{:S(2)}, u32[]{:S(2)}) collective-permute-start(bf16[8,16,640]{2,1,0:T(8,128)(2,1)S(1)} %bitcast_dynamic-update-slice_fusion), channel_id=1, source_target_pairs={{0,1},{1,0},{2,3},{3,2},{4,5},{5,4},{6,7},{7,6},{8,9},{9,8},{10,11... | collective-permute-start | bytes 491528 | tf_op jit(solution)/shard_map/ppermute | solution.py:525
  145.7 1.7 %assemble.1 = (bf16[256,512]{1,0:T(8,128)(2,1)}, bf16[64,256]{1,0:T(8,128)(2,1)}) custom-call(bf16[16,640]{1,0:T(8,128)(2,1)} %finish.1.refs_0_, bf16[16,640]{1,0:T(8,128)(2,1)} %copy-done.10, bf16[16,640]{1,0:T(8,128)(2,1)} %copy-done.11, bf16[16,640]{1,0:T(8,128)(2,1)} %copy-done.12, bf16[16,640]{1,0:T(8,128)(2,1)} %copy-done.9, ...), custom_call_target="tpu_custom_call" | custom-call | tf_op jit(solution)/shard_map/assemble/pallas_call | solution.py:489
  147.4 1.5 %fusion = (bf16[4,256,512]{2,1,0:T(8,128)(2,1)}, bf16[4,256,512]{2,1,0:T(8,128)(2,1)}) fusion(bf16[8,256,512]{2,1,0:T(8,128)(2,1)S(1)} %all-to-all-done.2), kind=kLoop, calls=%fused_computation.16 | loop fusion | bytes 4194304 | tf_op jit(solution)/shard_map/slice | solution.py:569
  (70 shorter events, 15.4 us)
Async XLA Ops:
  28.6 5.1 %copy-start.1 = (bf16[8,128,640]{2,1,0:T(8,128)(2,1)}, bf16[8,128,640]{2,1,0:T(8,128)(2,1)S(1)}, u32[]{:S(2)}) copy-start(bf16[8,128,640]{2,1,0:T(8,128)(2,1)S(1)} %all_to_all.15) | copy-start | bytes 3932164
  28.6 5.1 %collective-permute-start = (bf16[1024,640]{1,0:T(8,128)(2,1)S(1)}, bf16[1024,640]{1,0:T(8,128)(2,1)S(1)}, u32[]{:S(2)}, u32[]{:S(2)}) collective-permute-start(bf16[1024,640]{1,0:T(8,128)(2,1)S(1)} %bitcast.39), channel_id=1, source_target_pairs={{0,1},{1,0},{2,3},{3,2},{4,5},{5,4},{6,7},{7,6},{8,9},{9,8},{10,11... | collective-permute-start | bytes 3932168 | tf_op jit(solution)/shard_map/ppermute | solution.py:525
  33.7 1.1 copy-start.19
  51.6 36.0 %all-to-all-start.1 = ((bf16[8,256,512]{2,1,0:T(8,128)(2,1)}), bf16[8,256,512]{2,1,0:T(8,128)(2,1)S(1)}, u32[]{:S(2)}, u32[]{:S(2)}) async-start(bf16[8,256,512]{2,1,0:T(8,128)(2,1)} %bitcast.38), calls=%async_computation.1 | async-start | bytes 4194304 | tf_op jit(solution)/shard_map/all_to_all | solution.py:529
  61.5 3.5 %collective-permute-start.1 = (bf16[1024,640]{1,0:T(8,128)(2,1)}, bf16[1024,640]{1,0:T(8,128)(2,1)S(1)}, u32[]{:S(2)}, u32[]{:S(2)}) collective-permute-start(bf16[1024,640]{1,0:T(8,128)(2,1)} %get-tuple-element.47), channel_id=1, source_target_pairs={{0,1},{1,0},{2,3},{3,2},{4,5},{5,4},{6,7},{7,6},{8,9},{9,8},{10,11... | collective-permute-start | bytes 3932168 | tf_op jit(solution)/shard_map/ppermute | solution.py:525
  68.9 24.0 %collective-permute-start.2 = (bf16[256,640]{1,0:T(8,128)(2,1)}, bf16[256,640]{1,0:T(8,128)(2,1)S(1)}, u32[]{:S(2)}, u32[]{:S(2)}) collective-permute-start(bf16[256,640]{1,0:T(8,128)(2,1)} %get-tuple-element.49), channel_id=1, source_target_pairs={{0,4},{2,6},{4,0},{6,2},{1,5},{3,7},{5,1},{7,3},{8,12},{10,14},{12... | collective-permute-start | bytes 983048 | tf_op jit(solution)/shard_map/ppermute | solution.py:421
  71.8 21.1 %collective-permute-start.3 = (bf16[256,640]{1,0:T(8,128)(2,1)}, bf16[256,640]{1,0:T(8,128)(2,1)S(1)}, u32[]{:S(2)}, u32[]{:S(2)}) collective-permute-start(bf16[256,640]{1,0:T(8,128)(2,1)} %get-tuple-element.50), channel_id=1, source_target_pairs={{0,2},{2,4},{4,6},{6,0},{1,3},{3,5},{5,7},{7,1},{8,10},{10,12},{12... | collective-permute-start | bytes 983048 | tf_op jit(solution)/shard_map/ppermute | solution.py:421
  72.2 20.7 %collective-permute-start.4 = (bf16[256,640]{1,0:T(8,128)(2,1)}, bf16[256,640]{1,0:T(8,128)(2,1)S(1)}, u32[]{:S(2)}, u32[]{:S(2)}) collective-permute-start(bf16[256,640]{1,0:T(8,128)(2,1)} %get-tuple-element.51), channel_id=1, source_target_pairs={{0,6},{2,0},{4,2},{6,4},{1,7},{3,1},{5,3},{7,5},{8,14},{10,8},{12,... | collective-permute-start | bytes 983048 | tf_op jit(solution)/shard_map/ppermute | solution.py:421
  87.6 1.3 copy-start
  95.9 5.0 %collective-permute-start.5 = (bf16[64,640]{1,0:T(8,128)(2,1)}, bf16[64,640]{1,0:T(8,128)(2,1)S(1)}, u32[]{:S(2)}, u32[]{:S(2)}) collective-permute-start(bf16[64,640]{1,0:T(8,128)(2,1)} %get-tuple-element.58), channel_id=1, source_target_pairs={{0,32},{16,48},{32,0},{48,16},{1,33},{17,49},{33,1},{49,17},{2,34}... | collective-permute-start | bytes 245768 | tf_op jit(solution)/shard_map/ppermute | solution.py:421
  96.8 5.7 %collective-permute-start.6 = (bf16[64,640]{1,0:T(8,128)(2,1)}, bf16[64,640]{1,0:T(8,128)(2,1)S(1)}, u32[]{:S(2)}, u32[]{:S(2)}) collective-permute-start(bf16[64,640]{1,0:T(8,128)(2,1)} %get-tuple-element.59), channel_id=1, source_target_pairs={{0,16},{16,32},{32,48},{48,0},{1,17},{17,33},{33,49},{49,1},{2,18}... | collective-permute-start | bytes 245768 | tf_op jit(solution)/shard_map/ppermute | solution.py:421
  97.4 5.1 %collective-permute-start.7 = (bf16[64,640]{1,0:T(8,128)(2,1)}, bf16[64,640]{1,0:T(8,128)(2,1)S(1)}, u32[]{:S(2)}, u32[]{:S(2)}) collective-permute-start(bf16[64,640]{1,0:T(8,128)(2,1)} %get-tuple-element.60), channel_id=1, source_target_pairs={{0,48},{16,0},{32,16},{48,32},{1,49},{17,1},{33,17},{49,33},{2,50}... | collective-permute-start | bytes 245768 | tf_op jit(solution)/shard_map/ppermute | solution.py:421
  100.9 1.6 %copy-start.13 = (bf16[64,640]{1,0:T(8,128)(2,1)}, bf16[64,640]{1,0:T(8,128)(2,1)S(1)}, u32[]{:S(2)}) copy-start(bf16[64,640]{1,0:T(8,128)(2,1)S(1)} %collective-permute-done.5.refs_1_) | copy-start | bytes 245764
  104.8 7.9 %collective-permute-start.8 = (bf16[16,640]{1,0:T(8,128)(2,1)}, bf16[16,640]{1,0:T(8,128)(2,1)S(1)}, u32[]{:S(2)}, u32[]{:S(2)}) collective-permute-start(bf16[16,640]{1,0:T(8,128)(2,1)} %get-tuple-element.62), channel_id=1, source_target_pairs={{0,64},{8,72},{64,0},{72,8},{1,65},{9,73},{65,1},{73,9},{2,66},{10... | collective-permute-start | bytes 61448 | tf_op jit(solution)/shard_map/ppermute | solution.py:420
  106.7 6.1 %collective-permute-start.9 = (bf16[16,640]{1,0:T(8,128)(2,1)}, bf16[16,640]{1,0:T(8,128)(2,1)S(1)}, u32[]{:S(2)}, u32[]{:S(2)}) collective-permute-start(bf16[16,640]{1,0:T(8,128)(2,1)} %get-tuple-element.63), channel_id=1, source_target_pairs={{0,8},{8,0},{64,72},{72,64},{1,9},{9,1},{65,73},{73,65},{2,10},{10... | collective-permute-start | bytes 61448 | tf_op jit(solution)/shard_map/ppermute | solution.py:420
  109.1 4.1 %collective-permute-start.10 = (bf16[16,640]{1,0:T(8,128)(2,1)}, bf16[16,640]{1,0:T(8,128)(2,1)S(1)}, u32[]{:S(2)}, u32[]{:S(2)}) collective-permute-start(bf16[16,640]{1,0:T(8,128)(2,1)} %get-tuple-element.64), channel_id=1, source_target_pairs={{0,72},{8,64},{64,8},{72,0},{1,73},{9,65},{65,9},{73,1},{2,74},{10... | collective-permute-start | bytes 61448 | tf_op jit(solution)/shard_map/ppermute | solution.py:420
  109.1 38.3 %all-to-all-start.2 = ((bf16[8,256,512]{2,1,0:T(8,128)(2,1)}), bf16[8,256,512]{2,1,0:T(8,128)(2,1)S(1)}, u32[]{:S(2)}, u32[]{:S(2)}) async-start(bf16[8,256,512]{2,1,0:T(8,128)(2,1)} %total.1), calls=%async_computation.2 | async-start | bytes 4194304 | tf_op jit(solution)/shard_map/all_to_all | solution.py:529
  115.6 23.9 %collective-permute-start.17 = (bf16[16,640]{1,0:T(8,128)(2,1)}, bf16[16,640]{1,0:T(8,128)(2,1)S(1)}, u32[]{:S(2)}, u32[]{:S(2)}) collective-permute-start(bf16[16,640]{1,0:T(8,128)(2,1)} %finish.1.refs_0_), channel_id=1, source_target_pairs={{0,14},{2,8},{4,10},{6,12},{8,6},{10,0},{12,2},{14,4},{1,15},{3,9}... | collective-permute-start | bytes 61448 | tf_op jit(solution)/shard_map/ppermute | solution.py:560
  120.2 19.3 %collective-permute-start.16 = (bf16[16,640]{1,0:T(8,128)(2,1)}, bf16[16,640]{1,0:T(8,128)(2,1)S(1)}, u32[]{:S(2)}, u32[]{:S(2)}) collective-permute-start(bf16[16,640]{1,0:T(8,128)(2,1)} %finish.1.refs_0_), channel_id=1, source_target_pairs={{0,12},{2,14},{4,8},{6,10},{8,4},{10,6},{12,0},{14,2},{1,13},{3,15... | collective-permute-start | bytes 61448 | tf_op jit(solution)/shard_map/ppermute | solution.py:560
  121.0 18.4 %collective-permute-start.15 = (bf16[16,640]{1,0:T(8,128)(2,1)}, bf16[16,640]{1,0:T(8,128)(2,1)S(1)}, u32[]{:S(2)}, u32[]{:S(2)}) collective-permute-start(bf16[16,640]{1,0:T(8,128)(2,1)} %finish.1.refs_0_), channel_id=1, source_target_pairs={{0,10},{2,12},{4,14},{6,8},{8,2},{10,4},{12,6},{14,0},{1,11},{3,13... | collective-permute-start | bytes 61448 | tf_op jit(solution)/shard_map/ppermute | solution.py:560
  123.6 14.1 %collective-permute-start.14 = (bf16[16,640]{1,0:T(8,128)(2,1)}, bf16[16,640]{1,0:T(8,128)(2,1)S(1)}, u32[]{:S(2)}, u32[]{:S(2)}) collective-permute-start(bf16[16,640]{1,0:T(8,128)(2,1)} %finish.1.refs_0_), channel_id=1, source_target_pairs={{0,8},{2,10},{4,12},{6,14},{8,0},{10,2},{12,4},{14,6},{1,9},{3,11}... | collective-permute-start | bytes 61448 | tf_op jit(solution)/shard_map/ppermute | solution.py:560
  124.4 4.3 %collective-permute-start.11 = (bf16[16,640]{1,0:T(8,128)(2,1)}, bf16[16,640]{1,0:T(8,128)(2,1)S(1)}, u32[]{:S(2)}, u32[]{:S(2)}) collective-permute-start(bf16[16,640]{1,0:T(8,128)(2,1)} %finish.1.refs_0_), channel_id=1, source_target_pairs={{0,2},{2,4},{4,6},{6,0},{8,10},{10,12},{12,14},{14,8},{1,3},{3,5},... | collective-permute-start | bytes 61448 | tf_op jit(solution)/shard_map/ppermute | solution.py:560
  128.8 16.9 %copy-start.10 = (bf16[16,640]{1,0:T(8,128)(2,1)}, bf16[16,640]{1,0:T(8,128)(2,1)S(1)}, u32[]{:S(2)}) copy-start(bf16[16,640]{1,0:T(8,128)(2,1)S(1)} %collective-permute-done.11.refs_1_) | copy-start | bytes 61444
  128.8 4.7 %collective-permute-start.12 = (bf16[16,640]{1,0:T(8,128)(2,1)}, bf16[16,640]{1,0:T(8,128)(2,1)S(1)}, u32[]{:S(2)}, u32[]{:S(2)}) collective-permute-start(bf16[16,640]{1,0:T(8,128)(2,1)} %finish.1.refs_0_), channel_id=1, source_target_pairs={{0,4},{2,6},{4,0},{6,2},{8,12},{10,14},{12,8},{14,10},{1,5},{3,7},... | collective-permute-start | bytes 61448 | tf_op jit(solution)/shard_map/ppermute | solution.py:560
  133.5 12.2 %copy-start.11 = (bf16[16,640]{1,0:T(8,128)(2,1)}, bf16[16,640]{1,0:T(8,128)(2,1)S(1)}, u32[]{:S(2)}) copy-start(bf16[16,640]{1,0:T(8,128)(2,1)S(1)} %collective-permute-done.12.refs_2_) | copy-start | bytes 61444
  133.5 3.1 %collective-permute-start.13 = (bf16[16,640]{1,0:T(8,128)(2,1)}, bf16[16,640]{1,0:T(8,128)(2,1)S(1)}, u32[]{:S(2)}, u32[]{:S(2)}) collective-permute-start(bf16[16,640]{1,0:T(8,128)(2,1)} %finish.1.refs_0_), channel_id=1, source_target_pairs={{0,6},{2,0},{4,2},{6,4},{8,14},{10,8},{12,10},{14,12},{1,7},{3,1},... | collective-permute-start | bytes 61448 | tf_op jit(solution)/shard_map/ppermute | solution.py:560
  136.6 9.1 %copy-start.12 = (bf16[16,640]{1,0:T(8,128)(2,1)}, bf16[16,640]{1,0:T(8,128)(2,1)S(1)}, u32[]{:S(2)}) copy-start(bf16[16,640]{1,0:T(8,128)(2,1)S(1)} %collective-permute-done.13.refs_3_) | copy-start | bytes 61444
  137.7 8.0 %copy-start.9 = (bf16[16,640]{1,0:T(8,128)(2,1)}, bf16[16,640]{1,0:T(8,128)(2,1)S(1)}, u32[]{:S(2)}) copy-start(bf16[16,640]{1,0:T(8,128)(2,1)S(1)} %collective-permute-done.14.refs_4_) | copy-start | bytes 61444
  139.4 6.3 %copy-start.8 = (bf16[16,640]{1,0:T(8,128)(2,1)}, bf16[16,640]{1,0:T(8,128)(2,1)S(1)}, u32[]{:S(2)}) copy-start(bf16[16,640]{1,0:T(8,128)(2,1)S(1)} %collective-permute-done.15.refs_5_) | copy-start | bytes 61444
  139.5 6.2 %copy-start.7 = (bf16[16,640]{1,0:T(8,128)(2,1)}, bf16[16,640]{1,0:T(8,128)(2,1)S(1)}, u32[]{:S(2)}) copy-start(bf16[16,640]{1,0:T(8,128)(2,1)S(1)} %collective-permute-done.16.refs_6_) | copy-start | bytes 61444
  139.5 6.2 %copy-start.6 = (bf16[16,640]{1,0:T(8,128)(2,1)}, bf16[16,640]{1,0:T(8,128)(2,1)S(1)}, u32[]{:S(2)}) copy-start(bf16[16,640]{1,0:T(8,128)(2,1)S(1)} %collective-permute-done.17.refs_7_) | copy-start | bytes 61444
  139.5 5.5 %collective-permute-start.18 = (bf16[8,16,640]{2,1,0:T(8,128)(2,1)S(1)}, bf16[8,16,640]{2,1,0:T(8,128)(2,1)S(1)}, u32[]{:S(2)}, u32[]{:S(2)}) collective-permute-start(bf16[8,16,640]{2,1,0:T(8,128)(2,1)S(1)} %bitcast_dynamic-update-slice_fusion), channel_id=1, source_target_pairs={{0,1},{1,0},{2,3},{3,2},{4,5},{5,4},{6,7},{7,6},{8,9},{9,8},{10,11... | collective-permute-start | bytes 491528 | tf_op jit(solution)/shard_map/ppermute | solution.py:525
  (9 other events, 6.6 us)

commit v2 on v1

--- a/solution.py
+++ b/solution.py
@@ -22,7 +22,9 @@
 BLOCK = 16
 TILE = 256
 MAX_TILES = 6
-WIDE = (3,)
+SLOTS = 12
+WIDE = (3, 4)
+SMALL = pl.CostEstimate(flops=1, bytes_accessed=1, transcendentals=0)
 PACK = 640
 EXTRA = PACK - D_LAT
 PAD_COL = PACK - 1
@@ -45,8 +47,8 @@
 
 def attention_kernel(*refs):
     info, own, mine, other, bias, weight, qn, qr, do, wk, wv = refs[:11]
-    out, dqn, dqr, dw, kept, sent = refs[11:17]
-    keys, acc, kf, vv, s, dp, e, qf, qt, gb, git, wb, wt, wgrad, meta = refs[17:]
+    out, dqn, dqr, dw, kept, sent, meta = refs[11:18]
+    keys, acc, kf, vv, s, dp, e, qf, qt, gb, git, wb, wt, wgrad = refs[18:]
     step = pl.program_id(0)
 
     def key_rows(t):
@@ -72,6 +74,7 @@
         count = jnp.minimum(count, (MAX_TILES - 1) * (TILE // BLOCK))
         tiles = 1 + (count + TILE // BLOCK - 1) // (TILE // BLOCK)
         meta[0], meta[1], meta[2], meta[3], meta[4] = tiles, n1, block1, block2, count
+        meta[5] = chunk
         keys[0:ROWS, :] = own[...]
 
         def copy_block(index, carry):
@@ -119,11 +122,14 @@
 
     base2 = SCALING * math.log2(math.e)
 
+    def add_grads(cols, lat_grads, rope_grads):
+        acc[:D_LAT, cols] += lat_grads
+        acc[D_LAT:, cols] += rope_grads
+
     def finish_heads(dq, grad):
         for h in range(2):
             dqn[:, h * D_NOPE : (h + 1) * D_NOPE] = dq[h][:, :D_NOPE].astype(BF)
-            dw[0, h * D_NOPE : (h + 1) * D_NOPE] = grad[h * 256 : h * 256 + 128].astype(BF)
-            dw[1, h * D_V : (h + 1) * D_V] = grad[h * 256 + 128 : (h + 1) * 256].astype(BF)
+            dw[h] = grad[h * 256 : (h + 1) * 256].astype(BF)
         dqr[...] = jnp.concatenate(
             [dq[h][:, D_NOPE : D_NOPE + D_ROPE] for h in range(2)], axis=1
         ).astype(BF)
@@ -163,8 +169,7 @@
             parts += [dk[:D_NOPE].astype(BF), dv.astype(BF)]
             rope_sum = dk[D_NOPE:] if h == 0 else rope_sum + dk[D_NOPE:]
         dkv = jnp.concatenate(parts, axis=0)
-        acc[:D_LAT, :width] += dot(wt[...], dkv)
-        acc[D_LAT:, :width] += rope_sum
+        add_grads(slice(0, width), dot(wt[...], dkv), rope_sum)
         finish_heads(dq, dot(dkv, all_keys[:, :D_LAT]))
 
     def loop_step():
@@ -231,8 +236,7 @@
                 parts += [dk[:D_NOPE].astype(BF), dv.astype(BF)]
                 rope_sum = dk[D_NOPE:] if h == 0 else rope_sum + dk[D_NOPE:]
             dkv = jnp.concatenate(parts, axis=0)
-            acc[:D_LAT, key_rows(t)] += dot(wt[...], dkv)
-            acc[D_LAT:, key_rows(t)] += rope_sum
+            add_grads(key_rows(t), dot(wt[...], dkv), rope_sum)
             wgrad[...] += dot(dkv, tile_keys)
             return tuple(new)
 
@@ -266,26 +270,26 @@
 
         lax.fori_loop(0, tiles, turn, 0)
 
-        def place(index, carry):
-            past = index - ROWS // BLOCK
-            block = jnp.where(past < n1, block1 + past, block2 + past - n1)
-            block = jnp.where(past < 0, chunk * (ROWS // BLOCK) + index, block)
-            pair = block // 2
-            where = (pair % 4) * 16 + ((pair // 8) % 4) * 4 + (pair // 32) * 2 + (pair // 4) % 2
-            rows = pl.ds(pl.multiple_of(where * BLOCK, BLOCK), BLOCK)
-            values = keys[pl.ds(pl.multiple_of(index * BLOCK, BLOCK), BLOCK), :]
-
-            @pl.when((block + core) % 2 == 0)
-            def _():
-                kept[rows, :] = values
-
-            @pl.when((block + core) % 2 == 1)
-            def _():
-                sent[rows, :] = values
-
-            return carry
-
-        lax.fori_loop(0, ROWS // BLOCK + count, place, 0)
+        def put(target, slot, y, index):
+            target[slot, y] = keys[pl.ds(pl.multiple_of(index * BLOCK, BLOCK), BLOCK), :]
+
+        own_blocks = ROWS // BLOCK
+        for y in range(4):
+            for target, parity in ((kept, core), (sent, 1 - core)):
+                kind = 2 * y + parity
+                for i in range(2):
+                    put(target, i, y, 8 * i + kind)
+                slot = 2
+                for start, shift, length in ((block1, 0, n1), (block2, n1, count - n1)):
+                    skip = (kind - start) & 7
+                    number = jnp.maximum(length - skip + 7, 0) // 8
+
+                    def put_next(i, carry, target=target, y=y, slot=slot, skip=skip, shift=shift):
+                        put(target, slot + i, y, own_blocks + shift + skip + 8 * i)
+                        return carry
+
+                    lax.fori_loop(0, number, put_next, 0)
+                    slot = slot + number
 
 
 def attention(shared, q_nope, q_rope, d_out, w_uk, w_uv):
@@ -301,7 +305,7 @@
     whole = pl.BlockSpec(memory_space=pltpu.VMEM)
     in_specs = [pl.BlockSpec(memory_space=pltpu.SMEM)] + [whole] * 5
     in_specs += [columns(256), columns(128), columns(256), heads(256), heads(256)]
-    half = jax.ShapeDtypeStruct((TOKENS // 2, PACK), BF)
+    half = jax.ShapeDtypeStruct((SLOTS, 4, BLOCK, PACK), BF)
     return pl.pallas_call(
         attention_kernel,
         grid=(pairs,),
@@ -310,17 +314,19 @@
             columns(256),
             columns(256),
             columns(128),
-            pl.BlockSpec((2, 256, D_LAT), lambda i: (0, i, 0)),
+            pl.BlockSpec((2, 256, D_LAT), lambda i: (i, 0, 0)),
             whole,
             whole,
+            pl.BlockSpec(memory_space=pltpu.SMEM),
         ],
         out_shape=[
             jax.ShapeDtypeStruct(q_nope.shape, BF),
             jax.ShapeDtypeStruct(q_nope.shape, BF),
             jax.ShapeDtypeStruct(q_rope.shape, BF),
-            jax.ShapeDtypeStruct((2, pairs * 256, D_LAT), BF),
+            jax.ShapeDtypeStruct((2 * pairs, 256, D_LAT), BF),
             half,
             half,
+            jax.ShapeDtypeStruct((8,), jnp.int32),
         ],
         scratch_shapes=[
             pltpu.VMEM((MAX_TILES * TILE, PACK), BF),
@@ -337,7 +343,6 @@
             pltpu.VMEM((512, D_LAT), BF),
             pltpu.VMEM((D_LAT, 512), BF),
             pltpu.VMEM((512, D_LAT), F32),
-            pltpu.SMEM((8,), jnp.int32),
         ],
         compiler_params=pltpu.CompilerParams(vmem_limit_bytes=56 << 20),
         cost_estimate=pl.CostEstimate(
@@ -353,7 +358,7 @@
     latent_f = latent[...].astype(F32)
     inv = lax.rsqrt(jnp.mean(latent_f * latent_f, axis=1, keepdims=True) + 1e-06)
     inverse[...] = inv
-    normed = (latent_f * inv * gain[...].astype(F32)).astype(BF)
+    normed = (latent_f * inv * gain[...].astype(F32)[None, :]).astype(BF)
     group = jnp.broadcast_to(gid[...].astype(F32), (8, ROWS)).T[:, :1].astype(jnp.int32)
     comp = jnp.broadcast_to(cid[...].astype(F32), (8, ROWS)).T[:, :1].astype(jnp.int32)
     code = group * (COMP + 1) + comp
@@ -395,10 +400,11 @@
             jax.ShapeDtypeStruct((ROWS, 1), F32),
             jax.ShapeDtypeStruct((8,), jnp.int32),
         ],
+        cost_estimate=SMALL,
         name="prepare",
     )(
         latent,
-        latent_gain[None, :],
+        latent_gain,
         k_rope_t,
         group_ids[None, :],
         comp_ids[None, :],
@@ -408,12 +414,6 @@
     )
 
 
-def relative(axis, distance):
-    if axis == "x":
-        return (lax.axis_index("xl") * 2 + lax.axis_index("xh")) ^ distance
-    return (lax.axis_index(axis) + distance) & 3
-
-
 def move(x, axis, distance):
     if axis == "x":
         names = ("xl", "xh")
@@ -421,40 +421,92 @@
     return lax.ppermute(x, axis, [(i, (i + distance) % 4) for i in range(4)])
 
 
-def fold_kernel(axis, count, *refs):
-    parts, outs = refs[:count], refs[count:]
-    size = outs[0].shape[0]
-    for distance in range(4):
-        start = pl.multiple_of(relative(axis, distance) * size, BLOCK)
-        total = parts[0][pl.ds(start, size), :].astype(F32)
-        for part in parts[1:]:
-            total = total + part[pl.ds(start, size), :].astype(F32)
-        outs[distance][...] = total.astype(BF)
-
-
-def fold(axis, parts):
+def summed(parts, index):
+    total = parts[0][index].astype(F32)
+    for part in parts[1:]:
+        total = total + part[index].astype(F32)
+    return total.astype(BF)
+
+
+def fold_y_kernel(*refs):
+    parts, outs = refs[:2], refs[2:]
+    slots = outs[0].shape[0]
+    for distance, out in enumerate(outs):
+        place = (lax.axis_index("y") + distance) & 3
+        for slot in range(slots):
+            out[slot] = summed(parts, (slot, place))
+
+
+def fold_z_kernel(*refs):
+    meta, parts, outs = refs[0], refs[1:5], refs[5:9]
+    n1, block1, block2, count, chunk = meta[1], meta[2], meta[3], meta[4], meta[5]
+    kind = 2 * lax.axis_index("y") + lax.axis_index("core")
+    z = lax.axis_index("z")
+    spread = refs[9]
+    spread[...] = jnp.zeros(spread.shape, BF)
+
+    def put(slot, block):
+        pair = block // 8
+        spread[(((pair // 2) % 4) - z) & 3, (pair // 8) * 2 + pair % 2] = summed(parts, (slot,))
+
+    for i in range(2):
+        put(i, chunk * (ROWS // BLOCK) + 8 * i + kind)
+    slot = 2
+    for start, length in ((block1, n1), (block2, count - n1)):
+        skip = (kind - start) & 7
+        number = jnp.maximum(length - skip + 7, 0) // 8
+
+        def put_next(i, carry, slot=slot, first=start + skip):
+            put(slot + i, first + 8 * i)
+            return carry
+
+        lax.fori_loop(0, number, put_next, 0)
+        slot = slot + number
+    for distance, out in enumerate(outs):
+        out[...] = spread[distance]
+
+
+def fold_x_kernel(*refs):
+    parts, outs = refs[:4], refs[4:]
+    for distance, out in enumerate(outs):
+        place = lax.axis_index("xl") ^ distance
+        for xh in range(2):
+            out[xh] = summed(parts, (place * 2 + xh,))
+
+
+def fold(kernel, operands, cuts, shape, scratch=()):
     vector = pl.BlockSpec(memory_space=LOCAL)
-    shape = jax.ShapeDtypeStruct((parts[0].shape[0] // 4, PACK), BF)
+    scalar = pl.BlockSpec(memory_space=pltpu.SMEM)
     return pl.pallas_call(
-        functools.partial(fold_kernel, axis, len(parts)),
-        in_specs=[vector] * len(parts),
-        out_specs=[vector] * 4,
-        out_shape=[shape] * 4,
-        name="fold_" + axis,
-    )(*parts)
-
-
-def scatter(axis, parts):
-    cut = fold(axis, parts)
-    return [cut[0]] + [move(cut[d], axis, d) for d in (2, 1, 3)]
+        kernel,
+        in_specs=[scalar if x.dtype == jnp.int32 else vector for x in operands],
+        out_specs=[vector] * cuts,
+        out_shape=[jax.ShapeDtypeStruct(shape, BF)] * cuts,
+        scratch_shapes=scratch,
+        cost_estimate=SMALL,
+        name="fold",
+    )(*operands)
+
+
+def gather_grads(kept, sent, meta):
+    slots = sent.shape[0]
+    cut = fold(fold_y_kernel, [kept, swap_core(sent)], 4, (slots, BLOCK, PACK))
+    parts = [cut[0]] + [move(cut[d], "y", d) for d in (2, 1, 3)]
+    spread = pltpu.VMEM((4, 4, BLOCK, PACK), BF)
+    cut = fold(fold_z_kernel, [meta] + parts, 4, (4, BLOCK, PACK), [spread])
+    parts = [cut[0]] + [move(cut[d], "z", d) for d in (2, 1, 3)]
+    cut = fold(fold_x_kernel, parts, 2, (2, BLOCK, PACK))
+    return [cut[0], move(cut[0], "x", 1), move(cut[1], "x", 2), move(cut[1], "x", 3)]
 
 
 def finish_kernel(a, b, c, d, latent, inverse, gain, out):
-    head = lax.axis_index("xh") * 8 + lax.axis_index("y") * 2 + lax.axis_index("core")
-    rows = pl.ds(pl.multiple_of(head * BLOCK, BLOCK), BLOCK)
-    total = a[...].astype(F32) + b[...].astype(F32) + c[...].astype(F32) + d[...].astype(F32)
-    lifted = total[:, :D_LAT] * gain[...].astype(F32)
-    own, inv = latent[rows, :].astype(F32), inverse[rows, :]
+    head = lax.axis_index("y") * 2 + lax.axis_index("core")
+    total = sum([part[...].astype(F32) for part in (b, c, d)], a[...].astype(F32))
+    total = total.reshape(2 * BLOCK, PACK)
+    lifted = total[:, :D_LAT] * gain[...].astype(F32)[None, :]
+    places = [pl.ds(pl.multiple_of((xh * 8 + head) * BLOCK, BLOCK), BLOCK) for xh in range(2)]
+    own = jnp.concatenate([latent[rows, :] for rows in places], axis=0).astype(F32)
+    inv = jnp.concatenate([inverse[rows, :] for rows in places], axis=0)
     centred = jnp.mean(lifted * own, axis=1, keepdims=True)
     out[:, :D_LAT] = (inv * lifted - own * inv**3 * centred).astype(BF)
     out[:, D_LAT:] = total[:, D_LAT:].astype(BF)
@@ -466,57 +518,85 @@
         finish_kernel,
         in_specs=[vector] * 7,
         out_specs=vector,
-        out_shape=jax.ShapeDtypeStruct((BLOCK, PACK), BF),
+        out_shape=jax.ShapeDtypeStruct((2 * BLOCK, PACK), BF),
+        cost_estimate=SMALL,
         name="finish",
-    )(*parts, latent, inverse, latent_gain[None, :])
+    )(*parts, latent, inverse, latent_gain)
 
 
 def assemble_kernel(*refs):
-    pieces, out, rope = refs[:16], refs[16], refs[17]
-    xh, y, core = lax.axis_index("xh"), lax.axis_index("y"), lax.axis_index("core")
-    everything = []
-    for index, piece in enumerate(pieces):
-        other, place = index // 8, index % 8
-        head = (xh ^ (place // 4)) * 8 + ((y - place % 4) & 3) * 2 + (core ^ other)
-        rows = pl.ds(pl.multiple_of(head * BLOCK, BLOCK), BLOCK)
-        out[rows, :] = piece[:, :D_LAT]
-        refs[18][rows, :] = piece[:, D_LAT:].astype(F32)
-    rope[...] = refs[18][...].T[:D_ROPE].astype(BF)
+    pieces, out, rope, turned = refs[:4], refs[4], refs[5], refs[6]
+    y, core = lax.axis_index("y"), lax.axis_index("core")
+    for distance, piece in enumerate(pieces):
+        for other in range(2):
+            for xh in range(2):
+                head = xh * 8 + ((y - distance) & 3) * 2 + (core ^ other)
+                rows = pl.ds(pl.multiple_of(head * BLOCK, BLOCK), BLOCK)
+                place = (other * 2 + xh) * BLOCK
+                out[rows, :] = piece[place : place + BLOCK, :D_LAT]
+                turned[rows, :] = piece[place : place + BLOCK, D_LAT:].astype(F32)
+    rope[...] = turned[...].T[:D_ROPE].astype(BF)
 
 
 def assemble(pieces):
     vector = pl.BlockSpec(memory_space=LOCAL)
     return pl.pallas_call(
         assemble_kernel,
-        in_specs=[vector] * 16,
+        in_specs=[vector] * 4,
         out_specs=[vector] * 2,
         out_shape=[
             jax.ShapeDtypeStruct((ROWS, D_LAT), BF),
             jax.ShapeDtypeStruct((D_ROPE, ROWS), BF),
         ],
         scratch_shapes=[pltpu.VMEM((ROWS, EXTRA), F32)],
+        cost_estimate=SMALL,
         name="assemble",
     )(*pieces)
 
 
-def total_kernel(pieces, out):
-    total = pieces[0].astype(F32)
-    for i in range(1, CTX):
-        total = total + pieces[i].astype(F32)
-    total = total.astype(BF)
-    for i in range(CTX):
-        out[i] = total
+def total_kernel(pieces, out, parts, sums, in_sems, out_sems):
+    steps = in_sems.shape[0]
+    size = sums.shape[0] // steps
+
+    def load(step):
+        rows = pl.ds(step * size, size)
+        return pltpu.make_async_copy(pieces.at[:, rows, :], parts.at[:, rows, :], in_sems.at[step])
+
+    def store(step, i):
+        rows = pl.ds(step * size, size)
+        return pltpu.make_async_copy(sums.at[rows, :], out.at[i, rows, :], out_sems.at[step, i])
+
+    for step in range(steps):
+        load(step).start()
+    for step in range(steps):
+        load(step).wait()
+        rows = pl.ds(step * size, size)
+        total = parts[0, rows, :].astype(F32)
+        for i in range(1, CTX):
+            total = total + parts[i, rows, :].astype(F32)
+        sums[rows, :] = total.astype(BF)
+        for i in range(CTX):
+            store(step, i).start()
+    for step in range(steps):
+        for i in range(CTX):
+            store(step, i).wait()
 
 
 def total_and_copy(pieces):
-    count, rows, width = pieces.shape
-    spec = pl.BlockSpec((count, rows // 4, width), lambda i: (0, i, 0))
+    anywhere = pl.BlockSpec(memory_space=pl.ANY)
     return pl.pallas_call(
         total_kernel,
-        grid=(4,),
-        in_specs=[spec],
-        out_specs=spec,
+        in_specs=[anywhere],
+        out_specs=anywhere,
         out_shape=jax.ShapeDtypeStruct(pieces.shape, BF),
+        scratch_shapes=[
+            pltpu.VMEM(pieces.shape, BF),
+            pltpu.VMEM(pieces.shape[1:], BF),
+            pltpu.SemaphoreType.DMA((4,)),
+            pltpu.SemaphoreType.DMA((4, CTX)),
+        ],
+        compiler_params=pltpu.CompilerParams(vmem_limit_bytes=56 << 20),
+        cost_estimate=SMALL,
         name="total",
     )(pieces)
 
@@ -548,25 +628,18 @@
     mine = exchange(send, CTX_AXES).reshape(-1, PACK)
     other = swap_core(mine)
     shared = (info, own, mine, other, bias, weight)
-    out, dqn, dqr, dw, kept, sent = attention(shared, q_nope, q_rope, d_out, w_uk, w_uv)
-    pieces = exchange(dw.reshape(CTX, -1, D_LAT), CTX_AXES)
+    out, dqn, dqr, dw, kept, sent, meta = attention(shared, q_nope, q_rope, d_out, w_uk, w_uv)
+    pieces = exchange(dw, CTX_AXES)
     total = total_and_copy(pieces)
-    parts = scatter("y", [kept, swap_core(sent)])
+    parts = gather_grads(kept, sent, meta)
     parts, total = lax.optimization_barrier((parts, total))
-    weights = exchange(total, CTX_AXES).reshape(2, -1, D_LAT)
-    parts = scatter("x", scatter("z", parts))
+    weights = exchange(total, CTX_AXES)
     final = finish(parts, latent, inverse, latent_gain)
-    pieces = [final] + [
-        lax.ppermute(
-            final,
-            ("xh", "y"),
-            [(i, ((i // 4) ^ (d // 4)) * 4 + (i + d) % 4) for i in range(8)],
-        )
-        for d in range(1, 8)
+    pair = jnp.concatenate([final, swap_core(final)], axis=0)
+    d_latent, d_k_rope_t = assemble([pair] + [move(pair, "y", d) for d in (1, 2, 3)])
+    return out, dqn, dqr, d_latent, d_k_rope_t, *[
+        weights[:, i * D_NOPE : (i + 1) * D_NOPE].reshape(-1, D_LAT) for i in range(2)
     ]
-    swapped = swap_core(jnp.stack(pieces))
-    d_latent, d_k_rope_t = assemble(pieces + [swapped[i] for i in range(8)])
-    return out, dqn, dqr, d_latent, d_k_rope_t, weights[0], weights[1]
 
 
 def solution(mesh):

time: 149 us -> 135 us (0.906); the launches traced: 149 us -> 133 us
  starting transfers between devices: 46.4 us -> 39 us
  waiting for transfers between devices: 34.3 us -> 29.9 us
  local copies, waits for them, and re-layouts: 9.97 us -> 6.92 us
  Pallas kernels: 33.6 us -> 31.6 us
    ppermute x6 -> x9, waiting for transfers between devices: 3.07 us -> 17.8 us  [move(): return lax.ppermute(x, axis, [(i, (i + distance) % 4) for i in range(4)])]
    ppermute x7 -> x0, starting transfers between devices: 12 us -> none  [on_device(): lax.ppermute(final, ('xh', 'y'), [(i, (i // 4 ^ d // 4) * 4 + (i + d) % 4...]
    ppermute x7 -> x0, waiting for transfers between devices: 11.1 us -> none  [on_device(): lax.ppermute(final, ('xh', 'y'), [(i, (i // 4 ^ d // 4) * 4 + (i + d) % 4...]
    all_to_all x2, waiting for transfers between devices: 13.1 us -> 5.98 us  [exchange(): return lax.all_to_all(x, axes, 0, 0, tiled=True)]
    ppermute x6 -> x9, starting transfers between devices: 9.15 us -> 14.7 us  [move(): return lax.ppermute(x, axis, [(i, (i + distance) % 4) for i in range(4)])]
    unnamed x47 -> x34, local copies, waits for them, and re-layouts: 6.5 us -> 5.4 us
  transfers between devices with their start and end apart: 21 -> 17, of which waited for: 12 -> 10; matrix products, arithmetic and copies ran while one was open for 1% -> 1% of each run, Pallas kernels for 7% -> 10%
where the time goes in v2:
time: 135 us; the launch traced here: 133 us
  starting transfers between devices  39 us (29%)
  Pallas kernels  31.6 us (23%)
  waiting for transfers between devices  29.9 us (22%)
  blocking collectives  23.9 us (18%)
  local copies, waits for them, and re-layouts  6.92 us (5%)
    all_to_all x1, blocking collectives, exchange(): return lax.all_to_all(x, axes, 0, 0, tiled=True)  23.9 us
    ppermute x9, waiting for transfers between devices, move(): return lax.ppermute(x, axis, [(i, (i + distance) % 4) for i in range(4)])  17.8 us
    pallas_call x1, Pallas kernels, attention(): pl.pallas_call(attention_kernel, grid=(pairs,), in_specs=in_specs, out_sp...  16 us
    ppermute x9, starting transfers between devices, move(): return lax.ppermute(x, axis, [(i, (i + distance) % 4) for i in range(4)])  14.7 us
    all_to_all x2, starting transfers between devices, exchange(): return lax.all_to_all(x, axes, 0, 0, tiled=True)  13.9 us
    ppermute x3, starting transfers between devices, swap_core(): return lax.ppermute(x, 'core', [(0, 1), (1, 0)])  6.68 us
    pallas_call x3, Pallas kernels, fold(): pl.pallas_call(kernel, in_specs=[scalar if x.dtype == jnp.int32 else vect...  6.31 us
    ppermute x3, waiting for transfers between devices, swap_core(): return lax.ppermute(x, 'core', [(0, 1), (1, 0)])  6.15 us
  transfers between devices with their start and end apart: 17, of which 10 were waited for; matrix products, arithmetic and copies ran while one was open for 1% of the time, Pallas kernels for 10%

profile of v2, /device:TPU:1, one launch (start us, length us, event | category | flops | bytes accessed | tf_op | source)
XLA Modules:
  0.0 132.9 jit_solution(6545279060289699581)
XLA Ops:
  0.6 2.8 %prepare.1 = (bf16[256,640]{1,0:T(8,128)(2,1)}, bf16[8,128,640]{2,1,0:T(8,128)(2,1)}, bf16[256,64]{1,0:T(8,128)(2,1)}, f32[256,1]{1,0:T(8,128)}, f32[256,1]{1,0:T(8,128)}, /*index=5*/s32[8]{0:T(128)}) custom-call(bf16[256,512]{1,0:T(8,128)(2,1)} %latent.3, bf16[512]{0:T(512)(128)(2,1)} %gain.3, bf16[64,256]{1,0:T(8,128)(2,1)} %rope_t.1, s32[1,256]{1,0:T(1,128)} %bitcast.9, ...), custom_call_target="tpu_custom_call" | custom-call | flops 1 | bytes 1 | tf_op jit(solution)/shard_map/prepare/pallas_call | solution.py:391
  3.5 23.9 %all_to_all.15 = bf16[8,128,640]{2,1,0:T(8,128)(2,1)S(1)} all-to-all(bf16[8,128,640]{2,1,0:T(8,128)(2,1)} %get-tuple-element.39), channel_id=1, replica_groups=mesh['xl'=2,'z'=4,'xh'=2,'y'=4,'core'=2] {'xl','z'}, dimensions={0} | all-to-all | bytes 2621440 | tf_op jit(solution)/shard_map/all_to_all | solution.py:609
  27.4 2.5 %collective-permute-start = (bf16[1024,640]{1,0:T(8,128)(2,1)S(1)}, bf16[1024,640]{1,0:T(8,128)(2,1)S(1)}, u32[]{:S(2)}, u32[]{:S(2)}) collective-permute-start(bf16[1024,640]{1,0:T(8,128)(2,1)S(1)} %bitcast.5), channel_id=1, source_target_pairs={{0,1},{1,0},{2,3},{3,2},{4,5},{5,4},{6,7},{7,6},{8,9},{9,8},{10,11... | collective-permute-start | bytes 3932168 | tf_op jit(solution)/shard_map/ppermute | solution.py:605
  29.8 2.7 %collective-permute-done.refs_3_ = bf16[1024,640]{1,0:T(8,128)(2,1)S(1)} collective-permute-done((bf16[1024,640]{1,0:T(8,128)(2,1)S(1)}, bf16[1024,640]{1,0:T(8,128)(2,1)S(1)}, u32[]{:S(2)}, u32[]{:S(2)}) %collective-permute-start) | collective-permute-done | bytes 1310752 | tf_op jit(solution)/shard_map/ppermute | solution.py:605
  33.6 16.0 %attention.1 = (bf16[256,1024]{1,0:T(8,128)(2,1)}, bf16[256,1024]{1,0:T(8,128)(2,1)}, bf16[256,512]{1,0:T(8,128)(2,1)}, bf16[8,256,512]{2,1,0:T(8,128)(2,1)}, bf...) custom-call(s32[8]{0:T(128)} %get-tuple-element.37.refs_0_, ...), custom_call_target="tpu_custom_call" | custom-call | flops 10400000000 | bytes 16777216 | tf_op jit(solution)/shard_map/attention/pallas_call | solution.py:309
  49.6 8.9 %all-to-all-start.1 = ((bf16[8,256,512]{2,1,0:T(8,128)(2,1)}), bf16[8,256,512]{2,1,0:T(8,128)(2,1)S(1)}, u32[]{:S(2)}, u32[]{:S(2)}) async-start(bf16[8,256,512]{2,1,0:T(8,128)(2,1)} %get-tuple-element.58), calls=%async_computation.1 | async-start | bytes 4194304 | tf_op jit(solution)/shard_map/all_to_all | solution.py:609
  59.1 2.4 %collective-permute-done.1.refs_1_ = bf16[12,4,16,640]{3,2,1,0:T(8,128)(2,1)S(1)} collective-permute-done((bf16[12,4,16,640]{3,2,1,0:T(8,128)(2,1)}, bf16[12,4,16,640]{3,2,1,0:T(8,128)(2,1)S(1)}, u32[]{:S(2)}, u32[]{:S(2)}) %collective-permute-start.1) | collective-permute-done | bytes 983072 | tf_op jit(solution)/shard_map/ppermute | solution.py:605
  62.5 2.5 %fold.3 = (bf16[12,16,640]{2,1,0:T(8,128)(2,1)}, bf16[12,16,640]{2,1,0:T(8,128)(2,1)}, bf16[12,16,640]{2,1,0:T(8,128)(2,1)}, bf16[12,16,640]{2,1,0:T(8,128)(2,1)}) custom-call(bf16[12,4,16,640]{3,2,1,0:T(8,128)(2,1)} %get-tuple-element.46.refs_0_, bf16[12,4,16,640]{3,2,1,0:T(8,128)(2,1)} %copy-done.2), custom_call_target="tpu_custom_call" | custom-call | flops 1 | bytes 1 | tf_op jit(solution)/shard_map/fold/pallas_call | solution.py:480
  65.0 2.9 %collective-permute-start.2 = (bf16[12,16,640]{2,1,0:T(8,128)(2,1)}, bf16[12,16,640]{2,1,0:T(8,128)(2,1)S(1)}, u32[]{:S(2)}, u32[]{:S(2)}) collective-permute-start(bf16[12,16,640]{2,1,0:T(8,128)(2,1)} %get-tuple-element.49), channel_id=1, source_target_pairs={{0,4},{2,6},{4,0},{6,2},{1,5},{3,7},{5,1},{7,3},{8,12},{10,14},{12... | collective-permute-start | bytes 737288 | tf_op jit(solution)/shard_map/ppermute | solution.py:421
  68.3 2.3 %collective-permute-start.4 = (bf16[12,16,640]{2,1,0:T(8,128)(2,1)}, bf16[12,16,640]{2,1,0:T(8,128)(2,1)S(1)}, u32[]{:S(2)}, u32[]{:S(2)}) collective-permute-start(bf16[12,16,640]{2,1,0:T(8,128)(2,1)} %get-tuple-element.51), channel_id=1, source_target_pairs={{0,6},{2,0},{4,2},{6,4},{1,7},{3,1},{5,3},{7,5},{8,14},{10,8},{12,... | collective-permute-start | bytes 737288 | tf_op jit(solution)/shard_map/ppermute | solution.py:421
  70.6 3.3 %collective-permute-done.2.refs_2_ = bf16[12,16,640]{2,1,0:T(8,128)(2,1)S(1)} collective-permute-done((bf16[12,16,640]{2,1,0:T(8,128)(2,1)}, bf16[12,16,640]{2,1,0:T(8,128)(2,1)S(1)}, u32[]{:S(2)}, u32[]{:S(2)}) %collective-permute-start.2) | collective-permute-done | bytes 245792 | tf_op jit(solution)/shard_map/ppermute | solution.py:421
  73.9 5.9 %collective-permute-done.3.refs_3_ = bf16[12,16,640]{2,1,0:T(8,128)(2,1)S(1)} collective-permute-done((bf16[12,16,640]{2,1,0:T(8,128)(2,1)}, bf16[12,16,640]{2,1,0:T(8,128)(2,1)S(1)}, u32[]{:S(2)}, u32[]{:S(2)}) %collective-permute-start.3) | collective-permute-done | bytes 245792 | tf_op jit(solution)/shard_map/ppermute | solution.py:421
  80.6 2.1 %fold.4 = (bf16[4,16,640]{2,1,0:T(8,128)(2,1)}, bf16[4,16,640]{2,1,0:T(8,128)(2,1)}, bf16[4,16,640]{2,1,0:T(8,128)(2,1)}, bf16[4,16,640]{2,1,0:T(8,128)(2,1)}) custom-call(s32[8]{0:T(128)} %get-tuple-element.45.refs_0_, bf16[12,16,640]{2,1,0:T(8,128)(2,1)} %get-tuple-element.48.refs_1_, bf16[12,16,640]{2,1,0:T(8,128)(2,1)} %copy-done.4, ...), custom_call_target="tpu_custom_call" | custom-call | flops 1 | bytes 1 | tf_op jit(solution)/shard_map/fold/pallas_call | solution.py:480
  82.8 3.3 %collective-permute-start.5 = (bf16[4,16,640]{2,1,0:T(8,128)(2,1)}, bf16[4,16,640]{2,1,0:T(8,128)(2,1)S(1)}, u32[]{:S(2)}, u32[]{:S(2)}) collective-permute-start(bf16[4,16,640]{2,1,0:T(8,128)(2,1)} %get-tuple-element.53), channel_id=1, source_target_pairs={{0,32},{16,48},{32,0},{48,16},{1,33},{17,49},{33,1},{49,17},{2,34}... | collective-permute-start | bytes 245768 | tf_op jit(solution)/shard_map/ppermute | solution.py:421
  86.4 2.4 %collective-permute-start.7 = (bf16[4,16,640]{2,1,0:T(8,128)(2,1)}, bf16[4,16,640]{2,1,0:T(8,128)(2,1)S(1)}, u32[]{:S(2)}, u32[]{:S(2)}) collective-permute-start(bf16[4,16,640]{2,1,0:T(8,128)(2,1)} %get-tuple-element.55), channel_id=1, source_target_pairs={{0,48},{16,0},{32,16},{48,32},{1,49},{17,1},{33,17},{49,33},{2,50}... | collective-permute-start | bytes 245768 | tf_op jit(solution)/shard_map/ppermute | solution.py:421
  88.8 2.0 %collective-permute-done.6.refs_2_ = bf16[4,16,640]{2,1,0:T(8,128)(2,1)S(1)} collective-permute-done((bf16[4,16,640]{2,1,0:T(8,128)(2,1)}, bf16[4,16,640]{2,1,0:T(8,128)(2,1)S(1)}, u32[]{:S(2)}, u32[]{:S(2)}) %collective-permute-start.6) | collective-permute-done | bytes 81952 | tf_op jit(solution)/shard_map/ppermute | solution.py:421
  91.5 1.7 %fold.5 = (bf16[2,16,640]{2,1,0:T(8,128)(2,1)}, bf16[2,16,640]{2,1,0:T(8,128)(2,1)}) custom-call(bf16[4,16,640]{2,1,0:T(8,128)(2,1)} %get-tuple-element.52.refs_0_, bf16[4,16,640]{2,1,0:T(8,128)(2,1)} %copy-done.7, bf16[4,16,640]{2,1,0:T(8,128)(2,1)} %copy-done.8, bf16[4,16,640]{2,1,0:T(8,128)(2,1)} %copy-done.10), custom_call_target="tpu_custom_call" | custom-call | flops 1 | bytes 1 | tf_op jit(solution)/shard_map/fold/pallas_call | solution.py:480
  93.1 2.4 %collective-permute-start.8 = (bf16[2,16,640]{2,1,0:T(8,128)(2,1)}, bf16[2,16,640]{2,1,0:T(8,128)(2,1)S(1)}, u32[]{:S(2)}, u32[]{:S(2)}) collective-permute-start(bf16[2,16,640]{2,1,0:T(8,128)(2,1)} %get-tuple-element.59.a), channel_id=1, source_target_pairs={{0,8},{8,0},{64,72},{72,64},{1,9},{9,1},{65,73},{73,65},{2,10},{10... | collective-permute-start | bytes 122888 | tf_op jit(solution)/shard_map/ppermute | solution.py:420
  95.6 1.2 collective-permute-start.10
  96.8 1.3 copy-done
  98.1 2.8 %total.1 = bf16[8,256,512]{2,1,0:T(8,128)(2,1)} custom-call(bf16[8,256,512]{2,1,0:T(8,128)(2,1)} %copy-done), custom_call_target="tpu_custom_call" | custom-call | flops 1 | bytes 1 | tf_op jit(solution)/shard_map/total/pallas_call | solution.py:587
  101.0 5.1 %all-to-all-start.2 = ((bf16[8,256,512]{2,1,0:T(8,128)(2,1)}), bf16[8,256,512]{2,1,0:T(8,128)(2,1)S(1)}, u32[]{:S(2)}, u32[]{:S(2)}) async-start(bf16[8,256,512]{2,1,0:T(8,128)(2,1)} %total.1), calls=%async_computation.2 | async-start | bytes 4194304 | tf_op jit(solution)/shard_map/all_to_all | solution.py:609
  106.1 1.9 %finish.1 = bf16[32,640]{1,0:T(8,128)(2,1)} custom-call(bf16[2,16,640]{2,1,0:T(8,128)(2,1)} %get-tuple-element.59.a, bf16[2,16,640]{2,1,0:T(8,128)(2,1)} %copy-done.13, bf16[2,16,640]{2,1,0:T(8,128)(2,1)} %copy-done.15, bf16[2,16,640]{2,1,0:T(8,128)(2,1)} %copy-done.14, bf16[256,512]{1,0:T(8,128)(2,1)} %latent.3, f32[256,1]{1,0:T(8,128)} %get-tuple-element.63.inverse, ...), custom_call_target="tpu_custom_call" | custom-call | flops 1 | bytes 1 | tf_op jit(solution)/shard_map/finish/pallas_call | solution.py:517
  108.0 3.6 %collective-permute-start.11 = (bf16[32,640]{1,0:T(8,128)(2,1)}, bf16[32,640]{1,0:T(8,128)(2,1)S(1)}, u32[]{:S(2)}, u32[]{:S(2)}) collective-permute-start(bf16[32,640]{1,0:T(8,128)(2,1)} %finish.1), channel_id=1, source_target_pairs={{0,1},{1,0},{2,3},{3,2},{4,5},{5,4},{6,7},{7,6},{8,9},{9,8},{10,11... | collective-permute-start | bytes 122888 | tf_op jit(solution)/shard_map/ppermute | solution.py:605
  111.5 1.1 collective-permute-done.11
  113.4 2.4 %collective-permute-start.14 = (bf16[64,640]{1,0:T(8,128)(2,1)S(1)}, bf16[64,640]{1,0:T(8,128)(2,1)S(1)}, u32[]{:S(2)}, u32[]{:S(2)}) collective-permute-start(bf16[64,640]{1,0:T(8,128)(2,1)S(1)} %pad_maximum_fusion.refs_0_), channel_id=1, source_target_pairs={{0,6},{2,0},{4,2},{6,4},{1,7},{3,1},{5,3},{7,5},{8,14},{10,8},{12,... | collective-permute-start | bytes 245768 | tf_op jit(solution)/shard_map/ppermute | solution.py:421
  116.5 2.7 %collective-permute-done.14.refs_3_ = bf16[64,640]{1,0:T(8,128)(2,1)S(1)} collective-permute-done((bf16[64,640]{1,0:T(8,128)(2,1)S(1)}, bf16[64,640]{1,0:T(8,128)(2,1)S(1)}, u32[]{:S(2)}, u32[]{:S(2)}) %collective-permute-start.14) | collective-permute-done | bytes 81952 | tf_op jit(solution)/shard_map/ppermute | solution.py:421
  119.2 1.8 %collective-permute-done.13.refs_2_ = bf16[64,640]{1,0:T(8,128)(2,1)S(1)} collective-permute-done((bf16[64,640]{1,0:T(8,128)(2,1)S(1)}, bf16[64,640]{1,0:T(8,128)(2,1)S(1)}, u32[]{:S(2)}, u32[]{:S(2)}) %collective-permute-start.13) | collective-permute-done | bytes 81952 | tf_op jit(solution)/shard_map/ppermute | solution.py:421
  120.9 2.1 %collective-permute-done.12.refs_1_ = bf16[64,640]{1,0:T(8,128)(2,1)S(1)} collective-permute-done((bf16[64,640]{1,0:T(8,128)(2,1)S(1)}, bf16[64,640]{1,0:T(8,128)(2,1)S(1)}, u32[]{:S(2)}, u32[]{:S(2)}) %collective-permute-start.12) | collective-permute-done | bytes 81952 | tf_op jit(solution)/shard_map/ppermute | solution.py:421
  123.7 1.7 %assemble.1 = (bf16[256,512]{1,0:T(8,128)(2,1)}, bf16[64,256]{1,0:T(8,128)(2,1)}) custom-call(bf16[64,640]{1,0:T(8,128)(2,1)} %copy-done.3, bf16[64,640]{1,0:T(8,128)(2,1)} %copy-done.12, bf16[64,640]{1,0:T(8,128)(2,1)} %copy-done.11, bf16[64,640]{1,0:T(8,128)(2,1)} %copy-done.9), custom_call_target="tpu_custom_call" | custom-call | flops 1 | bytes 1 | tf_op jit(solution)/shard_map/assemble/pallas_call | solution.py:543
  125.4 6.0 %all-to-all-done.2 = bf16[8,256,512]{2,1,0:T(8,128)(2,1)S(1)} async-done(((bf16[8,256,512]{2,1,0:T(8,128)(2,1)}), bf16[8,256,512]{2,1,0:T(8,128)(2,1)S(1)}, u32[]{:S(2)}, u32[]{:S(2)}) %all-to-all-start.2) | async-done | bytes 2097184 | tf_op jit(solution)/shard_map/all_to_all | solution.py:609
  131.4 1.5 %fusion = (bf16[8,128,512]{2,1,0:T(8,128)(2,1)}, bf16[8,128,512]{2,1,0:T(8,128)(2,1)}) fusion(bf16[8,256,512]{2,1,0:T(8,128)(2,1)S(1)} %all-to-all-done.2), kind=kLoop, calls=%fused_computation.1 | loop fusion | bytes 4194304 | tf_op jit(solution)/shard_map/slice | solution.py:641
  (47 shorter events, 6.9 us)
Async XLA Ops:
  27.4 5.1 %copy-start.1 = (bf16[8,128,640]{2,1,0:T(8,128)(2,1)}, bf16[8,128,640]{2,1,0:T(8,128)(2,1)S(1)}, u32[]{:S(2)}) copy-start(bf16[8,128,640]{2,1,0:T(8,128)(2,1)S(1)} %all_to_all.15) | copy-start | bytes 3932164
  27.4 5.1 %collective-permute-start = (bf16[1024,640]{1,0:T(8,128)(2,1)S(1)}, bf16[1024,640]{1,0:T(8,128)(2,1)S(1)}, u32[]{:S(2)}, u32[]{:S(2)}) collective-permute-start(bf16[1024,640]{1,0:T(8,128)(2,1)S(1)} %bitcast.5), channel_id=1, source_target_pairs={{0,1},{1,0},{2,3},{3,2},{4,5},{5,4},{6,7},{7,6},{8,9},{9,8},{10,11... | collective-permute-start | bytes 3932168 | tf_op jit(solution)/shard_map/ppermute | solution.py:605
  32.5 1.0 copy-start.16
  49.6 47.2 %all-to-all-start.1 = ((bf16[8,256,512]{2,1,0:T(8,128)(2,1)}), bf16[8,256,512]{2,1,0:T(8,128)(2,1)S(1)}, u32[]{:S(2)}, u32[]{:S(2)}) async-start(bf16[8,256,512]{2,1,0:T(8,128)(2,1)} %get-tuple-element.58), calls=%async_computation.1 | async-start | bytes 4194304 | tf_op jit(solution)/shard_map/all_to_all | solution.py:609
  58.5 3.1 %collective-permute-start.1 = (bf16[12,4,16,640]{3,2,1,0:T(8,128)(2,1)}, bf16[12,4,16,640]{3,2,1,0:T(8,128)(2,1)S(1)}, u32[]{:S(2)}, u32[]{:S(2)}) collective-permute-start(bf16[12,4,16,640]{3,2,1,0:T(8,128)(2,1)} %get-tuple-element.47), channel_id=1, source_target_pairs={{0,1},{1,0},{2,3},{3,2},{4,5},{5,4},{6,7},{7,6},{8,9},{9,8},{10,11... | collective-permute-start | bytes 2949128 | tf_op jit(solution)/shard_map/ppermute | solution.py:605
  61.5 0.9 copy-start.2
  65.0 8.9 %collective-permute-start.2 = (bf16[12,16,640]{2,1,0:T(8,128)(2,1)}, bf16[12,16,640]{2,1,0:T(8,128)(2,1)S(1)}, u32[]{:S(2)}, u32[]{:S(2)}) collective-permute-start(bf16[12,16,640]{2,1,0:T(8,128)(2,1)} %get-tuple-element.49), channel_id=1, source_target_pairs={{0,4},{2,6},{4,0},{6,2},{1,5},{3,7},{5,1},{7,3},{8,12},{10,14},{12... | collective-permute-start | bytes 737288 | tf_op jit(solution)/shard_map/ppermute | solution.py:421
  67.9 11.9 %collective-permute-start.3 = (bf16[12,16,640]{2,1,0:T(8,128)(2,1)}, bf16[12,16,640]{2,1,0:T(8,128)(2,1)S(1)}, u32[]{:S(2)}, u32[]{:S(2)}) collective-permute-start(bf16[12,16,640]{2,1,0:T(8,128)(2,1)} %get-tuple-element.50), channel_id=1, source_target_pairs={{0,2},{2,4},{4,6},{6,0},{1,3},{3,5},{5,7},{7,1},{8,10},{10,12},{12... | collective-permute-start | bytes 737288 | tf_op jit(solution)/shard_map/ppermute | solution.py:421
  68.3 11.6 %collective-permute-start.4 = (bf16[12,16,640]{2,1,0:T(8,128)(2,1)}, bf16[12,16,640]{2,1,0:T(8,128)(2,1)S(1)}, u32[]{:S(2)}, u32[]{:S(2)}) collective-permute-start(bf16[12,16,640]{2,1,0:T(8,128)(2,1)} %get-tuple-element.51), channel_id=1, source_target_pairs={{0,6},{2,0},{4,2},{6,4},{1,7},{3,1},{5,3},{7,5},{8,14},{10,8},{12,... | collective-permute-start | bytes 737288 | tf_op jit(solution)/shard_map/ppermute | solution.py:421
  73.9 5.9 %copy-start.4 = (bf16[12,16,640]{2,1,0:T(8,128)(2,1)}, bf16[12,16,640]{2,1,0:T(8,128)(2,1)S(1)}, u32[]{:S(2)}) copy-start(bf16[12,16,640]{2,1,0:T(8,128)(2,1)S(1)} %collective-permute-done.2.refs_2_) | copy-start | bytes 737284
  79.9 0.7 copy-start.5
  79.9 0.8 copy-start.6
  82.8 6.0 %collective-permute-start.5 = (bf16[4,16,640]{2,1,0:T(8,128)(2,1)}, bf16[4,16,640]{2,1,0:T(8,128)(2,1)S(1)}, u32[]{:S(2)}, u32[]{:S(2)}) collective-permute-start(bf16[4,16,640]{2,1,0:T(8,128)(2,1)} %get-tuple-element.53), channel_id=1, source_target_pairs={{0,32},{16,48},{32,0},{48,16},{1,33},{17,49},{33,1},{49,17},{2,34}... | collective-permute-start | bytes 245768 | tf_op jit(solution)/shard_map/ppermute | solution.py:421
  86.1 4.7 %collective-permute-start.6 = (bf16[4,16,640]{2,1,0:T(8,128)(2,1)}, bf16[4,16,640]{2,1,0:T(8,128)(2,1)S(1)}, u32[]{:S(2)}, u32[]{:S(2)}) collective-permute-start(bf16[4,16,640]{2,1,0:T(8,128)(2,1)} %get-tuple-element.54), channel_id=1, source_target_pairs={{0,16},{16,32},{32,48},{48,0},{1,17},{17,33},{33,49},{49,1},{2,18}... | collective-permute-start | bytes 245768 | tf_op jit(solution)/shard_map/ppermute | solution.py:421
  86.4 4.4 %collective-permute-start.7 = (bf16[4,16,640]{2,1,0:T(8,128)(2,1)}, bf16[4,16,640]{2,1,0:T(8,128)(2,1)S(1)}, u32[]{:S(2)}, u32[]{:S(2)}) collective-permute-start(bf16[4,16,640]{2,1,0:T(8,128)(2,1)} %get-tuple-element.55), channel_id=1, source_target_pairs={{0,48},{16,0},{32,16},{48,32},{1,49},{17,1},{33,17},{49,33},{2,50}... | collective-permute-start | bytes 245768 | tf_op jit(solution)/shard_map/ppermute | solution.py:421
  88.8 2.0 %copy-start.7 = (bf16[4,16,640]{2,1,0:T(8,128)(2,1)}, bf16[4,16,640]{2,1,0:T(8,128)(2,1)S(1)}, u32[]{:S(2)}) copy-start(bf16[4,16,640]{2,1,0:T(8,128)(2,1)S(1)} %collective-permute-done.5.refs_1_) | copy-start | bytes 245764
  90.8 0.7 copy-start.10
  93.1 7.8 %collective-permute-start.8 = (bf16[2,16,640]{2,1,0:T(8,128)(2,1)}, bf16[2,16,640]{2,1,0:T(8,128)(2,1)S(1)}, u32[]{:S(2)}, u32[]{:S(2)}) collective-permute-start(bf16[2,16,640]{2,1,0:T(8,128)(2,1)} %get-tuple-element.59.a), channel_id=1, source_target_pairs={{0,8},{8,0},{64,72},{72,64},{1,9},{9,1},{65,73},{73,65},{2,10},{10... | collective-permute-start | bytes 122888 | tf_op jit(solution)/shard_map/ppermute | solution.py:420
  95.6 5.4 %collective-permute-start.10 = (bf16[2,16,640]{2,1,0:T(8,128)(2,1)}, bf16[2,16,640]{2,1,0:T(8,128)(2,1)S(1)}, u32[]{:S(2)}, u32[]{:S(2)}) collective-permute-start(bf16[2,16,640]{2,1,0:T(8,128)(2,1)} %get-tuple-element.57), channel_id=1, source_target_pairs={{0,72},{8,64},{64,8},{72,0},{1,73},{9,65},{65,9},{73,1},{2,74},{10... | collective-permute-start | bytes 122888 | tf_op jit(solution)/shard_map/ppermute | solution.py:420
  96.8 4.2 %collective-permute-start.9 = (bf16[2,16,640]{2,1,0:T(8,128)(2,1)}, bf16[2,16,640]{2,1,0:T(8,128)(2,1)S(1)}, u32[]{:S(2)}, u32[]{:S(2)}) collective-permute-start(bf16[2,16,640]{2,1,0:T(8,128)(2,1)} %get-tuple-element.57), channel_id=1, source_target_pairs={{0,64},{8,72},{64,0},{72,8},{1,65},{9,73},{65,1},{73,9},{2,66},{10... | collective-permute-start | bytes 122888 | tf_op jit(solution)/shard_map/ppermute | solution.py:420
  96.8 1.3 %copy-start = (bf16[8,256,512]{2,1,0:T(8,128)(2,1)}, bf16[8,256,512]{2,1,0:T(8,128)(2,1)S(1)}, u32[]{:S(2)}) copy-start(bf16[8,256,512]{2,1,0:T(8,128)(2,1)S(1)} %all-to-all-done.1.pieces) | copy-start | bytes 6291460
  100.9 5.1 %copy-start.13 = (bf16[2,16,640]{2,1,0:T(8,128)(2,1)}, bf16[2,16,640]{2,1,0:T(8,128)(2,1)S(1)}, u32[]{:S(2)}) copy-start(bf16[2,16,640]{2,1,0:T(8,128)(2,1)S(1)} %collective-permute-done.8.b) | copy-start | bytes 122884
  101.0 5.1 %copy-start.14 = (bf16[2,16,640]{2,1,0:T(8,128)(2,1)}, bf16[2,16,640]{2,1,0:T(8,128)(2,1)S(1)}, u32[]{:S(2)}) copy-start(bf16[2,16,640]{2,1,0:T(8,128)(2,1)S(1)} %collective-permute-done.10.d) | copy-start | bytes 122884
  101.0 5.1 %copy-start.15 = (bf16[2,16,640]{2,1,0:T(8,128)(2,1)}, bf16[2,16,640]{2,1,0:T(8,128)(2,1)S(1)}, u32[]{:S(2)}) copy-start(bf16[2,16,640]{2,1,0:T(8,128)(2,1)S(1)} %collective-permute-done.9.c) | copy-start | bytes 122884
  101.0 30.4 %all-to-all-start.2 = ((bf16[8,256,512]{2,1,0:T(8,128)(2,1)}), bf16[8,256,512]{2,1,0:T(8,128)(2,1)S(1)}, u32[]{:S(2)}, u32[]{:S(2)}) async-start(bf16[8,256,512]{2,1,0:T(8,128)(2,1)} %total.1), calls=%async_computation.2 | async-start | bytes 4194304 | tf_op jit(solution)/shard_map/all_to_all | solution.py:609
  108.0 4.6 %collective-permute-start.11 = (bf16[32,640]{1,0:T(8,128)(2,1)}, bf16[32,640]{1,0:T(8,128)(2,1)S(1)}, u32[]{:S(2)}, u32[]{:S(2)}) collective-permute-start(bf16[32,640]{1,0:T(8,128)(2,1)} %finish.1), channel_id=1, source_target_pairs={{0,1},{1,0},{2,3},{3,2},{4,5},{5,4},{6,7},{7,6},{8,9},{9,8},{10,11... | collective-permute-start | bytes 122888 | tf_op jit(solution)/shard_map/ppermute | solution.py:605
  113.4 9.6 %copy-start.3 = (bf16[64,640]{1,0:T(8,128)(2,1)}, bf16[64,640]{1,0:T(8,128)(2,1)S(1)}, u32[]{:S(2)}) copy-start(bf16[64,640]{1,0:T(8,128)(2,1)S(1)} %pad_maximum_fusion.refs_0_) | copy-start | bytes 245764
  113.4 5.8 %collective-permute-start.14 = (bf16[64,640]{1,0:T(8,128)(2,1)S(1)}, bf16[64,640]{1,0:T(8,128)(2,1)S(1)}, u32[]{:S(2)}, u32[]{:S(2)}) collective-permute-start(bf16[64,640]{1,0:T(8,128)(2,1)S(1)} %pad_maximum_fusion.refs_0_), channel_id=1, source_target_pairs={{0,6},{2,0},{4,2},{6,4},{1,7},{3,1},{5,3},{7,5},{8,14},{10,8},{12,... | collective-permute-start | bytes 245768 | tf_op jit(solution)/shard_map/ppermute | solution.py:421
  115.8 5.1 %collective-permute-start.13 = (bf16[64,640]{1,0:T(8,128)(2,1)S(1)}, bf16[64,640]{1,0:T(8,128)(2,1)S(1)}, u32[]{:S(2)}, u32[]{:S(2)}) collective-permute-start(bf16[64,640]{1,0:T(8,128)(2,1)S(1)} %pad_maximum_fusion.refs_0_), channel_id=1, source_target_pairs={{0,4},{2,6},{4,0},{6,2},{1,5},{3,7},{5,1},{7,3},{8,12},{10,14},{12... | collective-permute-start | bytes 245768 | tf_op jit(solution)/shard_map/ppermute | solution.py:421
  116.4 6.6 %collective-permute-start.12 = (bf16[64,640]{1,0:T(8,128)(2,1)S(1)}, bf16[64,640]{1,0:T(8,128)(2,1)S(1)}, u32[]{:S(2)}, u32[]{:S(2)}) collective-permute-start(bf16[64,640]{1,0:T(8,128)(2,1)S(1)} %pad_maximum_fusion.refs_0_), channel_id=1, source_target_pairs={{0,2},{2,4},{4,6},{6,0},{1,3},{3,5},{5,7},{7,1},{8,10},{10,12},{12... | collective-permute-start | bytes 245768 | tf_op jit(solution)/shard_map/ppermute | solution.py:421
  119.2 3.8 %copy-start.9 = (bf16[64,640]{1,0:T(8,128)(2,1)}, bf16[64,640]{1,0:T(8,128)(2,1)S(1)}, u32[]{:S(2)}) copy-start(bf16[64,640]{1,0:T(8,128)(2,1)S(1)} %collective-permute-done.14.refs_3_) | copy-start | bytes 245764
  120.9 2.1 %copy-start.11 = (bf16[64,640]{1,0:T(8,128)(2,1)}, bf16[64,640]{1,0:T(8,128)(2,1)S(1)}, u32[]{:S(2)}) copy-start(bf16[64,640]{1,0:T(8,128)(2,1)S(1)} %collective-permute-done.13.refs_2_) | copy-start | bytes 245764
  (2 other events, 1.3 us)

commit v3 on v2

--- a/solution.py
+++ b/solution.py
@@ -24,6 +24,7 @@
 MAX_TILES = 6
 SLOTS = 12
 WIDE = (3, 4)
+LONG = pl.CostEstimate(flops=100000000000, bytes_accessed=1, transcendentals=0)
 SMALL = pl.CostEstimate(flops=1, bytes_accessed=1, transcendentals=0)
 PACK = 640
 EXTRA = PACK - D_LAT
@@ -141,33 +142,30 @@
         shown = lax.broadcasted_iota(jnp.int32, (ROWS, TILE), 1) <= lax.broadcasted_iota(
             jnp.int32, (ROWS, TILE), 0
         )
+        heads = range(2)
         parts, rope_sum, dq = [], None, []
-        for h in range(2):
-            k_full = jnp.concatenate(
-                [both[:, h * 256 : h * 256 + 128], all_keys[:, D_LAT:]], axis=1
-            )
-            value = both[:, h * 256 + 128 : (h + 1) * 256]
-            score = dot_nt(qf[h], k_full)
-            score = jnp.concatenate(
-                [jnp.where(shown, score[:, :TILE], HIDE), score[:, TILE:]], axis=1
-            )
-            shift = jnp.max(score, axis=1, keepdims=True) * base2
-            expo = jnp.exp2(score * base2 - shift)
-            inv = 1.0 / jnp.sum(expo, axis=1, keepdims=True)
-            expo = expo.astype(BF)
-            mixed = dot(expo, value) * inv
-            out[:, h * D_V : (h + 1) * D_V] = mixed.astype(BF)
-            g = gb[h].astype(F32)
-            row_dot = jnp.sum(mixed * g, axis=1, keepdims=True)
-            slope = inv * SCALING
-            offset = row_dot * slope
-            dprobs = dot_nt(gb[h], value)
-            ds = (expo.astype(F32) * (dprobs * slope - offset)).astype(BF)
-            dq.append(dot(ds, k_full))
-            dk = dot(qt[h], ds)
-            dv = dot((g * inv).astype(BF).T, expo)
-            parts += [dk[:D_NOPE].astype(BF), dv.astype(BF)]
-            rope_sum = dk[D_NOPE:] if h == 0 else rope_sum + dk[D_NOPE:]
+        k_fulls = [jnp.concatenate([both[:, h * 256 : h * 256 + 128], all_keys[:, D_LAT:]], axis=1) for h in heads]
+        values = [both[:, h * 256 + 128 : (h + 1) * 256] for h in heads]
+        scores = [dot_nt(qf[h], k_fulls[h]) for h in heads]
+        scores = [jnp.concatenate([jnp.where(shown, x[:, :TILE], HIDE), x[:, TILE:]], axis=1) for x in scores]
+        dprobs = [dot_nt(gb[h], values[h]) for h in heads]
+        expos = [jnp.exp2(x * base2 - jnp.max(x, axis=1, keepdims=True) * base2) for x in scores]
+        invs = [1.0 / jnp.sum(x, axis=1, keepdims=True) for x in expos]
+        expos = [x.astype(BF) for x in expos]
+        mixes = [dot(expos[h], values[h]) * invs[h] for h in heads]
+        gs = [gb[h].astype(F32) for h in heads]
+        dvs = [dot((gs[h] * invs[h]).astype(BF).T, expos[h]) for h in heads]
+        dss = []
+        for h in heads:
+            out[:, h * D_V : (h + 1) * D_V] = mixes[h].astype(BF)
+            slope = invs[h] * SCALING
+            offset = jnp.sum(mixes[h] * gs[h], axis=1, keepdims=True) * slope
+            dss.append((expos[h].astype(F32) * (dprobs[h] * slope - offset)).astype(BF))
+        dks = [dot(qt[h], dss[h]) for h in heads]
+        dq = [dot(dss[h], k_fulls[h]) for h in heads]
+        for h in heads:
+            parts += [dks[h][:D_NOPE].astype(BF), dvs[h].astype(BF)]
+        rope_sum = dks[0][D_NOPE:] + dks[1][D_NOPE:]
         dkv = jnp.concatenate(parts, axis=0)
         add_grads(slice(0, width), dot(wt[...], dkv), rope_sum)
         finish_heads(dq, dot(dkv, all_keys[:, :D_LAT]))
@@ -483,20 +481,22 @@
         out_specs=[vector] * cuts,
         out_shape=[jax.ShapeDtypeStruct(shape, BF)] * cuts,
         scratch_shapes=scratch,
-        cost_estimate=SMALL,
+        cost_estimate=LONG if kernel is fold_y_kernel else SMALL,
         name="fold",
     )(*operands)
 
 
-def gather_grads(kept, sent, meta):
+def gather_grads(kept, sent, meta, total):
     slots = sent.shape[0]
     cut = fold(fold_y_kernel, [kept, swap_core(sent)], 4, (slots, BLOCK, PACK))
     parts = [cut[0]] + [move(cut[d], "y", d) for d in (2, 1, 3)]
     spread = pltpu.VMEM((4, 4, BLOCK, PACK), BF)
     cut = fold(fold_z_kernel, [meta] + parts, 4, (4, BLOCK, PACK), [spread])
     parts = [cut[0]] + [move(cut[d], "z", d) for d in (2, 1, 3)]
+    parts, total = lax.optimization_barrier((parts, total))
     cut = fold(fold_x_kernel, parts, 2, (2, BLOCK, PACK))
-    return [cut[0], move(cut[0], "x", 1), move(cut[1], "x", 2), move(cut[1], "x", 3)]
+    cut, total = lax.optimization_barrier((cut, total))
+    return total, [cut[0], move(cut[0], "x", 1), move(cut[1], "x", 2), move(cut[1], "x", 3)]
 
 
 def finish_kernel(a, b, c, d, latent, inverse, gain, out):
@@ -519,7 +519,7 @@
         in_specs=[vector] * 7,
         out_specs=vector,
         out_shape=jax.ShapeDtypeStruct((2 * BLOCK, PACK), BF),
-        cost_estimate=SMALL,
+        cost_estimate=LONG,
         name="finish",
     )(*parts, latent, inverse, latent_gain)
 
@@ -557,14 +557,11 @@
 def total_kernel(pieces, out, parts, sums, in_sems, out_sems):
     steps = in_sems.shape[0]
     size = sums.shape[0] // steps
+    copies = []
 
     def load(step):
         rows = pl.ds(step * size, size)
         return pltpu.make_async_copy(pieces.at[:, rows, :], parts.at[:, rows, :], in_sems.at[step])
-
-    def store(step, i):
-        rows = pl.ds(step * size, size)
-        return pltpu.make_async_copy(sums.at[rows, :], out.at[i, rows, :], out_sems.at[step, i])
 
     for step in range(steps):
         load(step).start()
@@ -576,10 +573,11 @@
             total = total + parts[i, rows, :].astype(F32)
         sums[rows, :] = total.astype(BF)
         for i in range(CTX):
-            store(step, i).start()
-    for step in range(steps):
-        for i in range(CTX):
-            store(step, i).wait()
+            copy = pltpu.make_async_copy(sums.at[rows, :], out.at[i, rows, :], out_sems.at[step, i])
+            copy.start()
+            copies.append(copy)
+    for copy in copies:
+        copy.wait()
 
 
 def total_and_copy(pieces):
@@ -595,7 +593,7 @@
             pltpu.SemaphoreType.DMA((4,)),
             pltpu.SemaphoreType.DMA((4, CTX)),
         ],
-        compiler_params=pltpu.CompilerParams(vmem_limit_bytes=56 << 20),
+        compiler_params=pltpu.CompilerParams(vmem_limit_bytes=62 << 20),
         cost_estimate=SMALL,
         name="total",
     )(pieces)
@@ -631,8 +629,7 @@
     out, dqn, dqr, dw, kept, sent, meta = attention(shared, q_nope, q_rope, d_out, w_uk, w_uv)
     pieces = exchange(dw, CTX_AXES)
     total = total_and_copy(pieces)
-    parts = gather_grads(kept, sent, meta)
-    parts, total = lax.optimization_barrier((parts, total))
+    total, parts = gather_grads(kept, sent, meta, total)
     weights = exchange(total, CTX_AXES)
     final = finish(parts, latent, inverse, latent_gain)
     pair = jnp.concatenate([final, swap_core(final)], axis=0)

time: 135 us -> 127 us (0.941)
  waiting for transfers between devices: 29.9 us -> 25.9 us
  starting transfers between devices: 39 us -> 36.9 us
    ppermute x3, waiting for transfers between devices: 6.15 us -> 3.75 us  [swap_core(): return lax.ppermute(x, 'core', [(0, 1), (1, 0)])]
    ppermute x9, waiting for transfers between devices: 17.8 us -> 15.9 us  [move(): return lax.ppermute(x, axis, [(i, (i + distance) % 4) for i in range(4)])]
    unnamed x34 -> x32, local copies, waits for them, and re-layouts: 5.4 us -> 4.67 us
  transfers between devices with their start and end apart: 17 -> 17, of which waited for: 10 -> 9; matrix products, arithmetic and copies ran while one was open for 1% -> 1% of each run, Pallas kernels for 10% -> 9%
where the time goes in v3:
time: 127 us; the launch traced here: 126 us
  starting transfers between devices  36.9 us (29%)
  Pallas kernels  31.5 us (25%)
  waiting for transfers between devices  25.9 us (20%)
  blocking collectives  23.9 us (19%)
  local copies, waits for them, and re-layouts  6.19 us (5%)
    all_to_all x1, blocking collectives, exchange(): return lax.all_to_all(x, axes, 0, 0, tiled=True)  23.9 us
    pallas_call x1, Pallas kernels, attention(): pl.pallas_call(attention_kernel, grid=(pairs,), in_specs=in_specs, out_sp...  16.1 us
    ppermute x9, waiting for transfers between devices, move(): return lax.ppermute(x, axis, [(i, (i + distance) % 4) for i in range(4)])  15.9 us
    ppermute x9, starting transfers between devices, move(): return lax.ppermute(x, axis, [(i, (i + distance) % 4) for i in range(4)])  14.3 us
    all_to_all x2, starting transfers between devices, exchange(): return lax.all_to_all(x, axes, 0, 0, tiled=True)  12.9 us
    pallas_call x3, Pallas kernels, fold(): pl.pallas_call(kernel, in_specs=[scalar if x.dtype == jnp.int32 else vect...  6.3 us
    all_to_all x2, waiting for transfers between devices, exchange(): return lax.all_to_all(x, axes, 0, 0, tiled=True)  6.25 us
    ppermute x3, starting transfers between devices, swap_core(): return lax.ppermute(x, 'core', [(0, 1), (1, 0)])  6.12 us
  transfers between devices with their start and end apart: 17, of which 9 were waited for; matrix products, arithmetic and copies ran while one was open for 1% of the time, Pallas kernels for 9%

profile of v3, /device:TPU:1, one launch (start us, length us, event | category | flops | bytes accessed | tf_op | source)
XLA Modules:
  0.0 126.0 jit_solution(10822863015776786746)
XLA Ops:
  0.6 2.8 %prepare.1 = (bf16[256,640]{1,0:T(8,128)(2,1)}, bf16[8,128,640]{2,1,0:T(8,128)(2,1)}, bf16[256,64]{1,0:T(8,128)(2,1)}, f32[256,1]{1,0:T(8,128)}, f32[256,1]{1,0:T(8,128)}, /*index=5*/s32[8]{0:T(128)}) custom-call(bf16[256,512]{1,0:T(8,128)(2,1)} %latent.3, bf16[512]{0:T(512)(128)(2,1)} %gain.3, bf16[64,256]{1,0:T(8,128)(2,1)} %rope_t.1, s32[1,256]{1,0:T(1,128)} %bitcast.9, ...), custom_call_target="tpu_custom_call" | custom-call | flops 1 | bytes 1 | tf_op jit(solution)/shard_map/prepare/pallas_call | solution.py:389
  3.4 23.9 %all_to_all.15 = bf16[8,128,640]{2,1,0:T(8,128)(2,1)S(1)} all-to-all(bf16[8,128,640]{2,1,0:T(8,128)(2,1)} %get-tuple-element.42), channel_id=1, replica_groups=mesh['xl'=2,'z'=4,'xh'=2,'y'=4,'core'=2] {'xl','z'}, dimensions={0} | all-to-all | bytes 2621440 | tf_op jit(solution)/shard_map/all_to_all | solution.py:607
  27.4 2.5 %collective-permute-start = (bf16[1024,640]{1,0:T(8,128)(2,1)S(1)}, bf16[1024,640]{1,0:T(8,128)(2,1)S(1)}, u32[]{:S(2)}, u32[]{:S(2)}) collective-permute-start(bf16[1024,640]{1,0:T(8,128)(2,1)S(1)} %bitcast.5), channel_id=1, source_target_pairs={{0,1},{1,0},{2,3},{3,2},{4,5},{5,4},{6,7},{7,6},{8,9},{9,8},{10,11... | collective-permute-start | bytes 3932168 | tf_op jit(solution)/shard_map/ppermute | solution.py:603
  29.8 2.7 %collective-permute-done.refs_3_ = bf16[1024,640]{1,0:T(8,128)(2,1)S(1)} collective-permute-done((bf16[1024,640]{1,0:T(8,128)(2,1)S(1)}, bf16[1024,640]{1,0:T(8,128)(2,1)S(1)}, u32[]{:S(2)}, u32[]{:S(2)}) %collective-permute-start) | collective-permute-done | bytes 1310752 | tf_op jit(solution)/shard_map/ppermute | solution.py:603
  32.5 1.0 copy-done.11
  33.5 16.1 %attention.1 = (bf16[256,1024]{1,0:T(8,128)(2,1)}, bf16[256,1024]{1,0:T(8,128)(2,1)}, bf16[256,512]{1,0:T(8,128)(2,1)}, bf16[8,256,512]{2,1,0:T(8,128)(2,1)}, bf...) custom-call(s32[8]{0:T(128)} %get-tuple-element.40.refs_0_, ...), custom_call_target="tpu_custom_call" | custom-call | flops 10400000000 | bytes 16777216 | tf_op jit(solution)/shard_map/attention/pallas_call | solution.py:307
  50.1 8.4 %all-to-all-start.1 = ((bf16[8,256,512]{2,1,0:T(8,128)(2,1)}), bf16[8,256,512]{2,1,0:T(8,128)(2,1)}, u32[]{:S(2)}, u32[]{:S(2)}) async-start(bf16[8,256,512]{2,1,0:T(8,128)(2,1)} %get-tuple-element.59), calls=%async_computation.1 | async-start | bytes 4194304 | tf_op jit(solution)/shard_map/all_to_all | solution.py:607
  58.5 0.9 copy-done.12
  59.4 2.5 %fold.3 = (bf16[12,16,640]{2,1,0:T(8,128)(2,1)}, bf16[12,16,640]{2,1,0:T(8,128)(2,1)}, bf16[12,16,640]{2,1,0:T(8,128)(2,1)}, bf16[12,16,640]{2,1,0:T(8,128)(2,1)}) custom-call(bf16[12,4,16,640]{3,2,1,0:T(8,128)(2,1)} %get-tuple-element.49.refs_0_, bf16[12,4,16,640]{3,2,1,0:T(8,128)(2,1)} %copy-done.12), custom_call_target="tpu_custom_call" | custom-call | flops 99999997952 | bytes 1 | tf_op jit(solution)/shard_map/fold/pallas_call | solution.py:478
  62.0 2.9 %collective-permute-start.2 = (bf16[12,16,640]{2,1,0:T(8,128)(2,1)}, bf16[12,16,640]{2,1,0:T(8,128)(2,1)S(1)}, u32[]{:S(2)}, u32[]{:S(2)}) collective-permute-start(bf16[12,16,640]{2,1,0:T(8,128)(2,1)} %get-tuple-element.52), channel_id=1, source_target_pairs={{0,4},{2,6},{4,0},{6,2},{1,5},{3,7},{5,1},{7,3},{8,12},{10,14},{12... | collective-permute-start | bytes 737288 | tf_op jit(solution)/shard_map/ppermute | solution.py:419
  65.3 2.3 %collective-permute-start.4 = (bf16[12,16,640]{2,1,0:T(8,128)(2,1)}, bf16[12,16,640]{2,1,0:T(8,128)(2,1)S(1)}, u32[]{:S(2)}, u32[]{:S(2)}) collective-permute-start(bf16[12,16,640]{2,1,0:T(8,128)(2,1)} %get-tuple-element.54), channel_id=1, source_target_pairs={{0,6},{2,0},{4,2},{6,4},{1,7},{3,1},{5,3},{7,5},{8,14},{10,8},{12,... | collective-permute-start | bytes 737288 | tf_op jit(solution)/shard_map/ppermute | solution.py:419
  67.6 3.4 %collective-permute-done.2.refs_2_ = bf16[12,16,640]{2,1,0:T(8,128)(2,1)S(1)} collective-permute-done((bf16[12,16,640]{2,1,0:T(8,128)(2,1)}, bf16[12,16,640]{2,1,0:T(8,128)(2,1)S(1)}, u32[]{:S(2)}, u32[]{:S(2)}) %collective-permute-start.2) | collective-permute-done | bytes 245792 | tf_op jit(solution)/shard_map/ppermute | solution.py:419
  70.9 6.0 %collective-permute-done.3.refs_3_ = bf16[12,16,640]{2,1,0:T(8,128)(2,1)S(1)} collective-permute-done((bf16[12,16,640]{2,1,0:T(8,128)(2,1)}, bf16[12,16,640]{2,1,0:T(8,128)(2,1)S(1)}, u32[]{:S(2)}, u32[]{:S(2)}) %collective-permute-start.3) | collective-permute-done | bytes 245792 | tf_op jit(solution)/shard_map/ppermute | solution.py:419
  77.7 2.1 %fold.4 = (bf16[4,16,640]{2,1,0:T(8,128)(2,1)}, bf16[4,16,640]{2,1,0:T(8,128)(2,1)}, bf16[4,16,640]{2,1,0:T(8,128)(2,1)}, bf16[4,16,640]{2,1,0:T(8,128)(2,1)}) custom-call(s32[8]{0:T(128)} %get-tuple-element.48.refs_0_, bf16[12,16,640]{2,1,0:T(8,128)(2,1)} %get-tuple-element.51.refs_1_, bf16[12,16,640]{2,1,0:T(8,128)(2,1)} %copy-done.2, ...), custom_call_target="tpu_custom_call" | custom-call | flops 1 | bytes 1 | tf_op jit(solution)/shard_map/fold/pallas_call | solution.py:478
  79.8 2.9 %collective-permute-start.5 = (bf16[4,16,640]{2,1,0:T(8,128)(2,1)}, bf16[4,16,640]{2,1,0:T(8,128)(2,1)S(1)}, u32[]{:S(2)}, u32[]{:S(2)}) collective-permute-start(bf16[4,16,640]{2,1,0:T(8,128)(2,1)} %get-tuple-element.56), channel_id=1, source_target_pairs={{0,32},{16,48},{32,0},{48,16},{1,33},{17,49},{33,1},{49,17},{2,34}... | collective-permute-start | bytes 245768 | tf_op jit(solution)/shard_map/ppermute | solution.py:419
  83.1 2.3 %collective-permute-start.7 = (bf16[4,16,640]{2,1,0:T(8,128)(2,1)}, bf16[4,16,640]{2,1,0:T(8,128)(2,1)S(1)}, u32[]{:S(2)}, u32[]{:S(2)}) collective-permute-start(bf16[4,16,640]{2,1,0:T(8,128)(2,1)} %get-tuple-element.58), channel_id=1, source_target_pairs={{0,48},{16,0},{32,16},{48,32},{1,49},{17,1},{33,17},{49,33},{2,50}... | collective-permute-start | bytes 245768 | tf_op jit(solution)/shard_map/ppermute | solution.py:419
  85.7 2.8 %total.1 = bf16[8,256,512]{2,1,0:T(8,128)(2,1)} custom-call(bf16[8,256,512]{2,1,0:T(8,128)(2,1)} %all-to-all-done.1.pieces), custom_call_target="tpu_custom_call" | custom-call | flops 1 | bytes 1 | tf_op jit(solution)/shard_map/total/pallas_call | solution.py:585
  89.1 1.7 %fold.5 = (bf16[2,16,640]{2,1,0:T(8,128)(2,1)}, bf16[2,16,640]{2,1,0:T(8,128)(2,1)}) custom-call(bf16[4,16,640]{2,1,0:T(8,128)(2,1)} %get-tuple-element.60.refs_0_, bf16[4,16,640]{2,1,0:T(8,128)(2,1)} %copy-done.5, bf16[4,16,640]{2,1,0:T(8,128)(2,1)} %copy-done.6, bf16[4,16,640]{2,1,0:T(8,128)(2,1)} %copy-done.7), custom_call_target="tpu_custom_call" | custom-call | flops 1 | bytes 1 | tf_op jit(solution)/shard_map/fold/pallas_call | solution.py:478
  90.8 2.5 %collective-permute-start.8 = (bf16[2,16,640]{2,1,0:T(8,128)(2,1)}, bf16[2,16,640]{2,1,0:T(8,128)(2,1)S(1)}, u32[]{:S(2)}, u32[]{:S(2)}) collective-permute-start(bf16[2,16,640]{2,1,0:T(8,128)(2,1)} %get-tuple-element.67.a), channel_id=1, source_target_pairs={{0,8},{8,0},{64,72},{72,64},{1,9},{9,1},{65,73},{73,65},{2,10},{10... | collective-permute-start | bytes 122888 | tf_op jit(solution)/shard_map/ppermute | solution.py:418
  93.3 1.1 collective-permute-start.10
  94.4 4.5 %all-to-all-start.2 = ((bf16[8,256,512]{2,1,0:T(8,128)(2,1)}), bf16[8,256,512]{2,1,0:T(8,128)(2,1)S(1)}, u32[]{:S(2)}, u32[]{:S(2)}) async-start(bf16[8,256,512]{2,1,0:T(8,128)(2,1)} %total.1), calls=%async_computation.2 | async-start | bytes 4194304 | tf_op jit(solution)/shard_map/all_to_all | solution.py:607
  99.5 1.8 %finish.1 = bf16[32,640]{1,0:T(8,128)(2,1)} custom-call(bf16[2,16,640]{2,1,0:T(8,128)(2,1)} %get-tuple-element.67.a, bf16[2,16,640]{2,1,0:T(8,128)(2,1)} %copy-done.13, bf16[2,16,640]{2,1,0:T(8,128)(2,1)} %copy-done.15, bf16[2,16,640]{2,1,0:T(8,128)(2,1)} %copy-done.14, bf16[256,512]{1,0:T(8,128)(2,1)} %latent.3, f32[256,1]{1,0:T(8,128)} %get-tuple-element.69.inverse, ...), custom_call_target="tpu_custom_call" | custom-call | flops 99999997952 | bytes 1 | tf_op jit(solution)/shard_map/finish/pallas_call | solution.py:517
  101.4 3.2 %collective-permute-start.11 = (bf16[32,640]{1,0:T(8,128)(2,1)}, bf16[32,640]{1,0:T(8,128)(2,1)S(1)}, u32[]{:S(2)}, u32[]{:S(2)}) collective-permute-start(bf16[32,640]{1,0:T(8,128)(2,1)} %finish.1), channel_id=1, source_target_pairs={{0,1},{1,0},{2,3},{3,2},{4,5},{5,4},{6,7},{7,6},{8,9},{9,8},{10,11... | collective-permute-start | bytes 122888 | tf_op jit(solution)/shard_map/ppermute | solution.py:603
  104.6 1.1 collective-permute-done.11
  105.7 0.8 pad_maximum_fusion.refs_0_
  106.5 2.5 %collective-permute-start.14 = (bf16[64,640]{1,0:T(8,128)(2,1)S(1)}, bf16[64,640]{1,0:T(8,128)(2,1)S(1)}, u32[]{:S(2)}, u32[]{:S(2)}) collective-permute-start(bf16[64,640]{1,0:T(8,128)(2,1)S(1)} %pad_maximum_fusion.refs_0_), channel_id=1, source_target_pairs={{0,6},{2,0},{4,2},{6,4},{1,7},{3,1},{5,3},{7,5},{8,14},{10,8},{12,... | collective-permute-start | bytes 245768 | tf_op jit(solution)/shard_map/ppermute | solution.py:419
  109.6 2.7 %collective-permute-done.14.refs_3_ = bf16[64,640]{1,0:T(8,128)(2,1)S(1)} collective-permute-done((bf16[64,640]{1,0:T(8,128)(2,1)S(1)}, bf16[64,640]{1,0:T(8,128)(2,1)S(1)}, u32[]{:S(2)}, u32[]{:S(2)}) %collective-permute-start.14) | collective-permute-done | bytes 81952 | tf_op jit(solution)/shard_map/ppermute | solution.py:419
  112.3 1.7 %collective-permute-done.13.refs_2_ = bf16[64,640]{1,0:T(8,128)(2,1)S(1)} collective-permute-done((bf16[64,640]{1,0:T(8,128)(2,1)S(1)}, bf16[64,640]{1,0:T(8,128)(2,1)S(1)}, u32[]{:S(2)}, u32[]{:S(2)}) %collective-permute-start.13) | collective-permute-done | bytes 81952 | tf_op jit(solution)/shard_map/ppermute | solution.py:419
  114.0 2.1 %collective-permute-done.12.refs_1_ = bf16[64,640]{1,0:T(8,128)(2,1)S(1)} collective-permute-done((bf16[64,640]{1,0:T(8,128)(2,1)S(1)}, bf16[64,640]{1,0:T(8,128)(2,1)S(1)}, u32[]{:S(2)}, u32[]{:S(2)}) %collective-permute-start.12) | collective-permute-done | bytes 81952 | tf_op jit(solution)/shard_map/ppermute | solution.py:419
  116.7 1.7 %assemble.1 = (bf16[256,512]{1,0:T(8,128)(2,1)}, bf16[64,256]{1,0:T(8,128)(2,1)}) custom-call(bf16[64,640]{1,0:T(8,128)(2,1)} %copy-done.1, bf16[64,640]{1,0:T(8,128)(2,1)} %copy-done.10, bf16[64,640]{1,0:T(8,128)(2,1)} %copy-done.9, bf16[64,640]{1,0:T(8,128)(2,1)} %copy-done.8), custom_call_target="tpu_custom_call" | custom-call | flops 1 | bytes 1 | tf_op jit(solution)/shard_map/assemble/pallas_call | solution.py:543
  118.5 6.0 %all-to-all-done.2 = bf16[8,256,512]{2,1,0:T(8,128)(2,1)S(1)} async-done(((bf16[8,256,512]{2,1,0:T(8,128)(2,1)}), bf16[8,256,512]{2,1,0:T(8,128)(2,1)S(1)}, u32[]{:S(2)}, u32[]{:S(2)}) %all-to-all-start.2) | async-done | bytes 2097184 | tf_op jit(solution)/shard_map/all_to_all | solution.py:607
  124.5 1.5 %fusion = (bf16[8,128,512]{2,1,0:T(8,128)(2,1)}, bf16[8,128,512]{2,1,0:T(8,128)(2,1)}) fusion(bf16[8,256,512]{2,1,0:T(8,128)(2,1)S(1)} %all-to-all-done.2), kind=kLoop, calls=%fused_computation.1 | loop fusion | bytes 4194304 | tf_op jit(solution)/shard_map/slice | solution.py:638
  (45 shorter events, 4.8 us)
Async XLA Ops:
  27.4 5.1 %copy-start = (bf16[8,128,640]{2,1,0:T(8,128)(2,1)}, bf16[8,128,640]{2,1,0:T(8,128)(2,1)S(1)}, u32[]{:S(2)}) copy-start(bf16[8,128,640]{2,1,0:T(8,128)(2,1)S(1)} %all_to_all.15) | copy-start | bytes 3932164
  27.4 5.1 %collective-permute-start = (bf16[1024,640]{1,0:T(8,128)(2,1)S(1)}, bf16[1024,640]{1,0:T(8,128)(2,1)S(1)}, u32[]{:S(2)}, u32[]{:S(2)}) collective-permute-start(bf16[1024,640]{1,0:T(8,128)(2,1)S(1)} %bitcast.5), channel_id=1, source_target_pairs={{0,1},{1,0},{2,3},{3,2},{4,5},{5,4},{6,7},{7,6},{8,9},{9,8},{10,11... | collective-permute-start | bytes 3932168 | tf_op jit(solution)/shard_map/ppermute | solution.py:603
  32.5 1.0 copy-start.11
  49.6 8.9 %collective-permute-start.1 = (bf16[12,4,16,640]{3,2,1,0:T(8,128)(2,1)}, bf16[12,4,16,640]{3,2,1,0:T(8,128)(2,1)S(1)}, u32[]{:S(2)}, u32[]{:S(2)}) collective-permute-start(bf16[12,4,16,640]{3,2,1,0:T(8,128)(2,1)} %get-tuple-element.50), channel_id=1, source_target_pairs={{0,1},{1,0},{2,3},{3,2},{4,5},{5,4},{6,7},{7,6},{8,9},{9,8},{10,11... | collective-permute-start | bytes 2949128 | tf_op jit(solution)/shard_map/ppermute | solution.py:603
  50.1 35.6 %all-to-all-start.1 = ((bf16[8,256,512]{2,1,0:T(8,128)(2,1)}), bf16[8,256,512]{2,1,0:T(8,128)(2,1)}, u32[]{:S(2)}, u32[]{:S(2)}) async-start(bf16[8,256,512]{2,1,0:T(8,128)(2,1)} %get-tuple-element.59), calls=%async_computation.1 | async-start | bytes 4194304 | tf_op jit(solution)/shard_map/all_to_all | solution.py:607
  58.5 0.9 copy-start.12
  62.0 8.9 %collective-permute-start.2 = (bf16[12,16,640]{2,1,0:T(8,128)(2,1)}, bf16[12,16,640]{2,1,0:T(8,128)(2,1)S(1)}, u32[]{:S(2)}, u32[]{:S(2)}) collective-permute-start(bf16[12,16,640]{2,1,0:T(8,128)(2,1)} %get-tuple-element.52), channel_id=1, source_target_pairs={{0,4},{2,6},{4,0},{6,2},{1,5},{3,7},{5,1},{7,3},{8,12},{10,14},{12... | collective-permute-start | bytes 737288 | tf_op jit(solution)/shard_map/ppermute | solution.py:419
  64.9 12.0 %collective-permute-start.3 = (bf16[12,16,640]{2,1,0:T(8,128)(2,1)}, bf16[12,16,640]{2,1,0:T(8,128)(2,1)S(1)}, u32[]{:S(2)}, u32[]{:S(2)}) collective-permute-start(bf16[12,16,640]{2,1,0:T(8,128)(2,1)} %get-tuple-element.53), channel_id=1, source_target_pairs={{0,2},{2,4},{4,6},{6,0},{1,3},{3,5},{5,7},{7,1},{8,10},{10,12},{12... | collective-permute-start | bytes 737288 | tf_op jit(solution)/shard_map/ppermute | solution.py:419
  65.3 11.7 %collective-permute-start.4 = (bf16[12,16,640]{2,1,0:T(8,128)(2,1)}, bf16[12,16,640]{2,1,0:T(8,128)(2,1)S(1)}, u32[]{:S(2)}, u32[]{:S(2)}) collective-permute-start(bf16[12,16,640]{2,1,0:T(8,128)(2,1)} %get-tuple-element.54), channel_id=1, source_target_pairs={{0,6},{2,0},{4,2},{6,4},{1,7},{3,1},{5,3},{7,5},{8,14},{10,8},{12,... | collective-permute-start | bytes 737288 | tf_op jit(solution)/shard_map/ppermute | solution.py:419
  70.9 6.0 %copy-start.2 = (bf16[12,16,640]{2,1,0:T(8,128)(2,1)}, bf16[12,16,640]{2,1,0:T(8,128)(2,1)S(1)}, u32[]{:S(2)}) copy-start(bf16[12,16,640]{2,1,0:T(8,128)(2,1)S(1)} %collective-permute-done.2.refs_2_) | copy-start | bytes 737284
  76.9 0.7 copy-start.3
  76.9 0.8 copy-start.4
  79.8 8.6 %collective-permute-start.5 = (bf16[4,16,640]{2,1,0:T(8,128)(2,1)}, bf16[4,16,640]{2,1,0:T(8,128)(2,1)S(1)}, u32[]{:S(2)}, u32[]{:S(2)}) collective-permute-start(bf16[4,16,640]{2,1,0:T(8,128)(2,1)} %get-tuple-element.56), channel_id=1, source_target_pairs={{0,32},{16,48},{32,0},{48,16},{1,33},{17,49},{33,1},{49,17},{2,34}... | collective-permute-start | bytes 245768 | tf_op jit(solution)/shard_map/ppermute | solution.py:419
  82.8 5.7 %collective-permute-start.6 = (bf16[4,16,640]{2,1,0:T(8,128)(2,1)}, bf16[4,16,640]{2,1,0:T(8,128)(2,1)S(1)}, u32[]{:S(2)}, u32[]{:S(2)}) collective-permute-start(bf16[4,16,640]{2,1,0:T(8,128)(2,1)} %get-tuple-element.57), channel_id=1, source_target_pairs={{0,16},{16,32},{32,48},{48,0},{1,17},{17,33},{33,49},{49,1},{2,18}... | collective-permute-start | bytes 245768 | tf_op jit(solution)/shard_map/ppermute | solution.py:419
  83.1 5.4 %collective-permute-start.7 = (bf16[4,16,640]{2,1,0:T(8,128)(2,1)}, bf16[4,16,640]{2,1,0:T(8,128)(2,1)S(1)}, u32[]{:S(2)}, u32[]{:S(2)}) collective-permute-start(bf16[4,16,640]{2,1,0:T(8,128)(2,1)} %get-tuple-element.58), channel_id=1, source_target_pairs={{0,48},{16,0},{32,16},{48,32},{1,49},{17,1},{33,17},{49,33},{2,50}... | collective-permute-start | bytes 245768 | tf_op jit(solution)/shard_map/ppermute | solution.py:419
  88.4 0.6 copy-start.5
  88.5 0.6 copy-start.6
  88.5 0.6 copy-start.7
  90.8 8.1 %collective-permute-start.8 = (bf16[2,16,640]{2,1,0:T(8,128)(2,1)}, bf16[2,16,640]{2,1,0:T(8,128)(2,1)S(1)}, u32[]{:S(2)}, u32[]{:S(2)}) collective-permute-start(bf16[2,16,640]{2,1,0:T(8,128)(2,1)} %get-tuple-element.67.a), channel_id=1, source_target_pairs={{0,8},{8,0},{64,72},{72,64},{1,9},{9,1},{65,73},{73,65},{2,10},{10... | collective-permute-start | bytes 122888 | tf_op jit(solution)/shard_map/ppermute | solution.py:418
  93.3 5.6 %collective-permute-start.10 = (bf16[2,16,640]{2,1,0:T(8,128)(2,1)}, bf16[2,16,640]{2,1,0:T(8,128)(2,1)S(1)}, u32[]{:S(2)}, u32[]{:S(2)}) collective-permute-start(bf16[2,16,640]{2,1,0:T(8,128)(2,1)} %get-tuple-element.68), channel_id=1, source_target_pairs={{0,72},{8,64},{64,8},{72,0},{1,73},{9,65},{65,9},{73,1},{2,74},{10... | collective-permute-start | bytes 122888 | tf_op jit(solution)/shard_map/ppermute | solution.py:418
  94.4 4.5 %collective-permute-start.9 = (bf16[2,16,640]{2,1,0:T(8,128)(2,1)}, bf16[2,16,640]{2,1,0:T(8,128)(2,1)S(1)}, u32[]{:S(2)}, u32[]{:S(2)}) collective-permute-start(bf16[2,16,640]{2,1,0:T(8,128)(2,1)} %get-tuple-element.68), channel_id=1, source_target_pairs={{0,64},{8,72},{64,0},{72,8},{1,65},{9,73},{65,1},{73,9},{2,66},{10... | collective-permute-start | bytes 122888 | tf_op jit(solution)/shard_map/ppermute | solution.py:418
  94.4 30.1 %all-to-all-start.2 = ((bf16[8,256,512]{2,1,0:T(8,128)(2,1)}), bf16[8,256,512]{2,1,0:T(8,128)(2,1)S(1)}, u32[]{:S(2)}, u32[]{:S(2)}) async-start(bf16[8,256,512]{2,1,0:T(8,128)(2,1)} %total.1), calls=%async_computation.2 | async-start | bytes 4194304 | tf_op jit(solution)/shard_map/all_to_all | solution.py:607
  98.9 0.6 copy-start.13
  98.9 0.6 copy-start.14
  101.4 4.3 %collective-permute-start.11 = (bf16[32,640]{1,0:T(8,128)(2,1)}, bf16[32,640]{1,0:T(8,128)(2,1)S(1)}, u32[]{:S(2)}, u32[]{:S(2)}) collective-permute-start(bf16[32,640]{1,0:T(8,128)(2,1)} %finish.1), channel_id=1, source_target_pairs={{0,1},{1,0},{2,3},{3,2},{4,5},{5,4},{6,7},{7,6},{8,9},{9,8},{10,11... | collective-permute-start | bytes 122888 | tf_op jit(solution)/shard_map/ppermute | solution.py:603
  106.5 9.6 %copy-start.1 = (bf16[64,640]{1,0:T(8,128)(2,1)}, bf16[64,640]{1,0:T(8,128)(2,1)S(1)}, u32[]{:S(2)}) copy-start(bf16[64,640]{1,0:T(8,128)(2,1)S(1)} %pad_maximum_fusion.refs_0_) | copy-start | bytes 245764
  106.5 5.8 %collective-permute-start.14 = (bf16[64,640]{1,0:T(8,128)(2,1)S(1)}, bf16[64,640]{1,0:T(8,128)(2,1)S(1)}, u32[]{:S(2)}, u32[]{:S(2)}) collective-permute-start(bf16[64,640]{1,0:T(8,128)(2,1)S(1)} %pad_maximum_fusion.refs_0_), channel_id=1, source_target_pairs={{0,6},{2,0},{4,2},{6,4},{1,7},{3,1},{5,3},{7,5},{8,14},{10,8},{12,... | collective-permute-start | bytes 245768 | tf_op jit(solution)/shard_map/ppermute | solution.py:419
  108.9 5.1 %collective-permute-start.13 = (bf16[64,640]{1,0:T(8,128)(2,1)S(1)}, bf16[64,640]{1,0:T(8,128)(2,1)S(1)}, u32[]{:S(2)}, u32[]{:S(2)}) collective-permute-start(bf16[64,640]{1,0:T(8,128)(2,1)S(1)} %pad_maximum_fusion.refs_0_), channel_id=1, source_target_pairs={{0,4},{2,6},{4,0},{6,2},{1,5},{3,7},{5,1},{7,3},{8,12},{10,14},{12... | collective-permute-start | bytes 245768 | tf_op jit(solution)/shard_map/ppermute | solution.py:419
  109.5 6.6 %collective-permute-start.12 = (bf16[64,640]{1,0:T(8,128)(2,1)S(1)}, bf16[64,640]{1,0:T(8,128)(2,1)S(1)}, u32[]{:S(2)}, u32[]{:S(2)}) collective-permute-start(bf16[64,640]{1,0:T(8,128)(2,1)S(1)} %pad_maximum_fusion.refs_0_), channel_id=1, source_target_pairs={{0,2},{2,4},{4,6},{6,0},{1,3},{3,5},{5,7},{7,1},{8,10},{10,12},{12... | collective-permute-start | bytes 245768 | tf_op jit(solution)/shard_map/ppermute | solution.py:419
  112.3 3.8 %copy-start.8 = (bf16[64,640]{1,0:T(8,128)(2,1)}, bf16[64,640]{1,0:T(8,128)(2,1)S(1)}, u32[]{:S(2)}) copy-start(bf16[64,640]{1,0:T(8,128)(2,1)S(1)} %collective-permute-done.14.refs_3_) | copy-start | bytes 245764
  114.0 2.1 %copy-start.9 = (bf16[64,640]{1,0:T(8,128)(2,1)}, bf16[64,640]{1,0:T(8,128)(2,1)S(1)}, u32[]{:S(2)}) copy-start(bf16[64,640]{1,0:T(8,128)(2,1)S(1)} %collective-permute-done.13.refs_2_) | copy-start | bytes 245764
  116.1 0.6 copy-start.10
  (1 other events, 0.6 us)

commit v4 on v3

--- a/solution.py
+++ b/solution.py
@@ -22,6 +22,7 @@
 BLOCK = 16
 TILE = 256
 MAX_TILES = 6
+HEADS = 4
 SLOTS = 12
 WIDE = (3, 4)
 LONG = pl.CostEstimate(flops=100000000000, bytes_accessed=1, transcendentals=0)
@@ -109,7 +110,7 @@
         return lax.fori_loop(0, tiles, body, carry)
 
     row_weight = weight[...]
-    for h in range(2):
+    for h in range(HEADS):
         nope = qn[:, h * D_NOPE : (h + 1) * D_NOPE]
         rope = qr[:, h * D_ROPE : (h + 1) * D_ROPE]
         qf[h] = jnp.concatenate([nope, rope, bias[...]], axis=1)
@@ -128,11 +129,11 @@
         acc[D_LAT:, cols] += rope_grads
 
     def finish_heads(dq, grad):
-        for h in range(2):
+        for h in range(HEADS):
             dqn[:, h * D_NOPE : (h + 1) * D_NOPE] = dq[h][:, :D_NOPE].astype(BF)
             dw[h] = grad[h * 256 : (h + 1) * 256].astype(BF)
         dqr[...] = jnp.concatenate(
-            [dq[h][:, D_NOPE : D_NOPE + D_ROPE] for h in range(2)], axis=1
+            [dq[h][:, D_NOPE : D_NOPE + D_ROPE] for h in range(HEADS)], axis=1
         ).astype(BF)
 
     def wide_step(count):
@@ -142,7 +143,7 @@
         shown = lax.broadcasted_iota(jnp.int32, (ROWS, TILE), 1) <= lax.broadcasted_iota(
             jnp.int32, (ROWS, TILE), 0
         )
-        heads = range(2)
+        heads = range(HEADS)
         parts, rope_sum, dq = [], None, []
         k_fulls = [jnp.concatenate([both[:, h * 256 : h * 256 + 128], all_keys[:, D_LAT:]], axis=1) for h in heads]
         values = [both[:, h * 256 + 128 : (h + 1) * 256] for h in heads]
@@ -165,7 +166,7 @@
         dq = [dot(dss[h], k_fulls[h]) for h in heads]
         for h in heads:
             parts += [dks[h][:D_NOPE].astype(BF), dvs[h].astype(BF)]
-        rope_sum = dks[0][D_NOPE:] + dks[1][D_NOPE:]
+        rope_sum = sum([x[D_NOPE:] for x in dks[1:]], dks[0][D_NOPE:])
         dkv = jnp.concatenate(parts, axis=0)
         add_grads(slice(0, width), dot(wt[...], dkv), rope_sum)
         finish_heads(dq, dot(dkv, all_keys[:, :D_LAT]))
@@ -179,7 +180,7 @@
             both = dot_nt(tile_keys[:, :D_LAT], wb[...]).astype(BF)
             shown = col <= row + t * (MAX_TILES * TILE)
             new = []
-            for h in range(2):
+            for h in range(HEADS):
                 k_nope = both[:, h * 256 : h * 256 + 128]
                 value = both[:, h * 256 + 128 : (h + 1) * 256]
                 k_full = jnp.concatenate([k_nope, tile_keys[:, D_LAT:]], axis=1)
@@ -192,12 +193,12 @@
             return tuple(new)
 
         low = jnp.full((ROWS, 128), HIDE, F32)
-        maxima = each_tile(score_tile, (low, low))
+        maxima = each_tile(score_tile, (low,) * HEADS)
         shifts = [jnp.max(m, axis=1, keepdims=True) * base2 for m in maxima]
 
         def prob_tile(t, carry):
             new = []
-            for h in range(2):
+            for h in range(HEADS):
                 total, mixed = carry[h]
                 expo = jnp.exp2(s[h, t] * base2 - shifts[h])
                 total = total + (expo[:, :128] + expo[:, 128:])
@@ -207,9 +208,9 @@
             return tuple(new)
 
         nothing = jnp.zeros((ROWS, 128), F32)
-        mixes = each_tile(prob_tile, ((nothing, nothing), (nothing, nothing)))
+        mixes = each_tile(prob_tile, ((nothing, nothing),) * HEADS)
         slopes, offsets = [], []
-        for h in range(2):
+        for h in range(HEADS):
             total, mixed = mixes[h]
             inv = 1.0 / jnp.sum(total, axis=1, keepdims=True)
             mixed = mixed * inv
@@ -225,7 +226,7 @@
         def back_tile(t, carry):
             tile_keys = keys[key_rows(t), :D_LAT]
             parts, rope_sum, new = [], None, []
-            for h in range(2):
+            for h in range(HEADS):
                 expo = e[h, t]
                 ds = (expo.astype(F32) * (dp[h, t] * slopes[h] - offsets[h])).astype(BF)
                 new.append(carry[h] + dot(ds, kf[h, t]))
@@ -239,7 +240,7 @@
             return tuple(new)
 
         empty = jnp.zeros((ROWS, 256), F32)
-        dq = each_tile(back_tile, (empty, empty))
+        dq = each_tile(back_tile, (empty,) * HEADS)
         finish_heads(dq, wgrad[...])
 
     for count in WIDE:
@@ -292,7 +293,7 @@
 
 def attention(shared, q_nope, q_rope, d_out, w_uk, w_uv):
     rows = q_nope.shape[0]
-    pairs = w_uk.shape[0] // (2 * D_NOPE)
+    pairs = w_uk.shape[0] // (HEADS * D_NOPE)
 
     def columns(size):
         return pl.BlockSpec((rows, size), lambda i: (0, i))
@@ -302,17 +303,17 @@
 
     whole = pl.BlockSpec(memory_space=pltpu.VMEM)
     in_specs = [pl.BlockSpec(memory_space=pltpu.SMEM)] + [whole] * 5
-    in_specs += [columns(256), columns(128), columns(256), heads(256), heads(256)]
+    in_specs += [columns(HEADS * D_NOPE), columns(HEADS * D_ROPE), columns(HEADS * D_V), heads(HEADS * D_NOPE), heads(HEADS * D_V)]
     half = jax.ShapeDtypeStruct((SLOTS, 4, BLOCK, PACK), BF)
     return pl.pallas_call(
         attention_kernel,
         grid=(pairs,),
         in_specs=in_specs,
         out_specs=[
-            columns(256),
-            columns(256),
-            columns(128),
-            pl.BlockSpec((2, 256, D_LAT), lambda i: (i, 0, 0)),
+            columns(HEADS * D_V),
+            columns(HEADS * D_NOPE),
+            columns(HEADS * D_ROPE),
+            pl.BlockSpec((HEADS, 256, D_LAT), lambda i: (i, 0, 0)),
             whole,
             whole,
             pl.BlockSpec(memory_space=pltpu.SMEM),
@@ -321,7 +322,7 @@
             jax.ShapeDtypeStruct(q_nope.shape, BF),
             jax.ShapeDtypeStruct(q_nope.shape, BF),
             jax.ShapeDtypeStruct(q_rope.shape, BF),
-            jax.ShapeDtypeStruct((2 * pairs, 256, D_LAT), BF),
+            jax.ShapeDtypeStruct((HEADS * pairs, 256, D_LAT), BF),
             half,
             half,
             jax.ShapeDtypeStruct((8,), jnp.int32),
@@ -329,22 +330,22 @@
         scratch_shapes=[
             pltpu.VMEM((MAX_TILES * TILE, PACK), BF),
             pltpu.VMEM((D_LAT + D_ROPE, MAX_TILES * TILE), F32),
-            pltpu.VMEM((2, MAX_TILES, TILE, 256), BF),
-            pltpu.VMEM((2, MAX_TILES, TILE, D_V), BF),
-            pltpu.VMEM((2, MAX_TILES, ROWS, TILE), F32),
-            pltpu.VMEM((2, MAX_TILES, ROWS, TILE), F32),
-            pltpu.VMEM((2, MAX_TILES, ROWS, TILE), BF),
-            pltpu.VMEM((2, ROWS, 256), BF),
-            pltpu.VMEM((2, D_NOPE + D_ROPE, ROWS), BF),
-            pltpu.VMEM((2, ROWS, D_V), BF),
-            pltpu.VMEM((2, D_V, ROWS), BF),
-            pltpu.VMEM((512, D_LAT), BF),
-            pltpu.VMEM((D_LAT, 512), BF),
-            pltpu.VMEM((512, D_LAT), F32),
+            pltpu.VMEM((HEADS, MAX_TILES, TILE, 256), BF),
+            pltpu.VMEM((HEADS, MAX_TILES, TILE, D_V), BF),
+            pltpu.VMEM((HEADS, MAX_TILES, ROWS, TILE), F32),
+            pltpu.VMEM((HEADS, MAX_TILES, ROWS, TILE), F32),
+            pltpu.VMEM((HEADS, MAX_TILES, ROWS, TILE), BF),
+            pltpu.VMEM((HEADS, ROWS, 256), BF),
+            pltpu.VMEM((HEADS, D_NOPE + D_ROPE, ROWS), BF),
+            pltpu.VMEM((HEADS, ROWS, D_V), BF),
+            pltpu.VMEM((HEADS, D_V, ROWS), BF),
+            pltpu.VMEM((HEADS * 256, D_LAT), BF),
+            pltpu.VMEM((D_LAT, HEADS * 256), BF),
+            pltpu.VMEM((HEADS * 256, D_LAT), F32),
         ],
         compiler_params=pltpu.CompilerParams(vmem_limit_bytes=56 << 20),
         cost_estimate=pl.CostEstimate(
-            flops=pairs * 2600000000, bytes_accessed=16 << 20, transcendentals=pairs * 400000
+            flops=pairs * HEADS * 1300000000, bytes_accessed=16 << 20, transcendentals=pairs * 400000
         ),
         name="attention",
     )(*shared, q_nope, q_rope, d_out, w_uk, w_uv)
@@ -464,14 +465,6 @@
         out[...] = spread[distance]
 
 
-def fold_x_kernel(*refs):
-    parts, outs = refs[:4], refs[4:]
-    for distance, out in enumerate(outs):
-        place = lax.axis_index("xl") ^ distance
-        for xh in range(2):
-            out[xh] = summed(parts, (place * 2 + xh,))
-
-
 def fold(kernel, operands, cuts, shape, scratch=()):
     vector = pl.BlockSpec(memory_space=LOCAL)
     scalar = pl.BlockSpec(memory_space=pltpu.SMEM)
@@ -494,14 +487,15 @@
     cut = fold(fold_z_kernel, [meta] + parts, 4, (4, BLOCK, PACK), [spread])
     parts = [cut[0]] + [move(cut[d], "z", d) for d in (2, 1, 3)]
     parts, total = lax.optimization_barrier((parts, total))
-    cut = fold(fold_x_kernel, parts, 2, (2, BLOCK, PACK))
-    cut, total = lax.optimization_barrier((cut, total))
-    return total, [cut[0], move(cut[0], "x", 1), move(cut[1], "x", 2), move(cut[1], "x", 3)]
+    part = sum([x.astype(F32) for x in parts[1:]], parts[0].astype(F32)).astype(BF)
+    part, total = lax.optimization_barrier((part, total))
+    return total, [part] + [move(part, "x", d) for d in (1, 2, 3)]
 
 
 def finish_kernel(a, b, c, d, latent, inverse, gain, out):
     head = lax.axis_index("y") * 2 + lax.axis_index("core")
-    total = sum([part[...].astype(F32) for part in (b, c, d)], a[...].astype(F32))
+    blocks = pl.ds(lax.axis_index("xl") * 2, 2)
+    total = sum([part[blocks].astype(F32) for part in (b, c, d)], a[blocks].astype(F32))
     total = total.reshape(2 * BLOCK, PACK)
     lifted = total[:, :D_LAT] * gain[...].astype(F32)[None, :]
     places = [pl.ds(pl.multiple_of((xh * 8 + head) * BLOCK, BLOCK), BLOCK) for xh in range(2)]

time: 127 us -> 122 us (0.961)
  Pallas kernels: 31.5 us -> 28.8 us
  starting transfers between devices: 36.9 us -> 34.5 us
    all_to_all x2, starting transfers between devices: 12.9 us -> 10.4 us  [exchange(): return lax.all_to_all(x, axes, 0, 0, tiled=True)]
    pallas_call x3 -> x2, Pallas kernels: 6.3 us -> 4.62 us  [fold(): pl.pallas_call(kernel, in_specs=[scalar if x.dtype == jnp.int32 else vect...]
    unnamed x32 -> x30, local copies, waits for them, and re-layouts: 4.67 us -> 4.07 us
  transfers between devices with their start and end apart: 17 -> 17, of which waited for: 9 -> 10; matrix products, arithmetic and copies ran while one was open for 1% -> 1% of each run, Pallas kernels for 9% -> 9%
where the time goes in v4:
time: 122 us; the launch traced here: 121 us
  starting transfers between devices  34.5 us (28%)
  Pallas kernels  28.8 us (24%)
  waiting for transfers between devices  26.2 us (21%)
  blocking collectives  23.9 us (20%)
  local copies, waits for them, and re-layouts  5.6 us (5%)
    all_to_all x1, blocking collectives, exchange(): return lax.all_to_all(x, axes, 0, 0, tiled=True)  23.9 us
    ppermute x9, waiting for transfers between devices, move(): return lax.ppermute(x, axis, [(i, (i + distance) % 4) for i in range(4)])  15.9 us
    pallas_call x1, Pallas kernels, attention(): pl.pallas_call(attention_kernel, grid=(pairs,), in_specs=in_specs, out_sp...  15 us
    ppermute x9, starting transfers between devices, move(): return lax.ppermute(x, axis, [(i, (i + distance) % 4) for i in range(4)])  14.4 us
    all_to_all x2, starting transfers between devices, exchange(): return lax.all_to_all(x, axes, 0, 0, tiled=True)  10.4 us
    all_to_all x2, waiting for transfers between devices, exchange(): return lax.all_to_all(x, axes, 0, 0, tiled=True)  6.45 us
    ppermute x3, starting transfers between devices, swap_core(): return lax.ppermute(x, 'core', [(0, 1), (1, 0)])  5.74 us
    pallas_call x2, Pallas kernels, fold(): pl.pallas_call(kernel, in_specs=[scalar if x.dtype == jnp.int32 else vect...  4.62 us
  transfers between devices with their start and end apart: 17, of which 10 were waited for; matrix products, arithmetic and copies ran while one was open for 1% of the time, Pallas kernels for 9%

profile of v4, /device:TPU:1, one launch (start us, length us, event | category | flops | bytes accessed | tf_op | source)
XLA Modules:
  0.0 120.7 jit_solution(18016616003203347831)
XLA Ops:
  0.6 2.8 %prepare.1 = (bf16[256,640]{1,0:T(8,128)(2,1)}, bf16[8,128,640]{2,1,0:T(8,128)(2,1)}, bf16[256,64]{1,0:T(8,128)(2,1)}, f32[256,1]{1,0:T(8,128)}, f32[256,1]{1,0:T(8,128)}, /*index=5*/s32[8]{0:T(128)}) custom-call(bf16[256,512]{1,0:T(8,128)(2,1)} %latent.3, bf16[512]{0:T(512)(128)(2,1)} %gain.3, bf16[64,256]{1,0:T(8,128)(2,1)} %rope_t.1, s32[1,256]{1,0:T(1,128)} %bitcast.9, ...), custom_call_target="tpu_custom_call" | custom-call | flops 1 | bytes 1 | tf_op jit(solution)/shard_map/prepare/pallas_call | solution.py:390
  3.4 23.9 %all_to_all.15 = bf16[8,128,640]{2,1,0:T(8,128)(2,1)S(1)} all-to-all(bf16[8,128,640]{2,1,0:T(8,128)(2,1)} %get-tuple-element.39), channel_id=1, replica_groups=mesh['xl'=2,'z'=4,'xh'=2,'y'=4,'core'=2] {'xl','z'}, dimensions={0} | all-to-all | bytes 2621440 | tf_op jit(solution)/shard_map/all_to_all | solution.py:601
  27.4 2.5 %collective-permute-start = (bf16[1024,640]{1,0:T(8,128)(2,1)S(1)}, bf16[1024,640]{1,0:T(8,128)(2,1)S(1)}, u32[]{:S(2)}, u32[]{:S(2)}) collective-permute-start(bf16[1024,640]{1,0:T(8,128)(2,1)S(1)} %bitcast.5), channel_id=1, source_target_pairs={{0,1},{1,0},{2,3},{3,2},{4,5},{5,4},{6,7},{7,6},{8,9},{9,8},{10,11... | collective-permute-start | bytes 3932168 | tf_op jit(solution)/shard_map/ppermute | solution.py:597
  29.8 2.7 %collective-permute-done.refs_3_ = bf16[1024,640]{1,0:T(8,128)(2,1)S(1)} collective-permute-done((bf16[1024,640]{1,0:T(8,128)(2,1)S(1)}, bf16[1024,640]{1,0:T(8,128)(2,1)S(1)}, u32[]{:S(2)}, u32[]{:S(2)}) %collective-permute-start) | collective-permute-done | bytes 1310752 | tf_op jit(solution)/shard_map/ppermute | solution.py:597
  32.5 1.0 copy-done.10
  33.5 15.0 %attention.1 = (bf16[256,1024]{1,0:T(8,128)(2,1)}, bf16[256,1024]{1,0:T(8,128)(2,1)}, bf16[256,512]{1,0:T(8,128)(2,1)}, bf16[8,256,512]{2,1,0:T(8,128)(2,1)}, bf...) custom-call(s32[8]{0:T(128)} %get-tuple-element.37.refs_0_, ...), custom_call_target="tpu_custom_call" | custom-call | flops 10400000000 | bytes 16777216 | tf_op jit(solution)/shard_map/attention/pallas_call | solution.py:308
  48.9 6.8 %all-to-all-start.1 = ((bf16[8,256,512]{2,1,0:T(8,128)(2,1)}), bf16[8,256,512]{2,1,0:T(8,128)(2,1)}, u32[]{:S(2)}, u32[]{:S(2)}) async-start(bf16[8,256,512]{2,1,0:T(8,128)(2,1)} %get-tuple-element.56), calls=%async_computation.1 | async-start | bytes 4194304 | tf_op jit(solution)/shard_map/all_to_all | solution.py:601
  55.8 0.9 copy-done.11
  56.7 2.5 %fold.2 = (bf16[12,16,640]{2,1,0:T(8,128)(2,1)}, bf16[12,16,640]{2,1,0:T(8,128)(2,1)}, bf16[12,16,640]{2,1,0:T(8,128)(2,1)}, bf16[12,16,640]{2,1,0:T(8,128)(2,1)}) custom-call(bf16[12,4,16,640]{3,2,1,0:T(8,128)(2,1)} %get-tuple-element.46.refs_0_, bf16[12,4,16,640]{3,2,1,0:T(8,128)(2,1)} %copy-done.11), custom_call_target="tpu_custom_call" | custom-call | flops 99999997952 | bytes 1 | tf_op jit(solution)/shard_map/fold/pallas_call | solution.py:471
  59.2 2.9 %collective-permute-start.2 = (bf16[12,16,640]{2,1,0:T(8,128)(2,1)}, bf16[12,16,640]{2,1,0:T(8,128)(2,1)S(1)}, u32[]{:S(2)}, u32[]{:S(2)}) collective-permute-start(bf16[12,16,640]{2,1,0:T(8,128)(2,1)} %get-tuple-element.49), channel_id=1, source_target_pairs={{0,4},{2,6},{4,0},{6,2},{1,5},{3,7},{5,1},{7,3},{8,12},{10,14},{12... | collective-permute-start | bytes 737288 | tf_op jit(solution)/shard_map/ppermute | solution.py:420
  62.5 2.3 %collective-permute-start.4 = (bf16[12,16,640]{2,1,0:T(8,128)(2,1)}, bf16[12,16,640]{2,1,0:T(8,128)(2,1)S(1)}, u32[]{:S(2)}, u32[]{:S(2)}) collective-permute-start(bf16[12,16,640]{2,1,0:T(8,128)(2,1)} %get-tuple-element.51), channel_id=1, source_target_pairs={{0,6},{2,0},{4,2},{6,4},{1,7},{3,1},{5,3},{7,5},{8,14},{10,8},{12,... | collective-permute-start | bytes 737288 | tf_op jit(solution)/shard_map/ppermute | solution.py:420
  64.8 3.3 %collective-permute-done.2.refs_2_ = bf16[12,16,640]{2,1,0:T(8,128)(2,1)S(1)} collective-permute-done((bf16[12,16,640]{2,1,0:T(8,128)(2,1)}, bf16[12,16,640]{2,1,0:T(8,128)(2,1)S(1)}, u32[]{:S(2)}, u32[]{:S(2)}) %collective-permute-start.2) | collective-permute-done | bytes 245792 | tf_op jit(solution)/shard_map/ppermute | solution.py:420
  68.2 6.0 %collective-permute-done.3.refs_3_ = bf16[12,16,640]{2,1,0:T(8,128)(2,1)S(1)} collective-permute-done((bf16[12,16,640]{2,1,0:T(8,128)(2,1)}, bf16[12,16,640]{2,1,0:T(8,128)(2,1)S(1)}, u32[]{:S(2)}, u32[]{:S(2)}) %collective-permute-start.3) | collective-permute-done | bytes 245792 | tf_op jit(solution)/shard_map/ppermute | solution.py:420
  74.2 0.7 copy-done.3
  75.0 2.1 %fold.3 = (bf16[4,16,640]{2,1,0:T(8,128)(2,1)}, bf16[4,16,640]{2,1,0:T(8,128)(2,1)}, bf16[4,16,640]{2,1,0:T(8,128)(2,1)}, bf16[4,16,640]{2,1,0:T(8,128)(2,1)}) custom-call(s32[8]{0:T(128)} %get-tuple-element.45.refs_0_, bf16[12,16,640]{2,1,0:T(8,128)(2,1)} %get-tuple-element.48.refs_1_, bf16[12,16,640]{2,1,0:T(8,128)(2,1)} %copy-done.2, ...), custom_call_target="tpu_custom_call" | custom-call | flops 1 | bytes 1 | tf_op jit(solution)/shard_map/fold/pallas_call | solution.py:471
  77.1 2.9 %collective-permute-start.5 = (bf16[4,16,640]{2,1,0:T(8,128)(2,1)}, bf16[4,16,640]{2,1,0:T(8,128)(2,1)S(1)}, u32[]{:S(2)}, u32[]{:S(2)}) collective-permute-start(bf16[4,16,640]{2,1,0:T(8,128)(2,1)} %get-tuple-element.53), channel_id=1, source_target_pairs={{0,32},{16,48},{32,0},{48,16},{1,33},{17,49},{33,1},{49,17},{2,34}... | collective-permute-start | bytes 245768 | tf_op jit(solution)/shard_map/ppermute | solution.py:420
  80.4 2.3 %collective-permute-start.7 = (bf16[4,16,640]{2,1,0:T(8,128)(2,1)}, bf16[4,16,640]{2,1,0:T(8,128)(2,1)S(1)}, u32[]{:S(2)}, u32[]{:S(2)}) collective-permute-start(bf16[4,16,640]{2,1,0:T(8,128)(2,1)} %get-tuple-element.55), channel_id=1, source_target_pairs={{0,48},{16,0},{32,16},{48,32},{1,49},{17,1},{33,17},{49,33},{2,50}... | collective-permute-start | bytes 245768 | tf_op jit(solution)/shard_map/ppermute | solution.py:420
  82.9 2.8 %total.1 = bf16[8,256,512]{2,1,0:T(8,128)(2,1)} custom-call(bf16[8,256,512]{2,1,0:T(8,128)(2,1)} %all-to-all-done.1.pieces), custom_call_target="tpu_custom_call" | custom-call | flops 1 | bytes 1 | tf_op jit(solution)/shard_map/total/pallas_call | solution.py:579
  85.8 2.5 %collective-permute-start.10 = (bf16[4,16,640]{2,1,0:T(8,128)(2,1)S(1)}, bf16[4,16,640]{2,1,0:T(8,128)(2,1)S(1)}, u32[]{:S(2)}, u32[]{:S(2)}) collective-permute-start(bf16[4,16,640]{2,1,0:T(8,128)(2,1)S(1)} %add_convert_fusion.a), channel_id=1, source_target_pairs={{0,72},{8,64},{64,8},{72,0},{1,73},{9,65},{65,9},{73,1},{2,74},{10... | collective-permute-start | bytes 245768 | tf_op jit(solution)/shard_map/ppermute | solution.py:419
  88.3 1.4 %collective-permute-start.8 = (bf16[4,16,640]{2,1,0:T(8,128)(2,1)S(1)}, bf16[4,16,640]{2,1,0:T(8,128)(2,1)S(1)}, u32[]{:S(2)}, u32[]{:S(2)}) collective-permute-start(bf16[4,16,640]{2,1,0:T(8,128)(2,1)S(1)} %add_convert_fusion.a), channel_id=1, source_target_pairs={{0,8},{8,0},{64,72},{72,64},{1,9},{9,1},{65,73},{73,65},{2,10},{10... | collective-permute-start | bytes 245768 | tf_op jit(solution)/shard_map/ppermute | solution.py:419
  89.8 3.6 %all-to-all-start.2 = ((bf16[8,256,512]{2,1,0:T(8,128)(2,1)}), bf16[8,256,512]{2,1,0:T(8,128)(2,1)S(1)}, u32[]{:S(2)}, u32[]{:S(2)}) async-start(bf16[8,256,512]{2,1,0:T(8,128)(2,1)} %total.1), calls=%async_computation.2 | async-start | bytes 4194304 | tf_op jit(solution)/shard_map/all_to_all | solution.py:601
  94.1 1.9 %finish.1 = bf16[32,640]{1,0:T(8,128)(2,1)} custom-call(bf16[4,16,640]{2,1,0:T(8,128)(2,1)} %copy-done.9, bf16[4,16,640]{2,1,0:T(8,128)(2,1)} %copy-done.14, bf16[4,16,640]{2,1,0:T(8,128)(2,1)} %copy-done.13, bf16[4,16,640]{2,1,0:T(8,128)(2,1)} %copy-done.12, bf16[256,512]{1,0:T(8,128)(2,1)} %latent.3, f32[256,1]{1,0:T(8,128)} %get-tuple-element.63.inverse, ...), custom_call_target="tpu_custom_call" | custom-call | flops 99999997952 | bytes 1 | tf_op jit(solution)/shard_map/finish/pallas_call | solution.py:511
  96.1 2.8 %collective-permute-start.11 = (bf16[32,640]{1,0:T(8,128)(2,1)}, bf16[32,640]{1,0:T(8,128)(2,1)S(1)}, u32[]{:S(2)}, u32[]{:S(2)}) collective-permute-start(bf16[32,640]{1,0:T(8,128)(2,1)} %finish.1), channel_id=1, source_target_pairs={{0,1},{1,0},{2,3},{3,2},{4,5},{5,4},{6,7},{7,6},{8,9},{9,8},{10,11... | collective-permute-start | bytes 122888 | tf_op jit(solution)/shard_map/ppermute | solution.py:597
  98.9 1.1 collective-permute-done.11
  100.0 0.8 pad_maximum_fusion.refs_0_
  100.8 2.5 %collective-permute-start.14 = (bf16[64,640]{1,0:T(8,128)(2,1)S(1)}, bf16[64,640]{1,0:T(8,128)(2,1)S(1)}, u32[]{:S(2)}, u32[]{:S(2)}) collective-permute-start(bf16[64,640]{1,0:T(8,128)(2,1)S(1)} %pad_maximum_fusion.refs_0_), channel_id=1, source_target_pairs={{0,6},{2,0},{4,2},{6,4},{1,7},{3,1},{5,3},{7,5},{8,14},{10,8},{12,... | collective-permute-start | bytes 245768 | tf_op jit(solution)/shard_map/ppermute | solution.py:420
  104.0 2.7 %collective-permute-done.14.refs_3_ = bf16[64,640]{1,0:T(8,128)(2,1)S(1)} collective-permute-done((bf16[64,640]{1,0:T(8,128)(2,1)S(1)}, bf16[64,640]{1,0:T(8,128)(2,1)S(1)}, u32[]{:S(2)}, u32[]{:S(2)}) %collective-permute-start.14) | collective-permute-done | bytes 81952 | tf_op jit(solution)/shard_map/ppermute | solution.py:420
  106.7 1.7 %collective-permute-done.13.refs_2_ = bf16[64,640]{1,0:T(8,128)(2,1)S(1)} collective-permute-done((bf16[64,640]{1,0:T(8,128)(2,1)S(1)}, bf16[64,640]{1,0:T(8,128)(2,1)S(1)}, u32[]{:S(2)}, u32[]{:S(2)}) %collective-permute-start.13) | collective-permute-done | bytes 81952 | tf_op jit(solution)/shard_map/ppermute | solution.py:420
  108.4 2.1 %collective-permute-done.12.refs_1_ = bf16[64,640]{1,0:T(8,128)(2,1)S(1)} collective-permute-done((bf16[64,640]{1,0:T(8,128)(2,1)S(1)}, bf16[64,640]{1,0:T(8,128)(2,1)S(1)}, u32[]{:S(2)}, u32[]{:S(2)}) %collective-permute-start.12) | collective-permute-done | bytes 81952 | tf_op jit(solution)/shard_map/ppermute | solution.py:420
  111.2 1.7 %assemble.1 = (bf16[256,512]{1,0:T(8,128)(2,1)}, bf16[64,256]{1,0:T(8,128)(2,1)}) custom-call(bf16[64,640]{1,0:T(8,128)(2,1)} %copy-done.1, bf16[64,640]{1,0:T(8,128)(2,1)} %copy-done.7, bf16[64,640]{1,0:T(8,128)(2,1)} %copy-done.6, bf16[64,640]{1,0:T(8,128)(2,1)} %copy-done.5), custom_call_target="tpu_custom_call" | custom-call | flops 1 | bytes 1 | tf_op jit(solution)/shard_map/assemble/pallas_call | solution.py:537
  112.9 6.2 %all-to-all-done.2 = bf16[8,256,512]{2,1,0:T(8,128)(2,1)S(1)} async-done(((bf16[8,256,512]{2,1,0:T(8,128)(2,1)}), bf16[8,256,512]{2,1,0:T(8,128)(2,1)S(1)}, u32[]{:S(2)}, u32[]{:S(2)}) %all-to-all-start.2) | async-done | bytes 2097184 | tf_op jit(solution)/shard_map/all_to_all | solution.py:601
  119.1 1.5 %fusion = (bf16[8,128,512]{2,1,0:T(8,128)(2,1)}, bf16[8,128,512]{2,1,0:T(8,128)(2,1)}) fusion(bf16[8,256,512]{2,1,0:T(8,128)(2,1)S(1)} %all-to-all-done.2), kind=kLoop, calls=%fused_computation.2 | loop fusion | bytes 4194304 | tf_op jit(solution)/shard_map/slice | solution.py:632
  (43 shorter events, 3.7 us)
Async XLA Ops:
  27.4 5.1 %copy-start = (bf16[8,128,640]{2,1,0:T(8,128)(2,1)}, bf16[8,128,640]{2,1,0:T(8,128)(2,1)S(1)}, u32[]{:S(2)}) copy-start(bf16[8,128,640]{2,1,0:T(8,128)(2,1)S(1)} %all_to_all.15) | copy-start | bytes 3932164
  27.4 5.1 %collective-permute-start = (bf16[1024,640]{1,0:T(8,128)(2,1)S(1)}, bf16[1024,640]{1,0:T(8,128)(2,1)S(1)}, u32[]{:S(2)}, u32[]{:S(2)}) collective-permute-start(bf16[1024,640]{1,0:T(8,128)(2,1)S(1)} %bitcast.5), channel_id=1, source_target_pairs={{0,1},{1,0},{2,3},{3,2},{4,5},{5,4},{6,7},{7,6},{8,9},{9,8},{10,11... | collective-permute-start | bytes 3932168 | tf_op jit(solution)/shard_map/ppermute | solution.py:597
  32.5 1.0 copy-start.10
  48.5 7.3 %collective-permute-start.1 = (bf16[12,4,16,640]{3,2,1,0:T(8,128)(2,1)}, bf16[12,4,16,640]{3,2,1,0:T(8,128)(2,1)S(1)}, u32[]{:S(2)}, u32[]{:S(2)}) collective-permute-start(bf16[12,4,16,640]{3,2,1,0:T(8,128)(2,1)} %get-tuple-element.47), channel_id=1, source_target_pairs={{0,1},{1,0},{2,3},{3,2},{4,5},{5,4},{6,7},{7,6},{8,9},{9,8},{10,11... | collective-permute-start | bytes 2949128 | tf_op jit(solution)/shard_map/ppermute | solution.py:597
  48.9 34.0 %all-to-all-start.1 = ((bf16[8,256,512]{2,1,0:T(8,128)(2,1)}), bf16[8,256,512]{2,1,0:T(8,128)(2,1)}, u32[]{:S(2)}, u32[]{:S(2)}) async-start(bf16[8,256,512]{2,1,0:T(8,128)(2,1)} %get-tuple-element.56), calls=%async_computation.1 | async-start | bytes 4194304 | tf_op jit(solution)/shard_map/all_to_all | solution.py:601
  55.8 0.9 copy-start.11
  59.2 8.9 %collective-permute-start.2 = (bf16[12,16,640]{2,1,0:T(8,128)(2,1)}, bf16[12,16,640]{2,1,0:T(8,128)(2,1)S(1)}, u32[]{:S(2)}, u32[]{:S(2)}) collective-permute-start(bf16[12,16,640]{2,1,0:T(8,128)(2,1)} %get-tuple-element.49), channel_id=1, source_target_pairs={{0,4},{2,6},{4,0},{6,2},{1,5},{3,7},{5,1},{7,3},{8,12},{10,14},{12... | collective-permute-start | bytes 737288 | tf_op jit(solution)/shard_map/ppermute | solution.py:420
  62.1 12.0 %collective-permute-start.3 = (bf16[12,16,640]{2,1,0:T(8,128)(2,1)}, bf16[12,16,640]{2,1,0:T(8,128)(2,1)S(1)}, u32[]{:S(2)}, u32[]{:S(2)}) collective-permute-start(bf16[12,16,640]{2,1,0:T(8,128)(2,1)} %get-tuple-element.50), channel_id=1, source_target_pairs={{0,2},{2,4},{4,6},{6,0},{1,3},{3,5},{5,7},{7,1},{8,10},{10,12},{12... | collective-permute-start | bytes 737288 | tf_op jit(solution)/shard_map/ppermute | solution.py:420
  62.5 11.7 %collective-permute-start.4 = (bf16[12,16,640]{2,1,0:T(8,128)(2,1)}, bf16[12,16,640]{2,1,0:T(8,128)(2,1)S(1)}, u32[]{:S(2)}, u32[]{:S(2)}) collective-permute-start(bf16[12,16,640]{2,1,0:T(8,128)(2,1)} %get-tuple-element.51), channel_id=1, source_target_pairs={{0,6},{2,0},{4,2},{6,4},{1,7},{3,1},{5,3},{7,5},{8,14},{10,8},{12,... | collective-permute-start | bytes 737288 | tf_op jit(solution)/shard_map/ppermute | solution.py:420
  68.2 6.0 %copy-start.2 = (bf16[12,16,640]{2,1,0:T(8,128)(2,1)}, bf16[12,16,640]{2,1,0:T(8,128)(2,1)S(1)}, u32[]{:S(2)}) copy-start(bf16[12,16,640]{2,1,0:T(8,128)(2,1)S(1)} %collective-permute-done.2.refs_2_) | copy-start | bytes 737284
  74.2 0.7 copy-start.3
  74.2 0.8 copy-start.4
  77.1 8.6 %collective-permute-start.5 = (bf16[4,16,640]{2,1,0:T(8,128)(2,1)}, bf16[4,16,640]{2,1,0:T(8,128)(2,1)S(1)}, u32[]{:S(2)}, u32[]{:S(2)}) collective-permute-start(bf16[4,16,640]{2,1,0:T(8,128)(2,1)} %get-tuple-element.53), channel_id=1, source_target_pairs={{0,32},{16,48},{32,0},{48,16},{1,33},{17,49},{33,1},{49,17},{2,34}... | collective-permute-start | bytes 245768 | tf_op jit(solution)/shard_map/ppermute | solution.py:420
  80.0 5.7 %collective-permute-start.6 = (bf16[4,16,640]{2,1,0:T(8,128)(2,1)}, bf16[4,16,640]{2,1,0:T(8,128)(2,1)S(1)}, u32[]{:S(2)}, u32[]{:S(2)}) collective-permute-start(bf16[4,16,640]{2,1,0:T(8,128)(2,1)} %get-tuple-element.54), channel_id=1, source_target_pairs={{0,16},{16,32},{32,48},{48,0},{1,17},{17,33},{33,49},{49,1},{2,18}... | collective-permute-start | bytes 245768 | tf_op jit(solution)/shard_map/ppermute | solution.py:420
  80.4 5.3 %copy-start.8 = (bf16[4,16,640]{2,1,0:T(8,128)(2,1)S(1)}, bf16[4,16,640]{2,1,0:T(8,128)(2,1)}, u32[]{:S(2)}) copy-start(bf16[4,16,640]{2,1,0:T(8,128)(2,1)} %get-tuple-element.57) | copy-start | bytes 245764
  80.4 5.3 %collective-permute-start.7 = (bf16[4,16,640]{2,1,0:T(8,128)(2,1)}, bf16[4,16,640]{2,1,0:T(8,128)(2,1)S(1)}, u32[]{:S(2)}, u32[]{:S(2)}) collective-permute-start(bf16[4,16,640]{2,1,0:T(8,128)(2,1)} %get-tuple-element.55), channel_id=1, source_target_pairs={{0,48},{16,0},{32,16},{48,32},{1,49},{17,1},{33,17},{49,33},{2,50}... | collective-permute-start | bytes 245768 | tf_op jit(solution)/shard_map/ppermute | solution.py:420
  85.8 4.0 %copy-start.9 = (bf16[4,16,640]{2,1,0:T(8,128)(2,1)}, bf16[4,16,640]{2,1,0:T(8,128)(2,1)S(1)}, u32[]{:S(2)}) copy-start(bf16[4,16,640]{2,1,0:T(8,128)(2,1)S(1)} %add_convert_fusion.a) | copy-start | bytes 245764
  85.8 7.6 %collective-permute-start.10 = (bf16[4,16,640]{2,1,0:T(8,128)(2,1)S(1)}, bf16[4,16,640]{2,1,0:T(8,128)(2,1)S(1)}, u32[]{:S(2)}, u32[]{:S(2)}) collective-permute-start(bf16[4,16,640]{2,1,0:T(8,128)(2,1)S(1)} %add_convert_fusion.a), channel_id=1, source_target_pairs={{0,72},{8,64},{64,8},{72,0},{1,73},{9,65},{65,9},{73,1},{2,74},{10... | collective-permute-start | bytes 245768 | tf_op jit(solution)/shard_map/ppermute | solution.py:419
  88.3 5.1 %collective-permute-start.9 = (bf16[4,16,640]{2,1,0:T(8,128)(2,1)S(1)}, bf16[4,16,640]{2,1,0:T(8,128)(2,1)S(1)}, u32[]{:S(2)}, u32[]{:S(2)}) collective-permute-start(bf16[4,16,640]{2,1,0:T(8,128)(2,1)S(1)} %add_convert_fusion.a), channel_id=1, source_target_pairs={{0,64},{8,72},{64,0},{72,8},{1,65},{9,73},{65,1},{73,9},{2,66},{10... | collective-permute-start | bytes 245768 | tf_op jit(solution)/shard_map/ppermute | solution.py:419
  88.3 5.2 %collective-permute-start.8 = (bf16[4,16,640]{2,1,0:T(8,128)(2,1)S(1)}, bf16[4,16,640]{2,1,0:T(8,128)(2,1)S(1)}, u32[]{:S(2)}, u32[]{:S(2)}) collective-permute-start(bf16[4,16,640]{2,1,0:T(8,128)(2,1)S(1)} %add_convert_fusion.a), channel_id=1, source_target_pairs={{0,8},{8,0},{64,72},{72,64},{1,9},{9,1},{65,73},{73,65},{2,10},{10... | collective-permute-start | bytes 245768 | tf_op jit(solution)/shard_map/ppermute | solution.py:419
  89.8 29.4 %all-to-all-start.2 = ((bf16[8,256,512]{2,1,0:T(8,128)(2,1)}), bf16[8,256,512]{2,1,0:T(8,128)(2,1)S(1)}, u32[]{:S(2)}, u32[]{:S(2)}) async-start(bf16[8,256,512]{2,1,0:T(8,128)(2,1)} %total.1), calls=%async_computation.2 | async-start | bytes 4194304 | tf_op jit(solution)/shard_map/all_to_all | solution.py:601
  93.4 0.6 copy-start.12
  93.4 0.6 copy-start.13
  93.5 0.6 copy-start.14
  96.1 3.9 %collective-permute-start.11 = (bf16[32,640]{1,0:T(8,128)(2,1)}, bf16[32,640]{1,0:T(8,128)(2,1)S(1)}, u32[]{:S(2)}, u32[]{:S(2)}) collective-permute-start(bf16[32,640]{1,0:T(8,128)(2,1)} %finish.1), channel_id=1, source_target_pairs={{0,1},{1,0},{2,3},{3,2},{4,5},{5,4},{6,7},{7,6},{8,9},{9,8},{10,11... | collective-permute-start | bytes 122888 | tf_op jit(solution)/shard_map/ppermute | solution.py:597
  100.8 9.7 %copy-start.1 = (bf16[64,640]{1,0:T(8,128)(2,1)}, bf16[64,640]{1,0:T(8,128)(2,1)S(1)}, u32[]{:S(2)}) copy-start(bf16[64,640]{1,0:T(8,128)(2,1)S(1)} %pad_maximum_fusion.refs_0_) | copy-start | bytes 245764
  100.8 5.9 %collective-permute-start.14 = (bf16[64,640]{1,0:T(8,128)(2,1)S(1)}, bf16[64,640]{1,0:T(8,128)(2,1)S(1)}, u32[]{:S(2)}, u32[]{:S(2)}) collective-permute-start(bf16[64,640]{1,0:T(8,128)(2,1)S(1)} %pad_maximum_fusion.refs_0_), channel_id=1, source_target_pairs={{0,6},{2,0},{4,2},{6,4},{1,7},{3,1},{5,3},{7,5},{8,14},{10,8},{12,... | collective-permute-start | bytes 245768 | tf_op jit(solution)/shard_map/ppermute | solution.py:420
  103.3 5.1 %collective-permute-start.13 = (bf16[64,640]{1,0:T(8,128)(2,1)S(1)}, bf16[64,640]{1,0:T(8,128)(2,1)S(1)}, u32[]{:S(2)}, u32[]{:S(2)}) collective-permute-start(bf16[64,640]{1,0:T(8,128)(2,1)S(1)} %pad_maximum_fusion.refs_0_), channel_id=1, source_target_pairs={{0,4},{2,6},{4,0},{6,2},{1,5},{3,7},{5,1},{7,3},{8,12},{10,14},{12... | collective-permute-start | bytes 245768 | tf_op jit(solution)/shard_map/ppermute | solution.py:420
  103.8 6.7 %collective-permute-start.12 = (bf16[64,640]{1,0:T(8,128)(2,1)S(1)}, bf16[64,640]{1,0:T(8,128)(2,1)S(1)}, u32[]{:S(2)}, u32[]{:S(2)}) collective-permute-start(bf16[64,640]{1,0:T(8,128)(2,1)S(1)} %pad_maximum_fusion.refs_0_), channel_id=1, source_target_pairs={{0,2},{2,4},{4,6},{6,0},{1,3},{3,5},{5,7},{7,1},{8,10},{10,12},{12... | collective-permute-start | bytes 245768 | tf_op jit(solution)/shard_map/ppermute | solution.py:420
  106.7 3.8 %copy-start.5 = (bf16[64,640]{1,0:T(8,128)(2,1)}, bf16[64,640]{1,0:T(8,128)(2,1)S(1)}, u32[]{:S(2)}) copy-start(bf16[64,640]{1,0:T(8,128)(2,1)S(1)} %collective-permute-done.14.refs_3_) | copy-start | bytes 245764
  108.4 2.1 %copy-start.6 = (bf16[64,640]{1,0:T(8,128)(2,1)}, bf16[64,640]{1,0:T(8,128)(2,1)S(1)}, u32[]{:S(2)}) copy-start(bf16[64,640]{1,0:T(8,128)(2,1)S(1)} %collective-permute-done.13.refs_2_) | copy-start | bytes 245764
  110.5 0.6 copy-start.7

commit v5 on v4

--- a/solution.py
+++ b/solution.py
@@ -351,31 +351,54 @@
     )(*shared, q_nope, q_rope, d_out, w_uk, w_uv)
 
 
-def prepare_kernel(latent, gain, rope_t, gid, cid, gid_s, cid_s, lengths, own, send, bias, weight, inverse, info):
-    chunk = lax.axis_index("xl") * 4 + lax.axis_index("z")
-    core = lax.axis_index("core")
+def pack_rows(latent, gain, rope_t, gid, cid):
     latent_f = latent[...].astype(F32)
     inv = lax.rsqrt(jnp.mean(latent_f * latent_f, axis=1, keepdims=True) + 1e-06)
-    inverse[...] = inv
     normed = (latent_f * inv * gain[...].astype(F32)[None, :]).astype(BF)
     group = jnp.broadcast_to(gid[...].astype(F32), (8, ROWS)).T[:, :1].astype(jnp.int32)
     comp = jnp.broadcast_to(cid[...].astype(F32), (8, ROWS)).T[:, :1].astype(jnp.int32)
     code = group * (COMP + 1) + comp
     column = lax.broadcasted_iota(jnp.int32, (ROWS, EXTRA - D_ROPE), 1)
     tags = jnp.where(column == code, 1.0, 0.0).astype(BF)
-    seen = (column == code) | (column == group * (COMP + 1))
-    bias[...] = jnp.where(seen, 0.0, HIDE).astype(BF)
-    own[...] = jnp.concatenate([normed, rope_t[...].T, tags], axis=1)
+    packed = jnp.concatenate([normed, rope_t[...].T, tags], axis=1)
+    return packed, inv, group, comp, code, column
+
+
+def pack_kernel(latent, gain, rope_t, gid, cid, send, own):
+    core = lax.axis_index("core")
+    own[...] = pack_rows(latent, gain, rope_t, gid, cid)[0]
     half = own[pl.ds(pl.multiple_of(core * (ROWS // 2), ROWS // 2), ROWS // 2), :]
     for i in range(CTX):
         send[i] = half
+
+
+def pack(latent, latent_gain, k_rope_t, group_ids, comp_ids):
+    vector = pl.BlockSpec(memory_space=LOCAL)
+    return pl.pallas_call(
+        pack_kernel,
+        in_specs=[vector] * 5,
+        out_specs=vector,
+        out_shape=jax.ShapeDtypeStruct((CTX, ROWS // 2, PACK), BF),
+        scratch_shapes=[pltpu.VMEM((ROWS, PACK), BF)],
+        cost_estimate=SMALL,
+        name="pack",
+    )(latent, latent_gain, k_rope_t, group_ids[None, :], comp_ids[None, :])
+
+
+def prepare_kernel(latent, gain, rope_t, gid, cid, gid_s, cid_s, lengths, own, bias, weight, inverse, info):
+    packed, inv, group, comp, code, column = pack_rows(latent, gain, rope_t, gid, cid)
+    own[...] = packed
+    inverse[...] = inv
+    seen = (column == code) | (column == group * (COMP + 1))
+    bias[...] = jnp.where(seen, 0.0, HIDE).astype(BF)
     length = jnp.ones((ROWS, 1), F32)
     for g in range(GROUPS):
         for k in range(COMP):
             length = jnp.where(code == g * (COMP + 1) + k + 1, lengths[g, k].astype(F32), length)
     weight[...] = jnp.where(comp > 0, 64.0 / length, 0.0)
     group0, comp0 = gid_s[0], cid_s[0]
-    info[0], info[1], info[2], info[3] = chunk, core, group0, comp0
+    info[0] = lax.axis_index("xl") * 4 + lax.axis_index("z")
+    info[1], info[2], info[3] = lax.axis_index("core"), group0, comp0
     info[4] = jnp.sum(
         jnp.where(gid[...] * (COMP + 1) + cid[...] == group0 * (COMP + 1) + comp0, 1.0, 0.0)
     ).astype(jnp.int32)
@@ -390,16 +413,15 @@
     return pl.pallas_call(
         prepare_kernel,
         in_specs=[vector] * 5 + [scalar] * 3,
-        out_specs=[vector] * 5 + [scalar],
+        out_specs=[vector] * 4 + [scalar],
         out_shape=[
             jax.ShapeDtypeStruct((ROWS, PACK), BF),
-            jax.ShapeDtypeStruct((CTX, ROWS // 2, PACK), BF),
             jax.ShapeDtypeStruct((ROWS, EXTRA - D_ROPE), BF),
             jax.ShapeDtypeStruct((ROWS, 1), F32),
             jax.ShapeDtypeStruct((ROWS, 1), F32),
             jax.ShapeDtypeStruct((8,), jnp.int32),
         ],
-        cost_estimate=SMALL,
+        cost_estimate=LONG,
         name="prepare",
     )(
         latent,
@@ -614,7 +636,8 @@
     comp_ids,
     comp_lengths,
 ):
-    own, send, bias, weight, inverse, info = prepare(
+    send = pack(latent, latent_gain, k_rope_t, group_ids, comp_ids)
+    own, bias, weight, inverse, info = prepare(
         latent, latent_gain, k_rope_t, group_ids, comp_ids, comp_lengths
     )
     mine = exchange(send, CTX_AXES).reshape(-1, PACK)

time: 122 us -> 121 us (level)
  waiting for transfers between devices: 26.2 us -> 23.9 us
  Pallas kernels: 28.8 us -> 30.9 us
    pallas_call x0 -> x1, Pallas kernels: none -> 2.57 us  [pack(): pl.pallas_call(pack_kernel, in_specs=[vector] * 5, out_specs=vector, out_...]
    ppermute x3, waiting for transfers between devices: 3.75 us -> 1.46 us  [swap_core(): return lax.ppermute(x, 'core', [(0, 1), (1, 0)])]
  transfers between devices with their start and end apart: 17 -> 17, of which waited for: 10 -> 10; matrix products, arithmetic and copies ran while one was open for 1% -> 1% of each run, Pallas kernels for 9% -> 11%
where the time goes in v5:
time: 121 us; the launch traced here: 120 us
  starting transfers between devices  34.5 us (29%)
  Pallas kernels  30.9 us (26%)
  blocking collectives  23.9 us (20%)
  waiting for transfers between devices  23.9 us (20%)
  local copies, waits for them, and re-layouts  5.6 us (5%)
    all_to_all x1, blocking collectives, exchange(): return lax.all_to_all(x, axes, 0, 0, tiled=True)  23.9 us
    ppermute x9, waiting for transfers between devices, move(): return lax.ppermute(x, axis, [(i, (i + distance) % 4) for i in range(4)])  15.9 us
    pallas_call x1, Pallas kernels, attention(): pl.pallas_call(attention_kernel, grid=(pairs,), in_specs=in_specs, out_sp...  15 us
    ppermute x9, starting transfers between devices, move(): return lax.ppermute(x, axis, [(i, (i + distance) % 4) for i in range(4)])  14.4 us
    all_to_all x2, starting transfers between devices, exchange(): return lax.all_to_all(x, axes, 0, 0, tiled=True)  10.4 us
    all_to_all x2, waiting for transfers between devices, exchange(): return lax.all_to_all(x, axes, 0, 0, tiled=True)  6.47 us
    ppermute x3, starting transfers between devices, swap_core(): return lax.ppermute(x, 'core', [(0, 1), (1, 0)])  5.76 us
    pallas_call x2, Pallas kernels, fold(): pl.pallas_call(kernel, in_specs=[scalar if x.dtype == jnp.int32 else vect...  4.62 us
  transfers between devices with their start and end apart: 17, of which 10 were waited for; matrix products, arithmetic and copies ran while one was open for 1% of the time, Pallas kernels for 11%

profile of v5, /device:TPU:1, one launch (start us, length us, event | category | flops | bytes accessed | tf_op | source)
XLA Modules:
  0.0 120.4 jit_solution(14778944343436161054)
XLA Ops:
  0.6 2.6 %pack.1 = bf16[8,128,640]{2,1,0:T(8,128)(2,1)} custom-call(bf16[256,512]{1,0:T(8,128)(2,1)} %latent.5, bf16[512]{0:T(512)(128)(2,1)} %gain.5, bf16[64,256]{1,0:T(8,128)(2,1)} %rope_t.3, s32[1,256]{1,0:T(1,128)} %bitcast.9, s32[1,256]{1,0:T(1,128)} %bitcast.11), custom_call_target="tpu_custom_call" | custom-call | flops 1 | bytes 1 | tf_op jit(solution)/shard_map/pack/pallas_call | solution.py:377
  3.2 23.9 %all_to_all.15 = bf16[8,128,640]{2,1,0:T(8,128)(2,1)S(1)} all-to-all(bf16[8,128,640]{2,1,0:T(8,128)(2,1)} %pack.1), channel_id=1, replica_groups=mesh['xl'=2,'z'=4,'xh'=2,'y'=4,'core'=2] {'xl','z'}, dimensions={0} | all-to-all | bytes 2621440 | tf_op jit(solution)/shard_map/all_to_all | solution.py:623
  27.1 2.4 %collective-permute-start = (bf16[1024,640]{1,0:T(8,128)(2,1)S(1)}, bf16[1024,640]{1,0:T(8,128)(2,1)S(1)}, u32[]{:S(2)}, u32[]{:S(2)}) collective-permute-start(bf16[1024,640]{1,0:T(8,128)(2,1)S(1)} %bitcast.5), channel_id=1, source_target_pairs={{0,1},{1,0},{2,3},{3,2},{4,5},{5,4},{6,7},{7,6},{8,9},{9,8},{10,11... | collective-permute-start | bytes 3932168 | tf_op jit(solution)/shard_map/ppermute | solution.py:619
  29.6 2.3 %prepare.1 = (bf16[256,640]{1,0:T(8,128)(2,1)}, bf16[256,64]{1,0:T(8,128)(2,1)}, f32[256,1]{1,0:T(8,128)}, f32[256,1]{1,0:T(8,128)}, s32[8]{0:T(128)}) custom-call(bf16[256,512]{1,0:T(8,128)(2,1)} %latent.5, bf16[512]{0:T(512)(128)(2,1)} %gain.5, bf16[64,256]{1,0:T(8,128)(2,1)} %rope_t.3, s32[1,256]{1,0:T(1,128)} %bitcast.10, s32[1,256]{1,0:T(1,128)} %bitcast.12, ...), custom_call_target="tpu_custom_call" | custom-call | flops 99999997952 | bytes 1 | tf_op jit(solution)/shard_map/prepare/pallas_call | solution.py:413
  32.2 1.0 copy-done.10
  33.3 15.0 %attention.1 = (bf16[256,1024]{1,0:T(8,128)(2,1)}, bf16[256,1024]{1,0:T(8,128)(2,1)}, bf16[256,512]{1,0:T(8,128)(2,1)}, bf16[8,256,512]{2,1,0:T(8,128)(2,1)}, bf...) custom-call(s32[8]{0:T(128)} %get-tuple-element.36.refs_0_, ...), custom_call_target="tpu_custom_call" | custom-call | flops 10400000000 | bytes 16777216 | tf_op jit(solution)/shard_map/attention/pallas_call | solution.py:308
  48.7 6.8 %all-to-all-start.1 = ((bf16[8,256,512]{2,1,0:T(8,128)(2,1)}), bf16[8,256,512]{2,1,0:T(8,128)(2,1)}, u32[]{:S(2)}, u32[]{:S(2)}) async-start(bf16[8,256,512]{2,1,0:T(8,128)(2,1)} %get-tuple-element.54), calls=%async_computation.1 | async-start | bytes 4194304 | tf_op jit(solution)/shard_map/all_to_all | solution.py:623
  55.6 0.9 copy-done.11
  56.5 2.5 %fold.2 = (bf16[12,16,640]{2,1,0:T(8,128)(2,1)}, bf16[12,16,640]{2,1,0:T(8,128)(2,1)}, bf16[12,16,640]{2,1,0:T(8,128)(2,1)}, bf16[12,16,640]{2,1,0:T(8,128)(2,1)}) custom-call(bf16[12,4,16,640]{3,2,1,0:T(8,128)(2,1)} %get-tuple-element.44.refs_0_, bf16[12,4,16,640]{3,2,1,0:T(8,128)(2,1)} %copy-done.11), custom_call_target="tpu_custom_call" | custom-call | flops 99999997952 | bytes 1 | tf_op jit(solution)/shard_map/fold/pallas_call | solution.py:493
  59.0 2.9 %collective-permute-start.2 = (bf16[12,16,640]{2,1,0:T(8,128)(2,1)}, bf16[12,16,640]{2,1,0:T(8,128)(2,1)S(1)}, u32[]{:S(2)}, u32[]{:S(2)}) collective-permute-start(bf16[12,16,640]{2,1,0:T(8,128)(2,1)} %get-tuple-element.47), channel_id=1, source_target_pairs={{0,4},{2,6},{4,0},{6,2},{1,5},{3,7},{5,1},{7,3},{8,12},{10,14},{12... | collective-permute-start | bytes 737288 | tf_op jit(solution)/shard_map/ppermute | solution.py:442
  62.3 2.3 %collective-permute-start.4 = (bf16[12,16,640]{2,1,0:T(8,128)(2,1)}, bf16[12,16,640]{2,1,0:T(8,128)(2,1)S(1)}, u32[]{:S(2)}, u32[]{:S(2)}) collective-permute-start(bf16[12,16,640]{2,1,0:T(8,128)(2,1)} %get-tuple-element.49), channel_id=1, source_target_pairs={{0,6},{2,0},{4,2},{6,4},{1,7},{3,1},{5,3},{7,5},{8,14},{10,8},{12,... | collective-permute-start | bytes 737288 | tf_op jit(solution)/shard_map/ppermute | solution.py:442
  64.6 3.3 %collective-permute-done.2.refs_2_ = bf16[12,16,640]{2,1,0:T(8,128)(2,1)S(1)} collective-permute-done((bf16[12,16,640]{2,1,0:T(8,128)(2,1)}, bf16[12,16,640]{2,1,0:T(8,128)(2,1)S(1)}, u32[]{:S(2)}, u32[]{:S(2)}) %collective-permute-start.2) | collective-permute-done | bytes 245792 | tf_op jit(solution)/shard_map/ppermute | solution.py:442
  67.9 6.0 %collective-permute-done.3.refs_3_ = bf16[12,16,640]{2,1,0:T(8,128)(2,1)S(1)} collective-permute-done((bf16[12,16,640]{2,1,0:T(8,128)(2,1)}, bf16[12,16,640]{2,1,0:T(8,128)(2,1)S(1)}, u32[]{:S(2)}, u32[]{:S(2)}) %collective-permute-start.3) | collective-permute-done | bytes 245792 | tf_op jit(solution)/shard_map/ppermute | solution.py:442
  74.0 0.7 copy-done.3
  74.8 2.1 %fold.3 = (bf16[4,16,640]{2,1,0:T(8,128)(2,1)}, bf16[4,16,640]{2,1,0:T(8,128)(2,1)}, bf16[4,16,640]{2,1,0:T(8,128)(2,1)}, bf16[4,16,640]{2,1,0:T(8,128)(2,1)}) custom-call(s32[8]{0:T(128)} %get-tuple-element.43.refs_0_, bf16[12,16,640]{2,1,0:T(8,128)(2,1)} %get-tuple-element.46.refs_1_, bf16[12,16,640]{2,1,0:T(8,128)(2,1)} %copy-done.2, ...), custom_call_target="tpu_custom_call" | custom-call | flops 1 | bytes 1 | tf_op jit(solution)/shard_map/fold/pallas_call | solution.py:493
  76.9 2.9 %collective-permute-start.5 = (bf16[4,16,640]{2,1,0:T(8,128)(2,1)}, bf16[4,16,640]{2,1,0:T(8,128)(2,1)S(1)}, u32[]{:S(2)}, u32[]{:S(2)}) collective-permute-start(bf16[4,16,640]{2,1,0:T(8,128)(2,1)} %get-tuple-element.51), channel_id=1, source_target_pairs={{0,32},{16,48},{32,0},{48,16},{1,33},{17,49},{33,1},{49,17},{2,34}... | collective-permute-start | bytes 245768 | tf_op jit(solution)/shard_map/ppermute | solution.py:442
  80.2 2.3 %collective-permute-start.7 = (bf16[4,16,640]{2,1,0:T(8,128)(2,1)}, bf16[4,16,640]{2,1,0:T(8,128)(2,1)S(1)}, u32[]{:S(2)}, u32[]{:S(2)}) collective-permute-start(bf16[4,16,640]{2,1,0:T(8,128)(2,1)} %get-tuple-element.53), channel_id=1, source_target_pairs={{0,48},{16,0},{32,16},{48,32},{1,49},{17,1},{33,17},{49,33},{2,50}... | collective-permute-start | bytes 245768 | tf_op jit(solution)/shard_map/ppermute | solution.py:442
  82.7 2.8 %total.1 = bf16[8,256,512]{2,1,0:T(8,128)(2,1)} custom-call(bf16[8,256,512]{2,1,0:T(8,128)(2,1)} %all-to-all-done.1.pieces), custom_call_target="tpu_custom_call" | custom-call | flops 1 | bytes 1 | tf_op jit(solution)/shard_map/total/pallas_call | solution.py:601
  85.6 2.5 %collective-permute-start.10 = (bf16[4,16,640]{2,1,0:T(8,128)(2,1)S(1)}, bf16[4,16,640]{2,1,0:T(8,128)(2,1)S(1)}, u32[]{:S(2)}, u32[]{:S(2)}) collective-permute-start(bf16[4,16,640]{2,1,0:T(8,128)(2,1)S(1)} %add_convert_fusion.a), channel_id=1, source_target_pairs={{0,72},{8,64},{64,8},{72,0},{1,73},{9,65},{65,9},{73,1},{2,74},{10... | collective-permute-start | bytes 245768 | tf_op jit(solution)/shard_map/ppermute | solution.py:441
  88.1 1.4 %collective-permute-start.8 = (bf16[4,16,640]{2,1,0:T(8,128)(2,1)S(1)}, bf16[4,16,640]{2,1,0:T(8,128)(2,1)S(1)}, u32[]{:S(2)}, u32[]{:S(2)}) collective-permute-start(bf16[4,16,640]{2,1,0:T(8,128)(2,1)S(1)} %add_convert_fusion.a), channel_id=1, source_target_pairs={{0,8},{8,0},{64,72},{72,64},{1,9},{9,1},{65,73},{73,65},{2,10},{10... | collective-permute-start | bytes 245768 | tf_op jit(solution)/shard_map/ppermute | solution.py:441
  89.5 3.6 %all-to-all-start.2 = ((bf16[8,256,512]{2,1,0:T(8,128)(2,1)}), bf16[8,256,512]{2,1,0:T(8,128)(2,1)S(1)}, u32[]{:S(2)}, u32[]{:S(2)}) async-start(bf16[8,256,512]{2,1,0:T(8,128)(2,1)} %total.1), calls=%async_computation.2 | async-start | bytes 4194304 | tf_op jit(solution)/shard_map/all_to_all | solution.py:623
  93.9 1.9 %finish.1 = bf16[32,640]{1,0:T(8,128)(2,1)} custom-call(bf16[4,16,640]{2,1,0:T(8,128)(2,1)} %copy-done.9, bf16[4,16,640]{2,1,0:T(8,128)(2,1)} %copy-done.14, bf16[4,16,640]{2,1,0:T(8,128)(2,1)} %copy-done.13, bf16[4,16,640]{2,1,0:T(8,128)(2,1)} %copy-done.12, bf16[256,512]{1,0:T(8,128)(2,1)} %latent.5, f32[256,1]{1,0:T(8,128)} %get-tuple-element.61.inverse, ...), custom_call_target="tpu_custom_call" | custom-call | flops 99999997952 | bytes 1 | tf_op jit(solution)/shard_map/finish/pallas_call | solution.py:533
  95.8 2.9 %collective-permute-start.11 = (bf16[32,640]{1,0:T(8,128)(2,1)}, bf16[32,640]{1,0:T(8,128)(2,1)S(1)}, u32[]{:S(2)}, u32[]{:S(2)}) collective-permute-start(bf16[32,640]{1,0:T(8,128)(2,1)} %finish.1), channel_id=1, source_target_pairs={{0,1},{1,0},{2,3},{3,2},{4,5},{5,4},{6,7},{7,6},{8,9},{9,8},{10,11... | collective-permute-start | bytes 122888 | tf_op jit(solution)/shard_map/ppermute | solution.py:619
  98.7 1.1 collective-permute-done.11
  99.8 0.8 pad_maximum_fusion.refs_0_
  100.6 2.5 %collective-permute-start.14 = (bf16[64,640]{1,0:T(8,128)(2,1)S(1)}, bf16[64,640]{1,0:T(8,128)(2,1)S(1)}, u32[]{:S(2)}, u32[]{:S(2)}) collective-permute-start(bf16[64,640]{1,0:T(8,128)(2,1)S(1)} %pad_maximum_fusion.refs_0_), channel_id=1, source_target_pairs={{0,6},{2,0},{4,2},{6,4},{1,7},{3,1},{5,3},{7,5},{8,14},{10,8},{12,... | collective-permute-start | bytes 245768 | tf_op jit(solution)/shard_map/ppermute | solution.py:442
  103.7 2.7 %collective-permute-done.14.refs_3_ = bf16[64,640]{1,0:T(8,128)(2,1)S(1)} collective-permute-done((bf16[64,640]{1,0:T(8,128)(2,1)S(1)}, bf16[64,640]{1,0:T(8,128)(2,1)S(1)}, u32[]{:S(2)}, u32[]{:S(2)}) %collective-permute-start.14) | collective-permute-done | bytes 81952 | tf_op jit(solution)/shard_map/ppermute | solution.py:442
  106.4 1.7 %collective-permute-done.13.refs_2_ = bf16[64,640]{1,0:T(8,128)(2,1)S(1)} collective-permute-done((bf16[64,640]{1,0:T(8,128)(2,1)S(1)}, bf16[64,640]{1,0:T(8,128)(2,1)S(1)}, u32[]{:S(2)}, u32[]{:S(2)}) %collective-permute-start.13) | collective-permute-done | bytes 81952 | tf_op jit(solution)/shard_map/ppermute | solution.py:442
  108.2 2.1 %collective-permute-done.12.refs_1_ = bf16[64,640]{1,0:T(8,128)(2,1)S(1)} collective-permute-done((bf16[64,640]{1,0:T(8,128)(2,1)S(1)}, bf16[64,640]{1,0:T(8,128)(2,1)S(1)}, u32[]{:S(2)}, u32[]{:S(2)}) %collective-permute-start.12) | collective-permute-done | bytes 81952 | tf_op jit(solution)/shard_map/ppermute | solution.py:442
  110.9 1.7 %assemble.1 = (bf16[256,512]{1,0:T(8,128)(2,1)}, bf16[64,256]{1,0:T(8,128)(2,1)}) custom-call(bf16[64,640]{1,0:T(8,128)(2,1)} %copy-done.1, bf16[64,640]{1,0:T(8,128)(2,1)} %copy-done.7, bf16[64,640]{1,0:T(8,128)(2,1)} %copy-done.6, bf16[64,640]{1,0:T(8,128)(2,1)} %copy-done.5), custom_call_target="tpu_custom_call" | custom-call | flops 1 | bytes 1 | tf_op jit(solution)/shard_map/assemble/pallas_call | solution.py:559
  112.6 6.3 %all-to-all-done.2 = bf16[8,256,512]{2,1,0:T(8,128)(2,1)S(1)} async-done(((bf16[8,256,512]{2,1,0:T(8,128)(2,1)}), bf16[8,256,512]{2,1,0:T(8,128)(2,1)S(1)}, u32[]{:S(2)}, u32[]{:S(2)}) %all-to-all-start.2) | async-done | bytes 2097184 | tf_op jit(solution)/shard_map/all_to_all | solution.py:623
  118.9 1.5 %fusion = (bf16[8,128,512]{2,1,0:T(8,128)(2,1)}, bf16[8,128,512]{2,1,0:T(8,128)(2,1)}) fusion(bf16[8,256,512]{2,1,0:T(8,128)(2,1)S(1)} %all-to-all-done.2), kind=kLoop, calls=%fused_computation.2 | loop fusion | bytes 4194304 | tf_op jit(solution)/shard_map/slice | solution.py:655
  (44 shorter events, 4.1 us)
Async XLA Ops:
  27.1 4.7 %copy-start = (bf16[8,128,640]{2,1,0:T(8,128)(2,1)}, bf16[8,128,640]{2,1,0:T(8,128)(2,1)S(1)}, u32[]{:S(2)}) copy-start(bf16[8,128,640]{2,1,0:T(8,128)(2,1)S(1)} %all_to_all.15) | copy-start | bytes 3932164
  27.1 5.1 %collective-permute-start = (bf16[1024,640]{1,0:T(8,128)(2,1)S(1)}, bf16[1024,640]{1,0:T(8,128)(2,1)S(1)}, u32[]{:S(2)}, u32[]{:S(2)}) collective-permute-start(bf16[1024,640]{1,0:T(8,128)(2,1)S(1)} %bitcast.5), channel_id=1, source_target_pairs={{0,1},{1,0},{2,3},{3,2},{4,5},{5,4},{6,7},{7,6},{8,9},{9,8},{10,11... | collective-permute-start | bytes 3932168 | tf_op jit(solution)/shard_map/ppermute | solution.py:619
  32.2 1.0 copy-start.10
  48.3 7.3 %collective-permute-start.1 = (bf16[12,4,16,640]{3,2,1,0:T(8,128)(2,1)}, bf16[12,4,16,640]{3,2,1,0:T(8,128)(2,1)S(1)}, u32[]{:S(2)}, u32[]{:S(2)}) collective-permute-start(bf16[12,4,16,640]{3,2,1,0:T(8,128)(2,1)} %get-tuple-element.45), channel_id=1, source_target_pairs={{0,1},{1,0},{2,3},{3,2},{4,5},{5,4},{6,7},{7,6},{8,9},{9,8},{10,11... | collective-permute-start | bytes 2949128 | tf_op jit(solution)/shard_map/ppermute | solution.py:619
  48.7 34.0 %all-to-all-start.1 = ((bf16[8,256,512]{2,1,0:T(8,128)(2,1)}), bf16[8,256,512]{2,1,0:T(8,128)(2,1)}, u32[]{:S(2)}, u32[]{:S(2)}) async-start(bf16[8,256,512]{2,1,0:T(8,128)(2,1)} %get-tuple-element.54), calls=%async_computation.1 | async-start | bytes 4194304 | tf_op jit(solution)/shard_map/all_to_all | solution.py:623
  55.5 0.9 copy-start.11
  59.0 8.9 %collective-permute-start.2 = (bf16[12,16,640]{2,1,0:T(8,128)(2,1)}, bf16[12,16,640]{2,1,0:T(8,128)(2,1)S(1)}, u32[]{:S(2)}, u32[]{:S(2)}) collective-permute-start(bf16[12,16,640]{2,1,0:T(8,128)(2,1)} %get-tuple-element.47), channel_id=1, source_target_pairs={{0,4},{2,6},{4,0},{6,2},{1,5},{3,7},{5,1},{7,3},{8,12},{10,14},{12... | collective-permute-start | bytes 737288 | tf_op jit(solution)/shard_map/ppermute | solution.py:442
  61.9 12.0 %collective-permute-start.3 = (bf16[12,16,640]{2,1,0:T(8,128)(2,1)}, bf16[12,16,640]{2,1,0:T(8,128)(2,1)S(1)}, u32[]{:S(2)}, u32[]{:S(2)}) collective-permute-start(bf16[12,16,640]{2,1,0:T(8,128)(2,1)} %get-tuple-element.48), channel_id=1, source_target_pairs={{0,2},{2,4},{4,6},{6,0},{1,3},{3,5},{5,7},{7,1},{8,10},{10,12},{12... | collective-permute-start | bytes 737288 | tf_op jit(solution)/shard_map/ppermute | solution.py:442
  62.3 11.6 %collective-permute-start.4 = (bf16[12,16,640]{2,1,0:T(8,128)(2,1)}, bf16[12,16,640]{2,1,0:T(8,128)(2,1)S(1)}, u32[]{:S(2)}, u32[]{:S(2)}) collective-permute-start(bf16[12,16,640]{2,1,0:T(8,128)(2,1)} %get-tuple-element.49), channel_id=1, source_target_pairs={{0,6},{2,0},{4,2},{6,4},{1,7},{3,1},{5,3},{7,5},{8,14},{10,8},{12,... | collective-permute-start | bytes 737288 | tf_op jit(solution)/shard_map/ppermute | solution.py:442
  67.9 6.0 %copy-start.2 = (bf16[12,16,640]{2,1,0:T(8,128)(2,1)}, bf16[12,16,640]{2,1,0:T(8,128)(2,1)S(1)}, u32[]{:S(2)}) copy-start(bf16[12,16,640]{2,1,0:T(8,128)(2,1)S(1)} %collective-permute-done.2.refs_2_) | copy-start | bytes 737284
  74.0 0.7 copy-start.3
  74.0 0.8 copy-start.4
  76.9 8.6 %collective-permute-start.5 = (bf16[4,16,640]{2,1,0:T(8,128)(2,1)}, bf16[4,16,640]{2,1,0:T(8,128)(2,1)S(1)}, u32[]{:S(2)}, u32[]{:S(2)}) collective-permute-start(bf16[4,16,640]{2,1,0:T(8,128)(2,1)} %get-tuple-element.51), channel_id=1, source_target_pairs={{0,32},{16,48},{32,0},{48,16},{1,33},{17,49},{33,1},{49,17},{2,34}... | collective-permute-start | bytes 245768 | tf_op jit(solution)/shard_map/ppermute | solution.py:442
  79.8 5.7 %collective-permute-start.6 = (bf16[4,16,640]{2,1,0:T(8,128)(2,1)}, bf16[4,16,640]{2,1,0:T(8,128)(2,1)S(1)}, u32[]{:S(2)}, u32[]{:S(2)}) collective-permute-start(bf16[4,16,640]{2,1,0:T(8,128)(2,1)} %get-tuple-element.52), channel_id=1, source_target_pairs={{0,16},{16,32},{32,48},{48,0},{1,17},{17,33},{33,49},{49,1},{2,18}... | collective-permute-start | bytes 245768 | tf_op jit(solution)/shard_map/ppermute | solution.py:442
  80.2 5.3 %copy-start.8 = (bf16[4,16,640]{2,1,0:T(8,128)(2,1)S(1)}, bf16[4,16,640]{2,1,0:T(8,128)(2,1)}, u32[]{:S(2)}) copy-start(bf16[4,16,640]{2,1,0:T(8,128)(2,1)} %get-tuple-element.55) | copy-start | bytes 245764
  80.2 5.3 %collective-permute-start.7 = (bf16[4,16,640]{2,1,0:T(8,128)(2,1)}, bf16[4,16,640]{2,1,0:T(8,128)(2,1)S(1)}, u32[]{:S(2)}, u32[]{:S(2)}) collective-permute-start(bf16[4,16,640]{2,1,0:T(8,128)(2,1)} %get-tuple-element.53), channel_id=1, source_target_pairs={{0,48},{16,0},{32,16},{48,32},{1,49},{17,1},{33,17},{49,33},{2,50}... | collective-permute-start | bytes 245768 | tf_op jit(solution)/shard_map/ppermute | solution.py:442
  85.6 4.0 %copy-start.9 = (bf16[4,16,640]{2,1,0:T(8,128)(2,1)}, bf16[4,16,640]{2,1,0:T(8,128)(2,1)S(1)}, u32[]{:S(2)}) copy-start(bf16[4,16,640]{2,1,0:T(8,128)(2,1)S(1)} %add_convert_fusion.a) | copy-start | bytes 245764
  85.6 7.6 %collective-permute-start.10 = (bf16[4,16,640]{2,1,0:T(8,128)(2,1)S(1)}, bf16[4,16,640]{2,1,0:T(8,128)(2,1)S(1)}, u32[]{:S(2)}, u32[]{:S(2)}) collective-permute-start(bf16[4,16,640]{2,1,0:T(8,128)(2,1)S(1)} %add_convert_fusion.a), channel_id=1, source_target_pairs={{0,72},{8,64},{64,8},{72,0},{1,73},{9,65},{65,9},{73,1},{2,74},{10... | collective-permute-start | bytes 245768 | tf_op jit(solution)/shard_map/ppermute | solution.py:441
  88.1 5.0 %collective-permute-start.9 = (bf16[4,16,640]{2,1,0:T(8,128)(2,1)S(1)}, bf16[4,16,640]{2,1,0:T(8,128)(2,1)S(1)}, u32[]{:S(2)}, u32[]{:S(2)}) collective-permute-start(bf16[4,16,640]{2,1,0:T(8,128)(2,1)S(1)} %add_convert_fusion.a), channel_id=1, source_target_pairs={{0,64},{8,72},{64,0},{72,8},{1,65},{9,73},{65,1},{73,9},{2,66},{10... | collective-permute-start | bytes 245768 | tf_op jit(solution)/shard_map/ppermute | solution.py:441
  88.1 5.2 %collective-permute-start.8 = (bf16[4,16,640]{2,1,0:T(8,128)(2,1)S(1)}, bf16[4,16,640]{2,1,0:T(8,128)(2,1)S(1)}, u32[]{:S(2)}, u32[]{:S(2)}) collective-permute-start(bf16[4,16,640]{2,1,0:T(8,128)(2,1)S(1)} %add_convert_fusion.a), channel_id=1, source_target_pairs={{0,8},{8,0},{64,72},{72,64},{1,9},{9,1},{65,73},{73,65},{2,10},{10... | collective-permute-start | bytes 245768 | tf_op jit(solution)/shard_map/ppermute | solution.py:441
  89.5 29.4 %all-to-all-start.2 = ((bf16[8,256,512]{2,1,0:T(8,128)(2,1)}), bf16[8,256,512]{2,1,0:T(8,128)(2,1)S(1)}, u32[]{:S(2)}, u32[]{:S(2)}) async-start(bf16[8,256,512]{2,1,0:T(8,128)(2,1)} %total.1), calls=%async_computation.2 | async-start | bytes 4194304 | tf_op jit(solution)/shard_map/all_to_all | solution.py:623
  93.2 0.6 copy-start.12
  93.2 0.6 copy-start.13
  93.3 0.6 copy-start.14
  95.8 3.9 %collective-permute-start.11 = (bf16[32,640]{1,0:T(8,128)(2,1)}, bf16[32,640]{1,0:T(8,128)(2,1)S(1)}, u32[]{:S(2)}, u32[]{:S(2)}) collective-permute-start(bf16[32,640]{1,0:T(8,128)(2,1)} %finish.1), channel_id=1, source_target_pairs={{0,1},{1,0},{2,3},{3,2},{4,5},{5,4},{6,7},{7,6},{8,9},{9,8},{10,11... | collective-permute-start | bytes 122888 | tf_op jit(solution)/shard_map/ppermute | solution.py:619
  100.6 9.7 %copy-start.1 = (bf16[64,640]{1,0:T(8,128)(2,1)}, bf16[64,640]{1,0:T(8,128)(2,1)S(1)}, u32[]{:S(2)}) copy-start(bf16[64,640]{1,0:T(8,128)(2,1)S(1)} %pad_maximum_fusion.refs_0_) | copy-start | bytes 245764
  100.6 5.9 %collective-permute-start.14 = (bf16[64,640]{1,0:T(8,128)(2,1)S(1)}, bf16[64,640]{1,0:T(8,128)(2,1)S(1)}, u32[]{:S(2)}, u32[]{:S(2)}) collective-permute-start(bf16[64,640]{1,0:T(8,128)(2,1)S(1)} %pad_maximum_fusion.refs_0_), channel_id=1, source_target_pairs={{0,6},{2,0},{4,2},{6,4},{1,7},{3,1},{5,3},{7,5},{8,14},{10,8},{12,... | collective-permute-start | bytes 245768 | tf_op jit(solution)/shard_map/ppermute | solution.py:442
  103.1 5.1 %collective-permute-start.13 = (bf16[64,640]{1,0:T(8,128)(2,1)S(1)}, bf16[64,640]{1,0:T(8,128)(2,1)S(1)}, u32[]{:S(2)}, u32[]{:S(2)}) collective-permute-start(bf16[64,640]{1,0:T(8,128)(2,1)S(1)} %pad_maximum_fusion.refs_0_), channel_id=1, source_target_pairs={{0,4},{2,6},{4,0},{6,2},{1,5},{3,7},{5,1},{7,3},{8,12},{10,14},{12... | collective-permute-start | bytes 245768 | tf_op jit(solution)/shard_map/ppermute | solution.py:442
  103.6 6.6 %collective-permute-start.12 = (bf16[64,640]{1,0:T(8,128)(2,1)S(1)}, bf16[64,640]{1,0:T(8,128)(2,1)S(1)}, u32[]{:S(2)}, u32[]{:S(2)}) collective-permute-start(bf16[64,640]{1,0:T(8,128)(2,1)S(1)} %pad_maximum_fusion.refs_0_), channel_id=1, source_target_pairs={{0,2},{2,4},{4,6},{6,0},{1,3},{3,5},{5,7},{7,1},{8,10},{10,12},{12... | collective-permute-start | bytes 245768 | tf_op jit(solution)/shard_map/ppermute | solution.py:442
  106.4 3.8 %copy-start.5 = (bf16[64,640]{1,0:T(8,128)(2,1)}, bf16[64,640]{1,0:T(8,128)(2,1)S(1)}, u32[]{:S(2)}) copy-start(bf16[64,640]{1,0:T(8,128)(2,1)S(1)} %collective-permute-done.14.refs_3_) | copy-start | bytes 245764
  108.2 2.1 %copy-start.6 = (bf16[64,640]{1,0:T(8,128)(2,1)}, bf16[64,640]{1,0:T(8,128)(2,1)S(1)}, u32[]{:S(2)}) copy-start(bf16[64,640]{1,0:T(8,128)(2,1)S(1)} %collective-permute-done.13.refs_2_) | copy-start | bytes 245764
  110.3 0.6 copy-start.7

commit v6 on v5

--- a/solution.py
+++ b/solution.py
@@ -504,10 +504,10 @@
 def gather_grads(kept, sent, meta, total):
     slots = sent.shape[0]
     cut = fold(fold_y_kernel, [kept, swap_core(sent)], 4, (slots, BLOCK, PACK))
-    parts = [cut[0]] + [move(cut[d], "y", d) for d in (2, 1, 3)]
+    parts = [cut[0]] + [move(cut[d], "y", d) for d in (1, 3, 2)]
     spread = pltpu.VMEM((4, 4, BLOCK, PACK), BF)
     cut = fold(fold_z_kernel, [meta] + parts, 4, (4, BLOCK, PACK), [spread])
-    parts = [cut[0]] + [move(cut[d], "z", d) for d in (2, 1, 3)]
+    parts = [cut[0]] + [move(cut[d], "z", d) for d in (1, 3, 2)]
     parts, total = lax.optimization_barrier((parts, total))
     part = sum([x.astype(F32) for x in parts[1:]], parts[0].astype(F32)).astype(BF)
     part, total = lax.optimization_barrier((part, total))

time: 121 us -> 122 us (level)
    ppermute x9, starting transfers between devices: 14.4 us -> 12.5 us  [move(): return lax.ppermute(x, axis, [(i, (i + distance) % 4) for i in range(4)])]
  transfers between devices with their start and end apart: 17 -> 17, of which waited for: 10 -> 9; matrix products, arithmetic and copies ran while one was open for 1% -> 1% of each run, Pallas kernels for 11% -> 11%
where the time goes in v6:
time: 122 us
  starting transfers between devices  34.7 us (28%)
  Pallas kernels  30.9 us (25%)
  waiting for transfers between devices  24.8 us (20%)
  blocking collectives  23.9 us (20%)
  local copies, waits for them, and re-layouts  5.53 us (5%)
    all_to_all x1, blocking collectives, exchange(): return lax.all_to_all(x, axes, 0, 0, tiled=True)  23.9 us
    ppermute x9, waiting for transfers between devices, move(): return lax.ppermute(x, axis, [(i, (i + distance) % 4) for i in range(4)])  16.5 us
    pallas_call x1, Pallas kernels, attention(): pl.pallas_call(attention_kernel, grid=(pairs,), in_specs=in_specs, out_sp...  15 us
    ppermute x9, starting transfers between devices, move(): return lax.ppermute(x, axis, [(i, (i + distance) % 4) for i in range(4)])  12.5 us
    all_to_all x2, starting transfers between devices, exchange(): return lax.all_to_all(x, axes, 0, 0, tiled=True)  10.5 us
    all_to_all x2, waiting for transfers between devices, exchange(): return lax.all_to_all(x, axes, 0, 0, tiled=True)  6.79 us
    ppermute x3, starting transfers between devices, swap_core(): return lax.ppermute(x, 'core', [(0, 1), (1, 0)])  6.75 us
    ppermute x3, starting transfers between devices, move(): return lax.ppermute(x, names, [(i, i ^ distance) for i in range(4)])  5.05 us
  transfers between devices with their start and end apart: 17, of which 9 were waited for; matrix products, arithmetic and copies ran while one was open for 1% of the time, Pallas kernels for 11%

profile of v6, /device:TPU:1, one launch (start us, length us, event | category | flops | bytes accessed | tf_op | source)
XLA Modules:
  0.0 121.5 jit_solution(9638467961414974830)
XLA Ops:
  0.6 2.6 %pack.1 = bf16[8,128,640]{2,1,0:T(8,128)(2,1)} custom-call(bf16[256,512]{1,0:T(8,128)(2,1)} %latent.5, bf16[512]{0:T(512)(128)(2,1)} %gain.5, bf16[64,256]{1,0:T(8,128)(2,1)} %rope_t.3, s32[1,256]{1,0:T(1,128)} %bitcast.9, s32[1,256]{1,0:T(1,128)} %bitcast.11), custom_call_target="tpu_custom_call" | custom-call | flops 1 | bytes 1 | tf_op jit(solution)/shard_map/pack/pallas_call | solution.py:377
  3.2 23.9 %all_to_all.15 = bf16[8,128,640]{2,1,0:T(8,128)(2,1)S(1)} all-to-all(bf16[8,128,640]{2,1,0:T(8,128)(2,1)} %pack.1), channel_id=1, replica_groups=mesh['xl'=2,'z'=4,'xh'=2,'y'=4,'core'=2] {'xl','z'}, dimensions={0} | all-to-all | bytes 2621440 | tf_op jit(solution)/shard_map/all_to_all | solution.py:623
  27.1 2.4 %collective-permute-start = (bf16[1024,640]{1,0:T(8,128)(2,1)S(1)}, bf16[1024,640]{1,0:T(8,128)(2,1)S(1)}, u32[]{:S(2)}, u32[]{:S(2)}) collective-permute-start(bf16[1024,640]{1,0:T(8,128)(2,1)S(1)} %bitcast.5), channel_id=1, source_target_pairs={{0,1},{1,0},{2,3},{3,2},{4,5},{5,4},{6,7},{7,6},{8,9},{9,8},{10,11... | collective-permute-start | bytes 3932168 | tf_op jit(solution)/shard_map/ppermute | solution.py:619
  29.6 2.3 %prepare.1 = (bf16[256,640]{1,0:T(8,128)(2,1)}, bf16[256,64]{1,0:T(8,128)(2,1)}, f32[256,1]{1,0:T(8,128)}, f32[256,1]{1,0:T(8,128)}, s32[8]{0:T(128)}) custom-call(bf16[256,512]{1,0:T(8,128)(2,1)} %latent.5, bf16[512]{0:T(512)(128)(2,1)} %gain.5, bf16[64,256]{1,0:T(8,128)(2,1)} %rope_t.3, s32[1,256]{1,0:T(1,128)} %bitcast.10, s32[1,256]{1,0:T(1,128)} %bitcast.12, ...), custom_call_target="tpu_custom_call" | custom-call | flops 99999997952 | bytes 1 | tf_op jit(solution)/shard_map/prepare/pallas_call | solution.py:413
  32.2 1.0 copy-done.10
  33.3 15.0 %attention.1 = (bf16[256,1024]{1,0:T(8,128)(2,1)}, bf16[256,1024]{1,0:T(8,128)(2,1)}, bf16[256,512]{1,0:T(8,128)(2,1)}, bf16[8,256,512]{2,1,0:T(8,128)(2,1)}, bf...) custom-call(s32[8]{0:T(128)} %get-tuple-element.36.refs_0_, ...), custom_call_target="tpu_custom_call" | custom-call | flops 10400000000 | bytes 16777216 | tf_op jit(solution)/shard_map/attention/pallas_call | solution.py:308
  48.7 6.9 %all-to-all-start.1 = ((bf16[8,256,512]{2,1,0:T(8,128)(2,1)}), bf16[8,256,512]{2,1,0:T(8,128)(2,1)}, u32[]{:S(2)}, u32[]{:S(2)}) async-start(bf16[8,256,512]{2,1,0:T(8,128)(2,1)} %get-tuple-element.54), calls=%async_computation.1 | async-start | bytes 4194304 | tf_op jit(solution)/shard_map/all_to_all | solution.py:623
  55.6 0.9 copy-done.11
  56.5 2.5 %fold.2 = (bf16[12,16,640]{2,1,0:T(8,128)(2,1)}, bf16[12,16,640]{2,1,0:T(8,128)(2,1)}, bf16[12,16,640]{2,1,0:T(8,128)(2,1)}, bf16[12,16,640]{2,1,0:T(8,128)(2,1)}) custom-call(bf16[12,4,16,640]{3,2,1,0:T(8,128)(2,1)} %get-tuple-element.44.refs_0_, bf16[12,4,16,640]{3,2,1,0:T(8,128)(2,1)} %copy-done.11), custom_call_target="tpu_custom_call" | custom-call | flops 99999997952 | bytes 1 | tf_op jit(solution)/shard_map/fold/pallas_call | solution.py:493
  59.0 1.3 %collective-permute-start.2 = (bf16[12,16,640]{2,1,0:T(8,128)(2,1)}, bf16[12,16,640]{2,1,0:T(8,128)(2,1)S(1)}, u32[]{:S(2)}, u32[]{:S(2)}) collective-permute-start(bf16[12,16,640]{2,1,0:T(8,128)(2,1)} %get-tuple-element.47), channel_id=1, source_target_pairs={{0,2},{2,4},{4,6},{6,0},{1,3},{3,5},{5,7},{7,1},{8,10},{10,12},{12... | collective-permute-start | bytes 737288 | tf_op jit(solution)/shard_map/ppermute | solution.py:442
  60.3 1.4 %collective-permute-start.3 = (bf16[12,16,640]{2,1,0:T(8,128)(2,1)}, bf16[12,16,640]{2,1,0:T(8,128)(2,1)S(1)}, u32[]{:S(2)}, u32[]{:S(2)}) collective-permute-start(bf16[12,16,640]{2,1,0:T(8,128)(2,1)} %get-tuple-element.48), channel_id=1, source_target_pairs={{0,6},{2,0},{4,2},{6,4},{1,7},{3,1},{5,3},{7,5},{8,14},{10,8},{12,... | collective-permute-start | bytes 737288 | tf_op jit(solution)/shard_map/ppermute | solution.py:442
  61.8 1.6 %collective-permute-start.4 = (bf16[12,16,640]{2,1,0:T(8,128)(2,1)}, bf16[12,16,640]{2,1,0:T(8,128)(2,1)S(1)}, u32[]{:S(2)}, u32[]{:S(2)}) collective-permute-start(bf16[12,16,640]{2,1,0:T(8,128)(2,1)} %get-tuple-element.49), channel_id=1, source_target_pairs={{0,4},{2,6},{4,0},{6,2},{1,5},{3,7},{5,1},{7,3},{8,12},{10,14},{12... | collective-permute-start | bytes 737288 | tf_op jit(solution)/shard_map/ppermute | solution.py:442
  63.4 4.4 %collective-permute-done.2.refs_2_ = bf16[12,16,640]{2,1,0:T(8,128)(2,1)S(1)} collective-permute-done((bf16[12,16,640]{2,1,0:T(8,128)(2,1)}, bf16[12,16,640]{2,1,0:T(8,128)(2,1)S(1)}, u32[]{:S(2)}, u32[]{:S(2)}) %collective-permute-start.2) | collective-permute-done | bytes 245792 | tf_op jit(solution)/shard_map/ppermute | solution.py:442
  67.8 6.4 %collective-permute-done.4.refs_4_ = bf16[12,16,640]{2,1,0:T(8,128)(2,1)S(1)} collective-permute-done((bf16[12,16,640]{2,1,0:T(8,128)(2,1)}, bf16[12,16,640]{2,1,0:T(8,128)(2,1)S(1)}, u32[]{:S(2)}, u32[]{:S(2)}) %collective-permute-start.4) | collective-permute-done | bytes 245792 | tf_op jit(solution)/shard_map/ppermute | solution.py:442
  74.9 2.1 %fold.3 = (bf16[4,16,640]{2,1,0:T(8,128)(2,1)}, bf16[4,16,640]{2,1,0:T(8,128)(2,1)}, bf16[4,16,640]{2,1,0:T(8,128)(2,1)}, bf16[4,16,640]{2,1,0:T(8,128)(2,1)}) custom-call(s32[8]{0:T(128)} %get-tuple-element.43.refs_0_, bf16[12,16,640]{2,1,0:T(8,128)(2,1)} %get-tuple-element.46.refs_1_, bf16[12,16,640]{2,1,0:T(8,128)(2,1)} %copy-done.2, ...), custom_call_target="tpu_custom_call" | custom-call | flops 1 | bytes 1 | tf_op jit(solution)/shard_map/fold/pallas_call | solution.py:493
  77.0 3.2 %collective-permute-start.5 = (bf16[4,16,640]{2,1,0:T(8,128)(2,1)}, bf16[4,16,640]{2,1,0:T(8,128)(2,1)S(1)}, u32[]{:S(2)}, u32[]{:S(2)}) collective-permute-start(bf16[4,16,640]{2,1,0:T(8,128)(2,1)} %get-tuple-element.51), channel_id=1, source_target_pairs={{0,16},{16,32},{32,48},{48,0},{1,17},{17,33},{33,49},{49,1},{2,18}... | collective-permute-start | bytes 245768 | tf_op jit(solution)/shard_map/ppermute | solution.py:442
  80.2 1.8 %collective-permute-start.7 = (bf16[4,16,640]{2,1,0:T(8,128)(2,1)}, bf16[4,16,640]{2,1,0:T(8,128)(2,1)S(1)}, u32[]{:S(2)}, u32[]{:S(2)}) collective-permute-start(bf16[4,16,640]{2,1,0:T(8,128)(2,1)} %get-tuple-element.53), channel_id=1, source_target_pairs={{0,32},{16,48},{32,0},{48,16},{1,33},{17,49},{33,1},{49,17},{2,34}... | collective-permute-start | bytes 245768 | tf_op jit(solution)/shard_map/ppermute | solution.py:442
  82.8 2.8 %total.1 = bf16[8,256,512]{2,1,0:T(8,128)(2,1)} custom-call(bf16[8,256,512]{2,1,0:T(8,128)(2,1)} %all-to-all-done.1.pieces), custom_call_target="tpu_custom_call" | custom-call | flops 1 | bytes 1 | tf_op jit(solution)/shard_map/total/pallas_call | solution.py:601
  85.7 3.8 %collective-permute-start.10 = (bf16[4,16,640]{2,1,0:T(8,128)(2,1)S(1)}, bf16[4,16,640]{2,1,0:T(8,128)(2,1)S(1)}, u32[]{:S(2)}, u32[]{:S(2)}) collective-permute-start(bf16[4,16,640]{2,1,0:T(8,128)(2,1)S(1)} %add_convert_fusion.a), channel_id=1, source_target_pairs={{0,72},{8,64},{64,8},{72,0},{1,73},{9,65},{65,9},{73,1},{2,74},{10... | collective-permute-start | bytes 245768 | tf_op jit(solution)/shard_map/ppermute | solution.py:441
  89.4 1.3 %collective-permute-start.8 = (bf16[4,16,640]{2,1,0:T(8,128)(2,1)S(1)}, bf16[4,16,640]{2,1,0:T(8,128)(2,1)S(1)}, u32[]{:S(2)}, u32[]{:S(2)}) collective-permute-start(bf16[4,16,640]{2,1,0:T(8,128)(2,1)S(1)} %add_convert_fusion.a), channel_id=1, source_target_pairs={{0,8},{8,0},{64,72},{72,64},{1,9},{9,1},{65,73},{73,65},{2,10},{10... | collective-permute-start | bytes 245768 | tf_op jit(solution)/shard_map/ppermute | solution.py:441
  90.7 3.6 %all-to-all-start.2 = ((bf16[8,256,512]{2,1,0:T(8,128)(2,1)}), bf16[8,256,512]{2,1,0:T(8,128)(2,1)S(1)}, u32[]{:S(2)}, u32[]{:S(2)}) async-start(bf16[8,256,512]{2,1,0:T(8,128)(2,1)} %total.1), calls=%async_computation.2 | async-start | bytes 4194304 | tf_op jit(solution)/shard_map/all_to_all | solution.py:623
  95.0 1.9 %finish.1 = bf16[32,640]{1,0:T(8,128)(2,1)} custom-call(bf16[4,16,640]{2,1,0:T(8,128)(2,1)} %copy-done.9, bf16[4,16,640]{2,1,0:T(8,128)(2,1)} %copy-done.14, bf16[4,16,640]{2,1,0:T(8,128)(2,1)} %copy-done.13, bf16[4,16,640]{2,1,0:T(8,128)(2,1)} %copy-done.12, bf16[256,512]{1,0:T(8,128)(2,1)} %latent.5, f32[256,1]{1,0:T(8,128)} %get-tuple-element.61.inverse, ...), custom_call_target="tpu_custom_call" | custom-call | flops 99999997952 | bytes 1 | tf_op jit(solution)/shard_map/finish/pallas_call | solution.py:533
  97.0 3.8 %collective-permute-start.11 = (bf16[32,640]{1,0:T(8,128)(2,1)}, bf16[32,640]{1,0:T(8,128)(2,1)S(1)}, u32[]{:S(2)}, u32[]{:S(2)}) collective-permute-start(bf16[32,640]{1,0:T(8,128)(2,1)} %finish.1), channel_id=1, source_target_pairs={{0,1},{1,0},{2,3},{3,2},{4,5},{5,4},{6,7},{7,6},{8,9},{9,8},{10,11... | collective-permute-start | bytes 122888 | tf_op jit(solution)/shard_map/ppermute | solution.py:619
  100.8 1.1 collective-permute-done.11
  101.9 0.8 pad_maximum_fusion.refs_0_
  102.7 1.7 %collective-permute-start.14 = (bf16[64,640]{1,0:T(8,128)(2,1)S(1)}, bf16[64,640]{1,0:T(8,128)(2,1)S(1)}, u32[]{:S(2)}, u32[]{:S(2)}) collective-permute-start(bf16[64,640]{1,0:T(8,128)(2,1)S(1)} %pad_maximum_fusion.refs_0_), channel_id=1, source_target_pairs={{0,6},{2,0},{4,2},{6,4},{1,7},{3,1},{5,3},{7,5},{8,14},{10,8},{12,... | collective-permute-start | bytes 245768 | tf_op jit(solution)/shard_map/ppermute | solution.py:442
  104.3 1.4 %collective-permute-start.13 = (bf16[64,640]{1,0:T(8,128)(2,1)S(1)}, bf16[64,640]{1,0:T(8,128)(2,1)S(1)}, u32[]{:S(2)}, u32[]{:S(2)}) collective-permute-start(bf16[64,640]{1,0:T(8,128)(2,1)S(1)} %pad_maximum_fusion.refs_0_), channel_id=1, source_target_pairs={{0,4},{2,6},{4,0},{6,2},{1,5},{3,7},{5,1},{7,3},{8,12},{10,14},{12... | collective-permute-start | bytes 245768 | tf_op jit(solution)/shard_map/ppermute | solution.py:442
  106.4 3.0 %collective-permute-done.13.refs_2_ = bf16[64,640]{1,0:T(8,128)(2,1)S(1)} collective-permute-done((bf16[64,640]{1,0:T(8,128)(2,1)S(1)}, bf16[64,640]{1,0:T(8,128)(2,1)S(1)}, u32[]{:S(2)}, u32[]{:S(2)}) %collective-permute-start.13) | collective-permute-done | bytes 81952 | tf_op jit(solution)/shard_map/ppermute | solution.py:442
  109.4 2.1 %collective-permute-done.12.refs_1_ = bf16[64,640]{1,0:T(8,128)(2,1)S(1)} collective-permute-done((bf16[64,640]{1,0:T(8,128)(2,1)S(1)}, bf16[64,640]{1,0:T(8,128)(2,1)S(1)}, u32[]{:S(2)}, u32[]{:S(2)}) %collective-permute-start.12) | collective-permute-done | bytes 81952 | tf_op jit(solution)/shard_map/ppermute | solution.py:442
  112.2 1.7 %assemble.1 = (bf16[256,512]{1,0:T(8,128)(2,1)}, bf16[64,256]{1,0:T(8,128)(2,1)}) custom-call(bf16[64,640]{1,0:T(8,128)(2,1)} %copy-done.1, bf16[64,640]{1,0:T(8,128)(2,1)} %copy-done.7, bf16[64,640]{1,0:T(8,128)(2,1)} %copy-done.6, bf16[64,640]{1,0:T(8,128)(2,1)} %copy-done.5), custom_call_target="tpu_custom_call" | custom-call | flops 1 | bytes 1 | tf_op jit(solution)/shard_map/assemble/pallas_call | solution.py:559
  113.9 6.1 %all-to-all-done.2 = bf16[8,256,512]{2,1,0:T(8,128)(2,1)S(1)} async-done(((bf16[8,256,512]{2,1,0:T(8,128)(2,1)}), bf16[8,256,512]{2,1,0:T(8,128)(2,1)S(1)}, u32[]{:S(2)}, u32[]{:S(2)}) %all-to-all-start.2) | async-done | bytes 2097184 | tf_op jit(solution)/shard_map/all_to_all | solution.py:623
  120.0 1.5 %fusion = (bf16[8,128,512]{2,1,0:T(8,128)(2,1)}, bf16[8,128,512]{2,1,0:T(8,128)(2,1)}) fusion(bf16[8,256,512]{2,1,0:T(8,128)(2,1)S(1)} %all-to-all-done.2), kind=kLoop, calls=%fused_computation.2 | loop fusion | bytes 4194304 | tf_op jit(solution)/shard_map/slice | solution.py:655
  (44 shorter events, 4.4 us)
Async XLA Ops:
  27.1 4.7 %copy-start = (bf16[8,128,640]{2,1,0:T(8,128)(2,1)}, bf16[8,128,640]{2,1,0:T(8,128)(2,1)S(1)}, u32[]{:S(2)}) copy-start(bf16[8,128,640]{2,1,0:T(8,128)(2,1)S(1)} %all_to_all.15) | copy-start | bytes 3932164
  27.1 5.1 %collective-permute-start = (bf16[1024,640]{1,0:T(8,128)(2,1)S(1)}, bf16[1024,640]{1,0:T(8,128)(2,1)S(1)}, u32[]{:S(2)}, u32[]{:S(2)}) collective-permute-start(bf16[1024,640]{1,0:T(8,128)(2,1)S(1)} %bitcast.5), channel_id=1, source_target_pairs={{0,1},{1,0},{2,3},{3,2},{4,5},{5,4},{6,7},{7,6},{8,9},{9,8},{10,11... | collective-permute-start | bytes 3932168 | tf_op jit(solution)/shard_map/ppermute | solution.py:619
  32.2 1.0 copy-start.10
  48.3 7.3 %collective-permute-start.1 = (bf16[12,4,16,640]{3,2,1,0:T(8,128)(2,1)}, bf16[12,4,16,640]{3,2,1,0:T(8,128)(2,1)S(1)}, u32[]{:S(2)}, u32[]{:S(2)}) collective-permute-start(bf16[12,4,16,640]{3,2,1,0:T(8,128)(2,1)} %get-tuple-element.45), channel_id=1, source_target_pairs={{0,1},{1,0},{2,3},{3,2},{4,5},{5,4},{6,7},{7,6},{8,9},{9,8},{10,11... | collective-permute-start | bytes 2949128 | tf_op jit(solution)/shard_map/ppermute | solution.py:619
  48.7 34.1 %all-to-all-start.1 = ((bf16[8,256,512]{2,1,0:T(8,128)(2,1)}), bf16[8,256,512]{2,1,0:T(8,128)(2,1)}, u32[]{:S(2)}, u32[]{:S(2)}) async-start(bf16[8,256,512]{2,1,0:T(8,128)(2,1)} %get-tuple-element.54), calls=%async_computation.1 | async-start | bytes 4194304 | tf_op jit(solution)/shard_map/all_to_all | solution.py:623
  55.6 0.9 copy-start.11
  59.0 8.7 %collective-permute-start.2 = (bf16[12,16,640]{2,1,0:T(8,128)(2,1)}, bf16[12,16,640]{2,1,0:T(8,128)(2,1)S(1)}, u32[]{:S(2)}, u32[]{:S(2)}) collective-permute-start(bf16[12,16,640]{2,1,0:T(8,128)(2,1)} %get-tuple-element.47), channel_id=1, source_target_pairs={{0,2},{2,4},{4,6},{6,0},{1,3},{3,5},{5,7},{7,1},{8,10},{10,12},{12... | collective-permute-start | bytes 737288 | tf_op jit(solution)/shard_map/ppermute | solution.py:442
  60.3 7.5 %collective-permute-start.3 = (bf16[12,16,640]{2,1,0:T(8,128)(2,1)}, bf16[12,16,640]{2,1,0:T(8,128)(2,1)S(1)}, u32[]{:S(2)}, u32[]{:S(2)}) collective-permute-start(bf16[12,16,640]{2,1,0:T(8,128)(2,1)} %get-tuple-element.48), channel_id=1, source_target_pairs={{0,6},{2,0},{4,2},{6,4},{1,7},{3,1},{5,3},{7,5},{8,14},{10,8},{12,... | collective-permute-start | bytes 737288 | tf_op jit(solution)/shard_map/ppermute | solution.py:442
  61.8 12.4 %collective-permute-start.4 = (bf16[12,16,640]{2,1,0:T(8,128)(2,1)}, bf16[12,16,640]{2,1,0:T(8,128)(2,1)S(1)}, u32[]{:S(2)}, u32[]{:S(2)}) collective-permute-start(bf16[12,16,640]{2,1,0:T(8,128)(2,1)} %get-tuple-element.49), channel_id=1, source_target_pairs={{0,4},{2,6},{4,0},{6,2},{1,5},{3,7},{5,1},{7,3},{8,12},{10,14},{12... | collective-permute-start | bytes 737288 | tf_op jit(solution)/shard_map/ppermute | solution.py:442
  67.8 6.4 %copy-start.2 = (bf16[12,16,640]{2,1,0:T(8,128)(2,1)}, bf16[12,16,640]{2,1,0:T(8,128)(2,1)S(1)}, u32[]{:S(2)}) copy-start(bf16[12,16,640]{2,1,0:T(8,128)(2,1)S(1)} %collective-permute-done.2.refs_2_) | copy-start | bytes 737284
  67.8 6.4 %copy-start.3 = (bf16[12,16,640]{2,1,0:T(8,128)(2,1)}, bf16[12,16,640]{2,1,0:T(8,128)(2,1)S(1)}, u32[]{:S(2)}) copy-start(bf16[12,16,640]{2,1,0:T(8,128)(2,1)S(1)} %collective-permute-done.3.refs_3_) | copy-start | bytes 737284
  74.2 0.7 copy-start.4
  77.0 8.5 %collective-permute-start.5 = (bf16[4,16,640]{2,1,0:T(8,128)(2,1)}, bf16[4,16,640]{2,1,0:T(8,128)(2,1)S(1)}, u32[]{:S(2)}, u32[]{:S(2)}) collective-permute-start(bf16[4,16,640]{2,1,0:T(8,128)(2,1)} %get-tuple-element.51), channel_id=1, source_target_pairs={{0,16},{16,32},{32,48},{48,0},{1,17},{17,33},{33,49},{49,1},{2,18}... | collective-permute-start | bytes 245768 | tf_op jit(solution)/shard_map/ppermute | solution.py:442
  80.2 5.4 %collective-permute-start.6 = (bf16[4,16,640]{2,1,0:T(8,128)(2,1)}, bf16[4,16,640]{2,1,0:T(8,128)(2,1)S(1)}, u32[]{:S(2)}, u32[]{:S(2)}) collective-permute-start(bf16[4,16,640]{2,1,0:T(8,128)(2,1)} %get-tuple-element.52), channel_id=1, source_target_pairs={{0,48},{16,0},{32,16},{48,32},{1,49},{17,1},{33,17},{49,33},{2,50}... | collective-permute-start | bytes 245768 | tf_op jit(solution)/shard_map/ppermute | solution.py:442
  80.2 5.4 %copy-start.8 = (bf16[4,16,640]{2,1,0:T(8,128)(2,1)S(1)}, bf16[4,16,640]{2,1,0:T(8,128)(2,1)}, u32[]{:S(2)}) copy-start(bf16[4,16,640]{2,1,0:T(8,128)(2,1)} %get-tuple-element.55) | copy-start | bytes 245764
  80.2 5.4 %collective-permute-start.7 = (bf16[4,16,640]{2,1,0:T(8,128)(2,1)}, bf16[4,16,640]{2,1,0:T(8,128)(2,1)S(1)}, u32[]{:S(2)}, u32[]{:S(2)}) collective-permute-start(bf16[4,16,640]{2,1,0:T(8,128)(2,1)} %get-tuple-element.53), channel_id=1, source_target_pairs={{0,32},{16,48},{32,0},{48,16},{1,33},{17,49},{33,1},{49,17},{2,34}... | collective-permute-start | bytes 245768 | tf_op jit(solution)/shard_map/ppermute | solution.py:442
  85.7 5.1 %copy-start.9 = (bf16[4,16,640]{2,1,0:T(8,128)(2,1)}, bf16[4,16,640]{2,1,0:T(8,128)(2,1)S(1)}, u32[]{:S(2)}) copy-start(bf16[4,16,640]{2,1,0:T(8,128)(2,1)S(1)} %add_convert_fusion.a) | copy-start | bytes 245764
  85.7 8.7 %collective-permute-start.10 = (bf16[4,16,640]{2,1,0:T(8,128)(2,1)S(1)}, bf16[4,16,640]{2,1,0:T(8,128)(2,1)S(1)}, u32[]{:S(2)}, u32[]{:S(2)}) collective-permute-start(bf16[4,16,640]{2,1,0:T(8,128)(2,1)S(1)} %add_convert_fusion.a), channel_id=1, source_target_pairs={{0,72},{8,64},{64,8},{72,0},{1,73},{9,65},{65,9},{73,1},{2,74},{10... | collective-permute-start | bytes 245768 | tf_op jit(solution)/shard_map/ppermute | solution.py:441
  89.4 4.9 %collective-permute-start.9 = (bf16[4,16,640]{2,1,0:T(8,128)(2,1)S(1)}, bf16[4,16,640]{2,1,0:T(8,128)(2,1)S(1)}, u32[]{:S(2)}, u32[]{:S(2)}) collective-permute-start(bf16[4,16,640]{2,1,0:T(8,128)(2,1)S(1)} %add_convert_fusion.a), channel_id=1, source_target_pairs={{0,64},{8,72},{64,0},{72,8},{1,65},{9,73},{65,1},{73,9},{2,66},{10... | collective-permute-start | bytes 245768 | tf_op jit(solution)/shard_map/ppermute | solution.py:441
  89.4 4.9 %collective-permute-start.8 = (bf16[4,16,640]{2,1,0:T(8,128)(2,1)S(1)}, bf16[4,16,640]{2,1,0:T(8,128)(2,1)S(1)}, u32[]{:S(2)}, u32[]{:S(2)}) collective-permute-start(bf16[4,16,640]{2,1,0:T(8,128)(2,1)S(1)} %add_convert_fusion.a), channel_id=1, source_target_pairs={{0,8},{8,0},{64,72},{72,64},{1,9},{9,1},{65,73},{73,65},{2,10},{10... | collective-permute-start | bytes 245768 | tf_op jit(solution)/shard_map/ppermute | solution.py:441
  90.7 29.3 %all-to-all-start.2 = ((bf16[8,256,512]{2,1,0:T(8,128)(2,1)}), bf16[8,256,512]{2,1,0:T(8,128)(2,1)S(1)}, u32[]{:S(2)}, u32[]{:S(2)}) async-start(bf16[8,256,512]{2,1,0:T(8,128)(2,1)} %total.1), calls=%async_computation.2 | async-start | bytes 4194304 | tf_op jit(solution)/shard_map/all_to_all | solution.py:623
  94.3 0.6 copy-start.12
  94.4 0.6 copy-start.13
  94.4 0.6 copy-start.14
  97.0 4.9 %collective-permute-start.11 = (bf16[32,640]{1,0:T(8,128)(2,1)}, bf16[32,640]{1,0:T(8,128)(2,1)S(1)}, u32[]{:S(2)}, u32[]{:S(2)}) collective-permute-start(bf16[32,640]{1,0:T(8,128)(2,1)} %finish.1), channel_id=1, source_target_pairs={{0,1},{1,0},{2,3},{3,2},{4,5},{5,4},{6,7},{7,6},{8,9},{9,8},{10,11... | collective-permute-start | bytes 122888 | tf_op jit(solution)/shard_map/ppermute | solution.py:619
  102.7 8.9 %copy-start.1 = (bf16[64,640]{1,0:T(8,128)(2,1)}, bf16[64,640]{1,0:T(8,128)(2,1)S(1)}, u32[]{:S(2)}) copy-start(bf16[64,640]{1,0:T(8,128)(2,1)S(1)} %pad_maximum_fusion.refs_0_) | copy-start | bytes 245764
  102.7 3.7 %collective-permute-start.14 = (bf16[64,640]{1,0:T(8,128)(2,1)S(1)}, bf16[64,640]{1,0:T(8,128)(2,1)S(1)}, u32[]{:S(2)}, u32[]{:S(2)}) collective-permute-start(bf16[64,640]{1,0:T(8,128)(2,1)S(1)} %pad_maximum_fusion.refs_0_), channel_id=1, source_target_pairs={{0,6},{2,0},{4,2},{6,4},{1,7},{3,1},{5,3},{7,5},{8,14},{10,8},{12,... | collective-permute-start | bytes 245768 | tf_op jit(solution)/shard_map/ppermute | solution.py:442
  104.3 5.1 %collective-permute-start.13 = (bf16[64,640]{1,0:T(8,128)(2,1)S(1)}, bf16[64,640]{1,0:T(8,128)(2,1)S(1)}, u32[]{:S(2)}, u32[]{:S(2)}) collective-permute-start(bf16[64,640]{1,0:T(8,128)(2,1)S(1)} %pad_maximum_fusion.refs_0_), channel_id=1, source_target_pairs={{0,4},{2,6},{4,0},{6,2},{1,5},{3,7},{5,1},{7,3},{8,12},{10,14},{12... | collective-permute-start | bytes 245768 | tf_op jit(solution)/shard_map/ppermute | solution.py:442
  105.7 5.8 %collective-permute-start.12 = (bf16[64,640]{1,0:T(8,128)(2,1)S(1)}, bf16[64,640]{1,0:T(8,128)(2,1)S(1)}, u32[]{:S(2)}, u32[]{:S(2)}) collective-permute-start(bf16[64,640]{1,0:T(8,128)(2,1)S(1)} %pad_maximum_fusion.refs_0_), channel_id=1, source_target_pairs={{0,2},{2,4},{4,6},{6,0},{1,3},{3,5},{5,7},{7,1},{8,10},{10,12},{12... | collective-permute-start | bytes 245768 | tf_op jit(solution)/shard_map/ppermute | solution.py:442
  106.4 5.1 %copy-start.5 = (bf16[64,640]{1,0:T(8,128)(2,1)}, bf16[64,640]{1,0:T(8,128)(2,1)S(1)}, u32[]{:S(2)}) copy-start(bf16[64,640]{1,0:T(8,128)(2,1)S(1)} %collective-permute-done.14.refs_3_) | copy-start | bytes 245764
  109.4 2.1 %copy-start.6 = (bf16[64,640]{1,0:T(8,128)(2,1)}, bf16[64,640]{1,0:T(8,128)(2,1)S(1)}, u32[]{:S(2)}) copy-start(bf16[64,640]{1,0:T(8,128)(2,1)S(1)} %collective-permute-done.13.refs_2_) | copy-start | bytes 245764
  111.5 0.6 copy-start.7
